TPU v7x, 256 devices: a whole 4x4x8 slice. The times are simulated.
256 devices in a mesh: dp: 2 (over core), expert: 128 (over y, z, x).
Axes of the slice: x: 4, y: 4, z: 8, core: 2. Of those that a mesh axis runs over, the one named last changes fastest.
Arguments:
- tokens: bfloat16 [32768, 1536], P(('dp', 'expert')), may hold values from -6 to 6
- out_grad: bfloat16 [32768, 1536], P(('dp', 'expert')), may hold values from -1.1953125 to 1.1953125
- routes: int32 [32768, 2], P(('dp', 'expert')), may hold values from 0 to 63, all different within a row; in each aligned block of 128 rows (0 to 127, 128 to 255, ...) at most 5 rows name the same one
- gate_probs: float32 [32768, 2], P(('dp', 'expert')), may hold values from 0.2 to 1
- weight_in: bfloat16 [1536, 196608], P('dp', 'expert'), may hold values from -0.15625 to 0.15625
- weight_out: bfloat16 [196608, 1536], P('expert', 'dp'), may hold values from -0.109375 to 0.109375
Outputs:
- token_grad: bfloat16 [32768, 1536], P(('dp', 'expert'))
- grad_in: bfloat16 [1536, 196608], P('dp', 'expert')
- grad_out: bfloat16 [196608, 1536], P('expert', 'dp')
Inputs may be any that keep to these rules, and one draw needn't show every extreme that they name: `routes`: within the rows of one device, no expert is named by more than 5 slots, and in every draw some expert is named by exactly 5 slots on some device; a token names two different experts; every expert is named somewhere.
All inputs are finite; a program needn't handle non-finite values.
Results may differ from a plain program's by a relative error of at most 0.012.
Values may be sent and summed in bfloat16 or wider, within the bound.
No kernel may reach another device: no remote copies, remote signals or barrier semaphores. Data moves between devices by JAX's collectives and lax.ppermute only.
A program may use at most 128 MiB of HBM per device.

v0:
```python
import jax
import jax.numpy as jnp
from jax import lax
from jax.sharding import PartitionSpec as P

root_two_pi = 0.7978845608
cubic_term = 0.044715


def gelu_value(pre):
    inner = root_two_pi * (pre + cubic_term * pre * pre * pre)
    return 0.5 * pre * (1.0 + jnp.tanh(inner))


def gelu_slope(pre):
    inner = root_two_pi * (pre + cubic_term * pre * pre * pre)
    tanh_value = jnp.tanh(inner)
    return 0.5 * (1.0 + tanh_value) + 0.5 * pre * (1.0 - tanh_value * tanh_value) * root_two_pi * (
        1.0 + 3.0 * cubic_term * pre * pre
    )


def slot_targets(route_block, expert_count, capacity):
    slot_expert = route_block.reshape(-1)
    labels = jnp.arange(expert_count, dtype=jnp.int32)
    one_hot = (slot_expert[:, None] == labels[None, :]).astype(jnp.int32)
    before = jnp.cumsum(one_hot, axis=0) - one_hot
    return slot_expert * capacity + jnp.sum(before * one_hot, axis=1)


def pack_rows(tokens, out_grad, routes, gate_probs, expert_count, capacity):
    target = slot_targets(routes, expert_count, capacity)
    slot_count = target.shape[0]
    places = jnp.arange(expert_count * capacity, dtype=jnp.int32)
    match = (target[None, :] == places[:, None]).astype(jnp.int32)
    source_slot = jnp.sum(match * jnp.arange(slot_count, dtype=jnp.int32)[None, :], axis=1)
    filled = jnp.sum(match, axis=1).astype(jnp.float32)[:, None]
    token_index = source_slot // 2
    token_rows = (tokens[token_index].astype(jnp.float32) * filled).astype(jnp.bfloat16)
    scale = gate_probs.reshape(-1)[source_slot][:, None] * filled
    grad_rows = (out_grad[token_index].astype(jnp.float32) * scale).astype(jnp.bfloat16)
    return (target, token_rows, grad_rows)


def expert_half(token_rows, grad_rows, w_first, w_second):
    pre = jnp.dot(token_rows, w_first, preferred_element_type=jnp.float32)
    hidden = gelu_value(pre).astype(jnp.bfloat16)
    back = lax.dot_general(
        grad_rows, w_second, (((1,), (1,)), ((), ())), preferred_element_type=jnp.float32
    )
    d_pre = (back * gelu_slope(pre)).astype(jnp.bfloat16)
    part = lax.dot_general(
        d_pre, w_first, (((1,), (1,)), ((), ())), preferred_element_type=jnp.float32
    ).astype(jnp.bfloat16)
    return (hidden, d_pre, part)


def contract_rows(left, right):
    return lax.dot_general(
        left, right, (((0,), (0,)), ((), ())), preferred_element_type=jnp.float32
    )


def per_device(tokens, out_grad, routes, gate_probs, weight_in, weight_out):
    expert_slots = lax.axis_size("expert")
    expert_count = expert_slots // 2
    token_count = routes.shape[0]
    capacity = max(2, (5 * token_count + 2 * expert_count - 1) // (2 * expert_count))
    width = tokens.shape[1]
    first_full, second_full = (
        lax.all_gather(weight_in, "dp", axis=0, tiled=True),
        lax.all_gather(weight_out, "dp", axis=1, tiled=True),
    )
    target, token_rows, grad_rows = pack_rows(
        tokens, out_grad, routes, gate_probs, expert_count, capacity
    )
    sent_tokens = jnp.repeat(token_rows.reshape(expert_count, capacity, width), 2, axis=0)
    sent_grads = jnp.repeat(grad_rows.reshape(expert_count, capacity, width), 2, axis=0)
    got_tokens, got_grads = (
        lax.all_to_all(sent_tokens, "expert", split_axis=0, concat_axis=0, tiled=True),
        lax.all_to_all(sent_grads, "expert", split_axis=0, concat_axis=0, tiled=True),
    )
    token_recv = got_tokens.reshape(-1, width)
    grad_recv = got_grads.reshape(-1, width)
    hidden, d_pre, part = expert_half(token_recv, grad_recv, first_full, second_full)
    part = part.reshape(expert_slots, capacity, width)
    back_rows = lax.all_to_all(part, "expert", split_axis=0, concat_axis=0, tiled=True)
    merged = (
        back_rows.reshape(expert_count, 2, capacity, width)
        .astype(jnp.float32)
        .sum(axis=1)
        .astype(jnp.bfloat16)
    )
    slot_grad = merged.reshape(expert_count * capacity, width)[target]
    token_grad = (
        slot_grad.reshape(-1, 2, width).astype(jnp.float32).sum(axis=1).astype(jnp.bfloat16)
    )
    grad_in, grad_out = (
        lax.psum_scatter(
            contract_rows(token_recv, d_pre).astype(jnp.bfloat16),
            "dp",
            scatter_dimension=0,
            tiled=True,
        ).astype(jnp.float32),
        lax.psum_scatter(
            contract_rows(hidden, grad_recv).astype(jnp.bfloat16),
            "dp",
            scatter_dimension=1,
            tiled=True,
        ).astype(jnp.float32),
    )
    return (token_grad, grad_in.astype(jnp.bfloat16), grad_out.astype(jnp.bfloat16))


def solution(mesh):
    return jax.shard_map(
        per_device,
        mesh=mesh,
        in_specs=(
            P(("dp", "expert"), None),
            P(("dp", "expert"), None),
            P(("dp", "expert"), None),
            P(("dp", "expert"), None),
            P("dp", "expert"),
            P("expert", "dp"),
        ),
        out_specs=(P(("dp", "expert"), None), P("dp", "expert"), P("expert", "dp")),
        check_vma=False,
    )
```

profile of v0, /device:TPU:8, one launch (start us, length us, event | category | flops | bytes accessed | tf_op | source)
XLA Modules:
  0.0 330.7 jit_solution(996690044793120261)
XLA Ops:
  7.2 0.0 all-gather.5.cloned.1.call-start
  7.2 0.7 all-gather.5.cloned.1.call-update
  7.9 0.8 copy.14
  8.7 0.1 reshape.188
  8.8 0.1 eq.39
  9.0 0.6 reduce-window.6
  9.6 0.2 slice_reduce_fusion
  9.8 0.1 fusion.13
  10.0 0.2 convert_reduce_fusion
  10.2 2.7 gather_fusion.2
  13.0 1.3 reshape.200
  14.3 0.1 convert_element_type.74
  14.5 0.2 multiply_convert_fusion.1
  14.7 1.9 broadcast_in_dim.5
  16.6 15.6 %all-to-all-start.1 = ((bf16[128,5,1536]{2,1,0:T(8,128)(2,1)}), bf16[128,5,1536]{2,1,0:T(8,128)(2,1)S(1)}, u32[]{:S(2)}, u32[]{:S(2)}) async-start(bf16[128,5,1536]{2,1,0:T(8,128)(2,1)} %bitcast.34), calls=%async_computation.1 | async-start | bytes 6291456 | tf_op jit(solution)/shard_map/all_to_all | solution.py:80
  32.2 0.0 all-gather.3.cloned.1.call-start
  32.2 0.7 all-gather.3.cloned.1.call-update
  32.9 2.7 gather_fusion
  35.7 2.9 reshape.199
  38.6 0.1 copy.17
  38.7 0.1 reshape.190
  38.8 2.5 gather_fusion.1
  41.3 0.1 gather.16
  41.4 3.3 multiply_convert_fusion.2
  44.7 61.7 %all-to-all-done.1 = bf16[128,5,1536]{2,1,0:T(8,128)(2,1)S(1)} async-done(((bf16[128,5,1536]{2,1,0:T(8,128)(2,1)}), bf16[128,5,1536]{2,1,0:T(8,128)(2,1)S(1)}, u32[]{:S(2)}, u32[]{:S(2)}) %all-to-all-start.1) | async-done | bytes 1966112 | tf_op jit(solution)/shard_map/all_to_all | solution.py:80
  106.4 3.3 %broadcast_in_dim.4 = bf16[64,2,5,1536]{3,2,1,0:T(8,128)(2,1)} broadcast(bf16[64,5,1536]{2,1,0:T(8,128)(2,1)} %multiply_convert_fusion.2), dimensions={0,2,3} | broadcast | bytes 2949120 | tf_op jit(solution)/shard_map/broadcast_in_dim | solution.py:78
  109.7 8.3 %all-to-all-start = ((bf16[128,5,1536]{2,1,0:T(8,128)(2,1)}), bf16[128,5,1536]{2,1,0:T(8,128)(2,1)}, u32[]{:S(2)}, u32[]{:S(2)}) async-start(bf16[128,5,1536]{2,1,0:T(8,128)(2,1)} %bitcast.35), calls=%async_computation | async-start | bytes 6291456 | tf_op jit(solution)/shard_map/all_to_all | solution.py:81
  118.0 0.2 reduce-scatter.3.cloned.1.call-start
  118.2 2.2 reshape.194
  120.4 70.9 %all-to-all-done = bf16[128,5,1536]{2,1,0:T(8,128)(2,1)} async-done(((bf16[128,5,1536]{2,1,0:T(8,128)(2,1)}), bf16[128,5,1536]{2,1,0:T(8,128)(2,1)}, u32[]{:S(2)}, u32[]{:S(2)}) %all-to-all-start) | async-done | bytes 1966112 | tf_op jit(solution)/shard_map/all_to_all | solution.py:81
  191.3 3.0 reshape.192
  194.4 8.0 %fusion.21 = f32[640,1536]{1,0:T(8,128)} fusion(bf16[640,1536]{1,0:T(8,128)(2,1)} %reshape.194, bf16[1536,1536]{1,0:T(8,128)(2,1)} %all-gather.5.cloned.1.call-done), kind=kOutput, calls=%fused_computation.54 | convolution fusion | flops 3019898880 | bytes 10616832 | tf_op jit(solution)/shard_map/dot_general | solution.py:46
  202.4 8.0 %fusion.6 = bf16[640,1536]{1,0:T(8,128)(2,1)S(1)} fusion(f32[640,1536]{1,0:T(8,128)} %fusion.21, bf16[640,1536]{1,0:T(8,128)(2,1)S(1)} %reshape.192, bf16[1536,1536]{1,0:T(8,128)(2,1)} %all-gather.3.cloned.1.call-done), kind=kOutput, calls=%fused_computation.14 | convolution fusion | flops 3038576640 | bytes 12582912 | tf_op jit(solution)/shard_map/dot_general | solution.py:48
  210.4 1.3 copy-done.8
  211.7 5.7 %convolution_convert_fusion.1 = bf16[1536,1536]{1,0:T(8,128)(2,1)} fusion(bf16[640,1536]{1,0:T(8,128)(2,1)S(1)} %copy-done.3, bf16[640,1536]{1,0:T(8,128)(2,1)S(1)} %fusion.6), kind=kOutput, calls=%fused_computation.5 | convolution fusion | flops 3022258176 | bytes 8650752 | tf_op jit(solution)/shard_map/dot_general | solution.py:59
  217.4 0.0 reduce-scatter.5.cloned.1.call-start
  217.5 8.9 %convolution_convert_fusion = bf16[1536,1536]{1,0:T(8,128)(2,1)} fusion(bf16[640,1536]{1,0:T(8,128)(2,1)S(1)} %reshape.192, f32[640,1536]{1,0:T(8,128)} %fusion.21), kind=kOutput, calls=%fused_computation.4 | convolution fusion | flops 3031105536 | bytes 10616832 | tf_op jit(solution)/shard_map/dot_general | solution.py:59
  226.4 7.2 %convolution_convert_fusion.2 = bf16[640,1536]{1,0:T(8,128)(2,1)S(1)} fusion(bf16[640,1536]{1,0:T(8,128)(2,1)} %copy-done.8, bf16[1536,1536]{1,0:T(8,128)(2,1)} %all-gather.5.cloned.1.call-done), kind=kOutput, calls=%fused_computation.16 | convolution fusion | flops 3020881920 | bytes 8650752 | tf_op jit(solution)/shard_map/dot_general | solution.py:52
  233.6 2.5 reshape.195
  236.0 7.9 %all-to-all-start.2 = ((bf16[128,5,1536]{2,1,0:T(8,128)(2,1)}), bf16[128,5,1536]{2,1,0:T(8,128)(2,1)S(1)}, u32[]{:S(2)}, u32[]{:S(2)}) async-start(bf16[128,5,1536]{2,1,0:T(8,128)(2,1)} %reshape.195), calls=%async_computation.2 | async-start | bytes 6291456 | tf_op jit(solution)/shard_map/all_to_all | solution.py:87
  244.0 0.1 copy.18
  244.1 0.1 mul.137
  244.2 71.8 %all-to-all-done.2 = bf16[128,5,1536]{2,1,0:T(8,128)(2,1)S(1)} async-done(((bf16[128,5,1536]{2,1,0:T(8,128)(2,1)}), bf16[128,5,1536]{2,1,0:T(8,128)(2,1)S(1)}, u32[]{:S(2)}, u32[]{:S(2)}) %all-to-all-start.2) | async-done | bytes 1966112 | tf_op jit(solution)/shard_map/all_to_all | solution.py:87
  316.0 2.0 bitcast_reduce_fusion
  318.1 1.6 reshape.197
  319.7 1.3 gather_fusion.3
  321.0 0.3 reshape.198
  321.3 2.9 reduce_sum.61
  (34 shorter events, 0.2 us)
Async XLA Ops:
  7.2 3.0 copy-start
  7.2 187.2 %all-gather.5.cloned.1.call-start = ((), (), s32[]{:S(2)}) async-start(), calls=%async_computation.6 | async-start | bytes 7077888 | tf_op jit(solution)/shard_map/all_gather | solution.py:71
  14.5 2.1 copy-start.4
  16.6 16.3 %copy-start.2 = (bf16[128,1536]{1,0:T(8,128)(2,1)S(1)}, bf16[128,1536]{1,0:T(8,128)(2,1)}, u32[]{:S(2)}) copy-start(bf16[128,1536]{1,0:T(8,128)(2,1)} %param.7) | copy-start | bytes 1179652
  16.6 89.8 %all-to-all-start.1 = ((bf16[128,5,1536]{2,1,0:T(8,128)(2,1)}), bf16[128,5,1536]{2,1,0:T(8,128)(2,1)S(1)}, u32[]{:S(2)}, u32[]{:S(2)}) async-start(bf16[128,5,1536]{2,1,0:T(8,128)(2,1)} %bitcast.34), calls=%async_computation.1 | async-start | bytes 6291456 | tf_op jit(solution)/shard_map/all_to_all | solution.py:80
  32.2 170.2 %all-gather.3.cloned.1.call-start = ((), (), s32[]{:S(2)}) async-start(), calls=%async_computation.5 | async-start | bytes 7077888 | tf_op jit(solution)/shard_map/all_gather | solution.py:72
  35.7 2.9 copy-start.7
  35.7 5.7 %copy-start.5 = (f32[64,5]{1,0:T(8,128)S(1)}, f32[64,5]{1,0:T(8,128)}, u32[]{:S(2)}) copy-start(f32[64,5]{1,0:T(8,128)} %copy-done.4) | copy-start | bytes 3844
  109.7 81.6 %all-to-all-start = ((bf16[128,5,1536]{2,1,0:T(8,128)(2,1)}), bf16[128,5,1536]{2,1,0:T(8,128)(2,1)}, u32[]{:S(2)}, u32[]{:S(2)}) async-start(bf16[128,5,1536]{2,1,0:T(8,128)(2,1)} %bitcast.35), calls=%async_computation | async-start | bytes 6291456 | tf_op jit(solution)/shard_map/all_to_all | solution.py:81
  118.0 206.2 %reduce-scatter.3.cloned.1.call-start = ((), (), s32[]{:S(2)}) async-start(), calls=%async_computation.7 | async-start | bytes 7077888 | tf_op jit(solution)/shard_map/reduce_scatter | solution.py:99
  202.4 9.3 %copy-start.3 = (bf16[640,1536]{1,0:T(8,128)(2,1)S(1)}, bf16[640,1536]{1,0:T(8,128)(2,1)}, u32[]{:S(2)}) copy-start(bf16[640,1536]{1,0:T(8,128)(2,1)} %reshape.194) | copy-start | bytes 5898244
  210.4 1.3 copy-start.8
  217.4 106.7 %reduce-scatter.5.cloned.1.call-start = ((), (), s32[]{:S(2)}) async-start(), calls=%async_computation.8 | async-start | bytes 7077888 | tf_op jit(solution)/shard_map/reduce_scatter | solution.py:105
  236.0 7.9 %copy-start.6 = (s32[128,2]{0,1:T(2,128)S(1)}, s32[128,2]{0,1:T(2,128)}, u32[]{:S(2)}) copy-start(s32[128,2]{0,1:T(2,128)} %param.8) | copy-start | bytes 3076
  236.0 80.0 %all-to-all-start.2 = ((bf16[128,5,1536]{2,1,0:T(8,128)(2,1)}), bf16[128,5,1536]{2,1,0:T(8,128)(2,1)S(1)}, u32[]{:S(2)}, u32[]{:S(2)}) async-start(bf16[128,5,1536]{2,1,0:T(8,128)(2,1)} %reshape.195), calls=%async_computation.2 | async-start | bytes 6291456 | tf_op jit(solution)/shard_map/all_to_all | solution.py:87
  318.1 6.1 %copy-start.1 = (bf16[128,1536]{1,0:T(8,128)(2,1)S(1)}, bf16[128,1536]{1,0:T(8,128)(2,1)}, u32[]{:S(2)}) copy-start(bf16[128,1536]{1,0:T(8,128)(2,1)} %param.6) | copy-start | bytes 1179652
Sparse Core Ops, SparseCore 0:
  9.8 22.6 all-gather.4
  34.8 20.9 all-gather.2
  217.5 13.1 reduce-scatter.2
  233.9 19.2 reduce-scatter.4
where the time goes:
time: 332 us; the launch traced here: 331 us
  waiting for transfers between devices  206 us (62%)
  matrix products  37.8 us (11%)
  starting transfers between devices  32.1 us (10%)
  local copies, waits for them, and re-layouts  31.5 us (9%)
  between operations  14 us (4%)
  other arithmetic  9.46 us (3%)
    all_to_all x1, waiting for transfers between devices, per_device(): lax.all_to_all(part, 'expert', split_axis=0, concat_axis=0, tiled=True)  71.8 us
    all_to_all x1, waiting for transfers between devices, per_device(): lax.all_to_all(sent_grads, 'expert', split_axis=0, concat_axis=0, tiled=T...  70.9 us
    all_to_all x1, waiting for transfers between devices, per_device(): lax.all_to_all(sent_tokens, 'expert', split_axis=0, concat_axis=0, tiled=...  61.7 us
    all_to_all x1, starting transfers between devices, per_device(): lax.all_to_all(sent_tokens, 'expert', split_axis=0, concat_axis=0, tiled=...  15.6 us
    dot_general x2, matrix products, contract_rows(): lax.dot_general(left, right, (((0,), (0,)), ((), ())), preferred_element_...  14.6 us
    all_to_all x1, starting transfers between devices, per_device(): lax.all_to_all(sent_grads, 'expert', split_axis=0, concat_axis=0, tiled=T...  8.28 us
    dot_general x1, matrix products, expert_half(): pre = jnp.dot(token_rows, w_first, preferred_element_type=jnp.float32)  8.02 us
    dot_general x1, matrix products, expert_half(): lax.dot_general(grad_rows, w_second, (((1,), (1,)), ((), ())), preferred_...  8.02 us
  transfers between devices with their start and end apart: 7, of which 3 were waited for; matrix products, arithmetic and copies ran while one was open for 19% of the time, Pallas kernels for 0%

commit v1 on v0

v1 whole, which is shorter than its diff:
```python
import functools

import jax
import jax.numpy as jnp
from jax import lax
from jax.experimental import pallas as pl
from jax.experimental.pallas import tpu as pltpu
from jax.sharding import PartitionSpec as P

ROOT_TWO_PI = 0.7978845608
CUBIC = 0.044715
BF = jnp.bfloat16
F32 = jnp.float32
D = 1536
TOK = 128
EXPERTS = 64
BLOCK = 768


def iota(shape, dim):
    return lax.broadcasted_iota(jnp.int32, shape, dim)


def mask(condition):
    return jnp.where(condition, 1.0, 0.0).astype(BF)


def dot(a, b):
    return jnp.dot(a, b, preferred_element_type=F32)


def dot_nt(a, b):
    return lax.dot_general(a, b, (((1,), (1,)), ((), ())), preferred_element_type=F32)


def dot_tn(a, b):
    return lax.dot_general(a, b, (((0,), (0,)), ((), ())), preferred_element_type=F32)


def whole(shape):
    return pl.BlockSpec(shape, lambda *_: (0,) * len(shape))


def params(mib=40):
    return pltpu.CompilerParams(vmem_limit_bytes=mib * 2**20)


def slot_matches(routes_t):
    expert = iota((EXPERTS * 8, TOK), 0) >> 3
    first = routes_t[0:1, :] == expert
    match = first | (routes_t[1:2, :] == expert)
    earlier = mask(iota((TOK, TOK), 0) < iota((TOK, TOK), 1))
    rank = dot(mask(match), earlier)
    return first, match, rank


def pack_kernel(routes_ref, gates_ref, tokens_ref, grads_ref, main_ref, last_ref):
    first, match, rank = slot_matches(routes_ref[...])
    gate = jnp.where(first, gates_ref[0:1, :], gates_ref[1:2, :])
    inner = iota((EXPERTS * 8, TOK), 0) & 7

    def scale_of(chosen):
        return jnp.sum(jnp.where(chosen, gate, 0.0), axis=1, keepdims=True)

    place = jnp.where(inner < 3, inner, inner - 3)
    chosen = match & (rank == place.astype(F32)) & (inner < 6)
    from_tokens, from_grads, scale = mask(chosen & (inner < 3)), mask(chosen & (inner >= 3)), scale_of(chosen)
    for j in range(3):
        columns = slice(j * 384, (j + 1) * 384)
        rows = dot(from_tokens, tokens_ref[:, columns])
        rows += dot(from_grads, grads_ref[:, columns]) * scale
        chosen = match & (rank == float(j))
        rows += dot(mask(chosen & (inner == 6)), tokens_ref[:, 1152:])
        rows += dot(mask(chosen & (inner == 7)), grads_ref[:, 1152:]) * scale_of(chosen)
        main_ref[:, columns] = rows.astype(BF)

    quarter = inner & 3
    chosen = match & (rank == (3 + (quarter & 1)).astype(F32))
    scale = scale_of(chosen)
    rows = jnp.zeros((EXPERTS * 8, 768), F32)
    for j in range(2):
        side = chosen & ((inner >> 2) == j)
        columns = slice(j * 768, (j + 1) * 768)
        rows += dot(mask(side & (quarter < 2)), tokens_ref[:, columns])
        rows += dot(mask(side & (quarter >= 2)), grads_ref[:, columns]) * scale
    last = rows.astype(BF)
    last_ref[0:512, :] = last
    last_ref[512:1024, :] = last


def pack(routes_t, gates_t, tokens, out_grad):
    return pl.pallas_call(
        pack_kernel,
        out_shape=(
            jax.ShapeDtypeStruct((512, 1152), BF),
            jax.ShapeDtypeStruct((1024, 768), BF),
        ),
        compiler_params=params(),
        cost_estimate=pl.CostEstimate(flops=10**9, bytes_accessed=5 * 10**6, transcendentals=0),
        name="pack",
    )(routes_t, gates_t, tokens, out_grad)


def unpack(last, got_ref, token_ref, grad_ref):
    row, column = iota((256, 256), 0), iota((256, 256), 1)
    move = mask(column == ((row & 31) << 3) + (row >> 5))
    for g in range(got_ref.shape[0] // 256):
        rows = dot(move, got_ref[g * 256:(g + 1) * 256, :]).astype(BF)
        if last:
            for j in range(2):
                columns = slice(j * 768, (j + 1) * 768)
                token_ref[g * 64:(g + 1) * 64, columns] = rows[j * 128:j * 128 + 64]
                grad_ref[g * 64:(g + 1) * 64, columns] = rows[j * 128 + 64:j * 128 + 128]
        else:
            token_ref[g * 96:(g + 1) * 96, :1152] = rows[:96]
            grad_ref[g * 96:(g + 1) * 96, :1152] = rows[96:192]
            for j in range(3):
                target = slice(g * 96 + j * 32, g * 96 + (j + 1) * 32)
                token_ref[target, 1152:] = rows[192:224, j * 384:(j + 1) * 384]
                grad_ref[target, 1152:] = rows[224:256, j * 384:(j + 1) * 384]


def expert_kernel(last, group_ref, got_ref, w1_ref, w2_ref, token_ref, grad_ref, hidden_ref, dpre_ref, *rest):
    *part_refs, total = rest
    step = pl.program_id(0)

    @pl.when(step == 0)
    def _():
        unpack(last, got_ref, token_ref, grad_ref)

    pre = dot(token_ref[...], w1_ref[...])
    back = dot_nt(grad_ref[...], w2_ref[...])
    square = pre * pre
    th = jnp.tanh(ROOT_TWO_PI * (pre + CUBIC * square * pre))
    half = 0.5 * (1.0 + th)
    hidden_ref[...] = (pre * half).astype(BF)
    slope = half + 0.5 * pre * (1.0 - th * th) * ROOT_TWO_PI * (1.0 + 3.0 * CUBIC * square)
    d_pre = (back * slope).astype(BF)
    dpre_ref[...] = d_pre
    term = dot_nt(d_pre, w1_ref[...])

    @pl.when(step == 0)
    def _():
        total[...] = term

    @pl.when(step > 0)
    def _():
        total[...] += term

    @pl.when(step == pl.num_programs(0) - 1)
    def _():
        if last:
            for k, part_ref in enumerate(part_refs):
                group = group_ref[0] if k == 0 else 1 - group_ref[0]
                part_ref[...] = total[pl.ds(pl.multiple_of(group * 128, 128), 128), :].astype(BF)
        else:
            part_refs[0][...] = total[...].astype(BF)


def expert_rows(last, group, got, w1, w2):
    rows = 256 if last else 192
    parts = [(128, D)] * 2 if last else [(192, D)]
    hidden_units = w1.shape[1]
    row_shape = jax.ShapeDtypeStruct((rows, D), BF)
    hid_shape = jax.ShapeDtypeStruct((rows, hidden_units), BF)
    return pl.pallas_call(
        functools.partial(expert_kernel, last),
        grid=(hidden_units // BLOCK,),
        in_specs=[
            pl.BlockSpec(memory_space=pltpu.SMEM),
            whole(got.shape),
            pl.BlockSpec((D, BLOCK), lambda h: (0, h)),
            pl.BlockSpec((BLOCK, D), lambda h: (h, 0)),
        ],
        out_specs=(
            whole((rows, D)),
            whole((rows, D)),
            pl.BlockSpec((rows, BLOCK), lambda h: (0, h)),
            pl.BlockSpec((rows, BLOCK), lambda h: (0, h)),
            *(whole(part) for part in parts),
        ),
        out_shape=(
            row_shape, row_shape, hid_shape, hid_shape, *(jax.ShapeDtypeStruct(part, BF) for part in parts)
        ),
        scratch_shapes=[pltpu.VMEM((rows, D), F32)],
        compiler_params=params(32),
        cost_estimate=pl.CostEstimate(
            flops=6 * rows * D * hidden_units, bytes_accessed=14 * 10**6, transcendentals=rows * hidden_units
        ),
        name="expert_last" if last else "expert_main",
    )(group, got, w1, w2)


def merge_kernel(main_a, main_b, last_a, last_b, out_ref):
    row, column = iota((256, 128), 0), iota((256, 128), 1)
    target = ((column & 31) << 3) + (column >> 5)
    row6, column6 = iota((256, 192), 0), iota((256, 192), 1)
    spread = mask(row6 == ((column6 & 31) << 3) + (column6 >> 5))
    for g in range(2):
        a, b = slice(g * 96, (g + 1) * 96), slice(g * 64, (g + 1) * 64)
        three = (main_a[a, :].astype(F32) + main_b[a, :].astype(F32)).astype(BF)
        two = (last_a[b, :].astype(F32) + last_b[b, :].astype(F32)).astype(BF)
        four = jnp.concatenate([three, two[:32]], axis=0)
        folded = dot(mask(row == target), four[:, :768]) + dot(mask(row == target + 4), four[:, 768:])
        out_ref[g * 256:(g + 1) * 256, :768] = folded.astype(BF)
        fifth = jnp.concatenate([two[32:, j * 256:(j + 1) * 256] for j in range(6)], axis=0)
        out_ref[g * 256:(g + 1) * 256, 768:] = dot(spread, fifth).astype(BF)


def merge(*parts):
    return pl.pallas_call(
        merge_kernel,
        out_shape=jax.ShapeDtypeStruct((512, 1024), BF),
        compiler_params=params(),
        cost_estimate=pl.CostEstimate(flops=3 * 10**8, bytes_accessed=3 * 10**6, transcendentals=0),
        name="merge",
    )(*parts)


def combine_kernel(routes_ref, got_ref, out_ref):
    _, match, rank = slot_matches(routes_ref[...])
    inner = iota((EXPERTS * 8, TOK), 0) & 7
    chosen = match & (rank == (inner & 3).astype(F32))
    sides = [mask(chosen & (inner < 4)), mask(chosen & (inner >= 4))]
    chosen = match & (rank == 4.0)
    for j in range(6):
        columns = slice((j % 3) * 256, (j % 3 + 1) * 256)
        total = dot_tn(sides[j // 3], got_ref[:, columns])
        total += dot_tn(mask(chosen & (inner == j)), got_ref[:, 768:])
        out_ref[:, j * 256:(j + 1) * 256] = total.astype(BF)


def combine(routes_t, got):
    return pl.pallas_call(
        combine_kernel,
        out_shape=jax.ShapeDtypeStruct((TOK, D), BF),
        compiler_params=params(),
        cost_estimate=pl.CostEstimate(flops=4 * 10**8, bytes_accessed=2 * 10**6, transcendentals=0),
        name="combine",
    )(routes_t, got)


def per_device(tokens, out_grad, routes, gate_probs, weight_in, weight_out):
    chips = [(i, i ^ 1) for i in range(128)]
    cores = [(0, 1), (1, 0)]
    outer = [4 * i + x for i in range(32) for x in (0, 3)]
    inner = [4 * i + x for i in range(32) for x in (1, 2)]
    halves, everyone = [outer, inner], [outer + inner]
    place = lax.axis_index("expert") & 3
    group = jnp.where((place == 1) | (place == 2), 1, 0).astype(jnp.int32).reshape(1)
    core = lax.axis_index("dp")
    fence = lax.optimization_barrier

    def exchange(rows, groups):
        count = len(groups[0])
        chunked = rows.reshape(count, rows.shape[0] // count, rows.shape[1])
        got = lax.all_to_all(
            chunked, "expert", split_axis=0, concat_axis=0, tiled=True, axis_index_groups=groups
        )
        return got.reshape(rows.shape)

    def gather(weight, axis):
        other = lax.ppermute(weight, "dp", cores)
        first, second = jnp.where(core == 0, weight, other), jnp.where(core == 0, other, weight)
        return jnp.concatenate([first, second], axis=axis)

    routes_t, gates_t = routes.T, gate_probs.T
    send_main, send_last = pack(routes_t, gates_t, tokens, out_grad)
    weight_in, weight_out, send_main = fence((weight_in, weight_out, send_main))
    w1, w2 = gather(weight_in, 0), gather(weight_out, 1)
    own_got = exchange(send_main, halves)
    pair_got = lax.ppermute(own_got, "expert", chips)
    send_last, _ = fence((send_last, own_got[:8, :128] + 1))
    last_got = exchange(send_last, everyone)
    own = expert_rows(False, group, own_got, w1, w2)
    pair_got, _ = fence((pair_got, own[4]))
    pair = expert_rows(False, group, pair_got, w1, w2)
    other_main = lax.ppermute(pair[4], "expert", chips)
    last_got, pair_part = fence((last_got, pair[4]))
    last = expert_rows(True, group, last_got, w1, w2)
    other_last = lax.ppermute(last[5], "expert", chips)
    merged = merge(own[4], other_main, last[4], other_last)
    got = exchange(merged, halves)

    token_all, grad_all, hidden_all, dpre_all = (
        jnp.concatenate([own[i], pair[i], last[i]], axis=0) for i in range(4)
    )

    def half(rows, index):
        return lax.dynamic_slice_in_dim(rows, index * (D // 2), D // 2, axis=1)

    def gradients(index, after):
        tokens, grads, hidden, d_pre, _ = fence((token_all, grad_all, hidden_all, dpre_all, after))
        return dot_tn(half(tokens, index), d_pre), dot_tn(hidden, half(grads, index))

    sent_in, sent_out = (lax.ppermute(v.astype(BF), "dp", cores) for v in gradients(1 - core, other_main))
    kept_in, kept_out = gradients(core, merged)
    grad_in = (kept_in + sent_in.astype(F32)).astype(BF)
    grad_out = (kept_out + sent_out.astype(F32)).astype(BF)
    got, grad_in, grad_out = fence((got, grad_in, grad_out))
    return combine(routes_t, got), grad_in, grad_out


def solution(mesh):
    return jax.shard_map(
        per_device,
        mesh=mesh,
        in_specs=(
            P(("dp", "expert"), None),
            P(("dp", "expert"), None),
            P(("dp", "expert"), None),
            P(("dp", "expert"), None),
            P("dp", "expert"),
            P("expert", "dp"),
        ),
        out_specs=(P(("dp", "expert"), None), P("dp", "expert"), P("expert", "dp")),
        check_vma=False,
    )
```

time: 332 us -> 192 us (0.58)
  waiting for transfers between devices: 206 us -> 85.6 us
  Pallas kernels: 0 us -> 25.5 us
  matrix products: 37.8 us -> 17.7 us
  local copies, waits for them, and re-layouts: 31.5 us -> 15.9 us
  between operations: 14 us -> 0.97 us
  starting transfers between devices: 32.1 us -> 38.3 us
    all_to_all x3, waiting for transfers between devices: 204 us -> 50.4 us  [exchange(): lax.all_to_all(chunked, 'expert', split_axis=0, concat_axis=0, tiled=True...]
    ppermute x0 -> x7, waiting for transfers between devices: none -> 35.2 us  [the longest x1 25.4 us: per_device(): pair_got = lax.ppermute(own_got, 'expert', chips)]
    pallas_call x0 -> x6, Pallas kernels: none -> 25.5 us  [the longest x3 17.2 us: expert_rows(): pl.pallas_call(functools.partial(expert_kernel, last), grid=(hidden_units...]
    dot_general x5 -> x4, matrix products: 37.8 us -> 17.7 us  [dot_tn(): lax.dot_general(a, b, (((0,), (0,)), ((), ())), preferred_element_type=F32)]
    unnamed x20 -> x54, local copies, waits for them, and re-layouts: 2.21 us -> 15.6 us
    reshape x7 -> x0, local copies, waits for them, and re-layouts: 9.85 us -> none  [the longest x1 2.99 us: per_device(): grad_recv = got_grads.reshape(-1, width)]
    gather x5 -> x0, local copies, waits for them, and re-layouts: 9.33 us -> none  [the longest x1 2.74 us: pack_rows(): tokens[token_index].astype(jnp.float32) * filled]
    select_n x2, other arithmetic: 0.04 us -> 7.07 us  [gather(): jnp.where(core == 0, weight, other)]
  transfers between devices with their start and end apart: 7 -> 10, of which waited for: 3 -> 4; matrix products, arithmetic and copies ran while one was open for 19% -> 13% of each run, Pallas kernels for 0% -> 10%
where the time goes in v1:
time: 192 us
  waiting for transfers between devices  85.6 us (45%)
  starting transfers between devices  38.3 us (20%)
  Pallas kernels  25.5 us (13%)
  matrix products  17.7 us (9%)
  local copies, waits for them, and re-layouts  15.9 us (8%)
  other arithmetic  7.74 us (4%)
    all_to_all x3, waiting for transfers between devices, exchange(): lax.all_to_all(chunked, 'expert', split_axis=0, concat_axis=0, tiled=True...  50.4 us
    all_to_all x3, starting transfers between devices, exchange(): lax.all_to_all(chunked, 'expert', split_axis=0, concat_axis=0, tiled=True...  33.5 us
    ppermute x1, waiting for transfers between devices, per_device(): pair_got = lax.ppermute(own_got, 'expert', chips)  25.4 us
    dot_general x4, matrix products, dot_tn(): lax.dot_general(a, b, (((0,), (0,)), ((), ())), preferred_element_type=F32)  17.7 us
    pallas_call x3, Pallas kernels, expert_rows(): pl.pallas_call(functools.partial(expert_kernel, last), grid=(hidden_units...  17.2 us
    unnamed x54, local copies, waits for them, and re-layouts  15.6 us
    ppermute x1, waiting for transfers between devices, per_device(): other_last = lax.ppermute(last[5], 'expert', chips)  9.71 us
    select_n x2, other arithmetic, gather(): jnp.where(core == 0, weight, other)  7.07 us
  transfers between devices with their start and end apart: 10, of which 4 were waited for; matrix products, arithmetic and copies ran while one was open for 13% of the time, Pallas kernels for 10%

profile of v1, /device:TPU:8, one launch (start us, length us, event | category | flops | bytes accessed | tf_op | source)
XLA Modules:
  0.0 191.6 jit_solution(12452761457896372072)
XLA Ops:
  0.6 1.0 copy-done.8
  1.6 1.0 copy-done.9
  2.6 0.7 copy-done.10
  3.3 0.7 copy-done.11
  4.0 3.8 %pack.1 = (bf16[512,1152]{1,0:T(8,128)(2,1)}, bf16[1024,768]{1,0:T(8,128)(2,1)}) custom-call(s32[2,128]{1,0:T(2,128)S(1)} %bitcast.18, f32[2,128]{1,0:T(2,128)S(1)} %bitcast.17, bf16[128,1536]{1,0:T(8,128)(2,1)S(1)} %copy-done.8, bf16[128,1536]{1,0:T(8,128)(2,1)S(1)} %copy-done.9), custom_call_target="tpu_custom_call" | custom-call | flops 1000000000 | bytes 5000000 | tf_op jit(solution)/shard_map/pack/pallas_call | solution.py:92
  7.8 0.0 collective-permute-start
  7.8 14.3 %all-to-all-start = ((bf16[64,8,1152]{2,1,0:T(8,128)(2,1)}), bf16[64,8,1152]{2,1,0:T(8,128)(2,1)S(1)}, u32[]{:S(2)}, u32[]{:S(2)}) async-start(bf16[64,8,1152]{2,1,0:T(8,128)(2,1)} %bitcast.3), calls=%async_computation | async-start | bytes 2359296 | tf_op jit(solution)/shard_map/all_to_all | solution.py:257
  22.1 0.1 collective-permute-start.1
  22.2 32.8 %all-to-all-done = bf16[64,8,1152]{2,1,0:T(8,128)(2,1)S(1)} async-done(((bf16[64,8,1152]{2,1,0:T(8,128)(2,1)}), bf16[64,8,1152]{2,1,0:T(8,128)(2,1)S(1)}, u32[]{:S(2)}, u32[]{:S(2)}) %all-to-all-start) | async-done | bytes 1179680 | tf_op jit(solution)/shard_map/all_to_all | solution.py:257
  55.0 7.4 %all-to-all-start.1 = ((bf16[128,8,768]{2,1,0:T(8,128)(2,1)}), bf16[128,8,768]{2,1,0:T(8,128)(2,1)S(1)}, u32[]{:S(2)}, u32[]{:S(2)}) async-start(bf16[128,8,768]{2,1,0:T(8,128)(2,1)} %bitcast.5), calls=%async_computation.1 | async-start | bytes 3145728 | tf_op jit(solution)/shard_map/all_to_all | solution.py:257
  62.4 2.2 %collective-permute-start.2 = (bf16[512,1152]{1,0:T(8,128)(2,1)S(1)}, bf16[512,1152]{1,0:T(8,128)(2,1)S(1)}, u32[]{:S(2)}, u32[]{:S(2)}) collective-permute-start(bf16[512,1152]{1,0:T(8,128)(2,1)S(1)} %bitcast.13), channel_id=1, source_target_pairs={{0,1},{1,0},{2,3},{3,2},{4,5},{5,4},{6,7},{7,6},{8,9},{9,8},{10,11... | collective-permute-start | bytes 3538952 | tf_op jit(solution)/shard_map/ppermute | solution.py:272
  64.6 2.7 %broadcast_select_fusion.3 = (bf16[768,1536]{1,0:T(8,128)(2,1)S(1)}, bf16[768,1536]{1,0:T(8,128)(2,1)S(1)}) fusion(bf16[768,1536]{1,0:T(8,128)(2,1)} %param.10, bf16[768,1536]{1,0:T(8,128)(2,1)} %collective-permute-done, pred[]{:T(512)S(6)} %eq.14), kind=kLoop, calls=%fused_computation.9 | loop fusion | flops 2359296 | bytes 9437185 | tf_op jit(solution)/shard_map/jit(_where)/select_n | solution.py:264
  67.3 0.3 pad_maximum_fusion.w1_ref
  67.6 4.4 %broadcast_select_fusion.1 = (bf16[1536,768]{1,0:T(8,128)(2,1)S(1)}, bf16[1536,768]{1,0:T(8,128)(2,1)S(1)}) fusion(bf16[1536,768]{1,0:T(8,128)(2,1)} %param.11, bf16[1536,768]{1,0:T(8,128)(2,1)} %collective-permute-done.1, pred[]{:T(512)S(6)} %eq.14), kind=kLoop, calls=%fused_computation.7 | loop fusion | flops 2359296 | bytes 9437185 | tf_op jit(solution)/shard_map/jit(_where)/select_n | solution.py:264
  72.0 0.4 pad_maximum_fusion.1.w2_ref
  72.4 5.5 %expert_main.2 = (bf16[192,1536]{1,0:T(8,128)(2,1)S(1)}, bf16[192,1536]{1,0:T(8,128)(2,1)S(1)}, bf16[192,1536]{1,0:T(8,128)(2,1)S(1)}, bf16[192,1536]{1,0:T(8,128)(2,1)S(1)}, bf16[192,1536]{1,0:T(8,128)(2,1)S(1)}) custom-call(s32[1]{0:T(128)} %bitcast.1.group_ref, bf16[512,1152]{1,0:T(8,128)(2,1)S(1)} %bitcast.14, ...), custom_call_target="tpu_custom_call" | custom-call | flops 2717908992 | bytes 14000000 | tf_op jit(solution)/shard_map/expert_main/pallas_call | solution.py:166
  77.9 1.2 constant_dynamic-update-slice_fusion.2
  79.1 1.1 constant_dynamic-update-slice_fusion.8
  80.2 25.4 %collective-permute-done.2.got_ref = bf16[512,1152]{1,0:T(8,128)(2,1)S(1)} collective-permute-done((bf16[512,1152]{1,0:T(8,128)(2,1)S(1)}, bf16[512,1152]{1,0:T(8,128)(2,1)S(1)}, u32[]{:S(2)}, u32[]{:S(2)}) %collective-permute-start.2) | collective-permute-done | bytes 1179680 | tf_op jit(solution)/shard_map/ppermute | solution.py:272
  105.6 6.3 %expert_main.3 = (bf16[192,1536]{1,0:T(8,128)(2,1)S(1)}, bf16[192,1536]{1,0:T(8,128)(2,1)S(1)}, bf16[192,1536]{1,0:T(8,128)(2,1)S(1)}, bf16[192,1536]{1,0:T(8,128)(2,1)S(1)}, bf16[192,1536]{1,0:T(8,128)(2,1)}) custom-call(s32[1]{0:T(128)} %bitcast.1.group_ref, bf16[512,1152]{1,0:T(8,128)(2,1)S(1)} %collective-permute-done.2.got_ref, ...), custom_call_target="tpu_custom_call" | custom-call | flops 2717908992 | bytes 14000000 | tf_op jit(solution)/shard_map/expert_main/pallas_call | solution.py:166
  111.9 0.8 copy-done.4
  112.8 0.7 collective-permute-start.3
  113.4 2.3 %copy-done.1 = bf16[1536,1536]{1,0:T(8,128)(2,1)S(1)} copy-done((bf16[1536,1536]{1,0:T(8,128)(2,1)S(1)}, bf16[1536,1536]{1,0:T(8,128)(2,1)}, u32[]{:S(2)}) %copy-start.1) | copy-done | bytes 4718616
  115.8 2.3 %copy-done.3 = bf16[1536,1536]{1,0:T(8,128)(2,1)S(1)} copy-done((bf16[1536,1536]{1,0:T(8,128)(2,1)S(1)}, bf16[1536,1536]{1,0:T(8,128)(2,1)}, u32[]{:S(2)}) %copy-start.3) | copy-done | bytes 4718616
  118.1 5.4 %expert_last.1 = (bf16[256,1536]{1,0:T(8,128)(2,1)S(1)}, bf16[256,1536]{1,0:T(8,128)(2,1)S(1)}, bf16[256,1536]{1,0:T(8,128)(2,1)S(1)}, bf16[256,1536]{1,0:T(8,12...) custom-call(s32[1]{0:T(128)} %bitcast.1.group_ref, bf16[1024,768]{1,0:T(8,128)(2,1)S(1)} %bitcast.15, ...), custom_call_target="tpu_custom_call" | custom-call | flops 3623878656 | bytes 14000000 | tf_op jit(solution)/shard_map/expert_last/pallas_call | solution.py:166
  123.6 0.0 copy-start.16
  123.6 0.1 constant_dynamic-update-slice_fusion
  123.7 2.1 %copy-done.19 = bf16[640,1536]{1,0:T(8,128)(2,1)S(1)} copy-done((bf16[640,1536]{1,0:T(8,128)(2,1)S(1)}, bf16[640,1536]{1,0:T(8,128)(2,1)}, u32[]{:S(2)}) %copy-start.19) | copy-done | bytes 1966104
  125.8 0.1 constant_dynamic-update-slice_fusion.3
  125.9 0.5 copy-done.16
  126.4 1.7 copy-done.13
  128.2 0.1 constant_dynamic-update-slice_fusion.6
  128.3 0.1 constant_dynamic-update-slice_fusion.9
  128.3 0.0 copy-start.14
  128.3 0.0 collective-permute-done.3.main_b
  128.4 3.5 %convolution_convert_fusion.1 = bf16[768,1536]{1,0:T(8,128)(2,1)} fusion(bf16[640,1536]{1,0:T(8,128)(2,1)S(1)} %constant_dynamic-update-slice_fusion.9, bf16[640,1536]{1,0:T(8,128)(2,1)S(1)} %constant_dynamic-update-slice_fusion, s32[]{:T(128)S(6)} %select_n.44), kind=kOutput, calls=%fused_computation.5 | convolution fusion | flops 1511129088 | bytes 5308420 | tf_op jit(solution)/shard_map/dot_general | solution.py:37
  131.8 0.0 collective-permute-start.5
  131.9 3.5 %convolution_convert_fusion = bf16[1536,768]{1,0:T(8,128)(2,1)} fusion(bf16[640,1536]{1,0:T(8,128)(2,1)S(1)} %constant_dynamic-update-slice_fusion.6, bf16[640,1536]{1,0:T(8,128)(2,1)S(1)} %constant_dynamic-update-slice_fusion.3, s32[]{:T(128)S(6)} %select_n.44), kind=kOutput, calls=%fused_computation.4 | convolution fusion | flops 1511129088 | bytes 5308420 | tf_op jit(solution)/shard_map/dot_general | solution.py:37
  135.4 0.5 collective-permute-start.6
  135.8 1.3 collective-permute-start.4
  137.2 9.7 %collective-permute-done.4.last_b = bf16[128,1536]{1,0:T(8,128)(2,1)S(1)} collective-permute-done((bf16[128,1536]{1,0:T(8,128)(2,1)S(1)}, bf16[128,1536]{1,0:T(8,128)(2,1)S(1)}, u32[]{:S(2)}, u32[]{:S(2)}) %collective-permute-start.4) | collective-permute-done | bytes 393248 | tf_op jit(solution)/shard_map/ppermute | solution.py:281
  146.9 2.8 %merge.1 = bf16[512,1024]{1,0:T(8,128)(2,1)} custom-call(bf16[192,1536]{1,0:T(8,128)(2,1)S(1)} %copy-done.7, bf16[192,1536]{1,0:T(8,128)(2,1)} %collective-permute-done.3.main_b, bf16[128,1536]{1,0:T(8,128)(2,1)S(1)} %get-tuple-element.46.last_a, bf16[128,1536]{1,0:T(8,128)(2,1)S(1)} %collective-permute-done.4.last_b), custom_call_target="tpu_custom_call" | custom-call | flops 300000000 | bytes 3000000 | tf_op jit(solution)/shard_map/merge/pallas_call | solution.py:211
  149.7 11.8 %all-to-all-start.2 = ((bf16[64,8,1024]{2,1,0:T(8,128)(2,1)}), bf16[64,8,1024]{2,1,0:T(8,128)(2,1)S(1)}, u32[]{:S(2)}, u32[]{:S(2)}) async-start(bf16[64,8,1024]{2,1,0:T(8,128)(2,1)} %bitcast.7), calls=%async_computation.2 | async-start | bytes 2097152 | tf_op jit(solution)/shard_map/all_to_all | solution.py:257
  161.6 0.0 collective-permute-done.5
  161.6 5.6 %add_convert_fusion.1 = bf16[768,1536]{1,0:T(8,128)(2,1)} fusion(bf16[768,1536]{1,0:T(8,128)(2,1)} %collective-permute-done.5, bf16[640,1536]{1,0:T(8,128)(2,1)S(1)} %copy-done.15, bf16[640,1536]{1,0:T(8,128)(2,1)} %copy-done.23, s32[]{:T(128)S(6)} %select_n.43), kind=kOutput, calls=%fused_computation.3 | convolution fusion | flops 1513488384 | bytes 7667716 | tf_op jit(solution)/shard_map/dot_general | solution.py:37
  167.2 5.2 %add_convert_fusion = bf16[1536,768]{1,0:T(8,128)(2,1)} fusion(bf16[1536,768]{1,0:T(8,128)(2,1)} %collective-permute-done.6, bf16[640,1536]{1,0:T(8,128)(2,1)S(1)} %copy-done.18, bf16[640,1536]{1,0:T(8,128)(2,1)S(1)} %copy-done.21, s32[]{:T(128)S(6)} %select_n.43), kind=kOutput, calls=%fused_computation.2 | convolution fusion | flops 1513488384 | bytes 7667716 | tf_op jit(solution)/shard_map/dot_general | solution.py:37
  172.3 17.6 %all-to-all-done.2 = bf16[64,8,1024]{2,1,0:T(8,128)(2,1)S(1)} async-done(((bf16[64,8,1024]{2,1,0:T(8,128)(2,1)}), bf16[64,8,1024]{2,1,0:T(8,128)(2,1)S(1)}, u32[]{:S(2)}, u32[]{:S(2)}) %all-to-all-start.2) | async-done | bytes 1048608 | tf_op jit(solution)/shard_map/all_to_all | solution.py:257
  189.9 1.7 combine.1
  (44 shorter events, 0.2 us)
Async XLA Ops:
  0.6 1.0 copy-start.8
  1.6 1.0 copy-start.9
  2.6 0.7 copy-start.10
  3.3 0.7 copy-start.11
  7.8 56.8 %collective-permute-start = (bf16[768,1536]{1,0:T(8,128)(2,1)}, bf16[768,1536]{1,0:T(8,128)(2,1)}, u32[]{:S(2)}, u32[]{:S(2)}) collective-permute-start(bf16[768,1536]{1,0:T(8,128)(2,1)} %param.10), channel_id=1, source_target_pairs={{0,128},{128,0},{1,129},{129,1},{2,130},{130,2},{3,131},{131,3},{4... | collective-permute-start | bytes 7077896 | tf_op jit(solution)/shard_map/ppermute | solution.py:263
  7.8 47.3 %all-to-all-start = ((bf16[64,8,1152]{2,1,0:T(8,128)(2,1)}), bf16[64,8,1152]{2,1,0:T(8,128)(2,1)S(1)}, u32[]{:S(2)}, u32[]{:S(2)}) async-start(bf16[64,8,1152]{2,1,0:T(8,128)(2,1)} %bitcast.3), calls=%async_computation | async-start | bytes 2359296 | tf_op jit(solution)/shard_map/all_to_all | solution.py:257
  22.1 45.5 %collective-permute-start.1 = (bf16[1536,768]{1,0:T(8,128)(2,1)}, bf16[1536,768]{1,0:T(8,128)(2,1)}, u32[]{:S(2)}, u32[]{:S(2)}) collective-permute-start(bf16[1536,768]{1,0:T(8,128)(2,1)} %param.11), channel_id=1, source_target_pairs={{0,128},{128,0},{1,129},{129,1},{2,130},{130,2},{3,131},{131,3},{4... | collective-permute-start | bytes 7077896 | tf_op jit(solution)/shard_map/ppermute | solution.py:263
  55.0 58.4 %all-to-all-start.1 = ((bf16[128,8,768]{2,1,0:T(8,128)(2,1)}), bf16[128,8,768]{2,1,0:T(8,128)(2,1)S(1)}, u32[]{:S(2)}, u32[]{:S(2)}) async-start(bf16[128,8,768]{2,1,0:T(8,128)(2,1)} %bitcast.5), calls=%async_computation.1 | async-start | bytes 3145728 | tf_op jit(solution)/shard_map/all_to_all | solution.py:257
  62.4 43.2 %collective-permute-start.2 = (bf16[512,1152]{1,0:T(8,128)(2,1)S(1)}, bf16[512,1152]{1,0:T(8,128)(2,1)S(1)}, u32[]{:S(2)}, u32[]{:S(2)}) collective-permute-start(bf16[512,1152]{1,0:T(8,128)(2,1)S(1)} %bitcast.13), channel_id=1, source_target_pairs={{0,1},{1,0},{2,3},{3,2},{4,5},{5,4},{6,7},{7,6},{8,9},{9,8},{10,11... | collective-permute-start | bytes 3538952 | tf_op jit(solution)/shard_map/ppermute | solution.py:272
  67.6 38.0 %copy-start = (bf16[1536,1536]{1,0:T(8,128)(2,1)}, bf16[1536,1536]{1,0:T(8,128)(2,1)S(1)}, u32[]{:S(2)}) copy-start(bf16[1536,1536]{1,0:T(8,128)(2,1)S(1)} %pad_maximum_fusion.w1_ref) | copy-start | bytes 14155780
  72.4 33.2 %copy-start.2 = (bf16[1536,1536]{1,0:T(8,128)(2,1)}, bf16[1536,1536]{1,0:T(8,128)(2,1)S(1)}, u32[]{:S(2)}) copy-start(bf16[1536,1536]{1,0:T(8,128)(2,1)S(1)} %pad_maximum_fusion.1.w2_ref) | copy-start | bytes 14155780
  77.9 2.3 %copy-start.6 = (bf16[192,1536]{1,0:T(8,128)(2,1)}, bf16[192,1536]{1,0:T(8,128)(2,1)S(1)}, u32[]{:S(2)}) copy-start(bf16[192,1536]{1,0:T(8,128)(2,1)S(1)} %get-tuple-element.41.main_a) | copy-start | bytes 1769476
  111.9 0.8 copy-start.4
  112.8 15.6 %collective-permute-start.3 = (bf16[192,1536]{1,0:T(8,128)(2,1)}, bf16[192,1536]{1,0:T(8,128)(2,1)}, u32[]{:S(2)}, u32[]{:S(2)}) collective-permute-start(bf16[192,1536]{1,0:T(8,128)(2,1)} %get-tuple-element.43), channel_id=1, source_target_pairs={{0,1},{1,0},{2,3},{3,2},{4,5},{5,4},{6,7},{7,6},{8,9},{9,8},{10,11... | collective-permute-start | bytes 1769480 | tf_op jit(solution)/shard_map/ppermute | solution.py:278
  113.4 2.3 %copy-start.1 = (bf16[1536,1536]{1,0:T(8,128)(2,1)S(1)}, bf16[1536,1536]{1,0:T(8,128)(2,1)}, u32[]{:S(2)}) copy-start(bf16[1536,1536]{1,0:T(8,128)(2,1)} %copy-done) | copy-start | bytes 14155780
  115.8 2.3 %copy-start.3 = (bf16[1536,1536]{1,0:T(8,128)(2,1)S(1)}, bf16[1536,1536]{1,0:T(8,128)(2,1)}, u32[]{:S(2)}) copy-start(bf16[1536,1536]{1,0:T(8,128)(2,1)} %copy-done.2) | copy-start | bytes 14155780
  118.1 5.4 %copy-start.5 = (bf16[192,1536]{1,0:T(8,128)(2,1)S(1)}, bf16[192,1536]{1,0:T(8,128)(2,1)}, u32[]{:S(2)}) copy-start(bf16[192,1536]{1,0:T(8,128)(2,1)} %copy-done.4) | copy-start | bytes 1769476
  118.1 5.4 %copy-start.22 = (bf16[640,1536]{1,0:T(8,128)(2,1)S(1)}, bf16[640,1536]{1,0:T(8,128)(2,1)}, u32[]{:S(2)}) copy-start(bf16[640,1536]{1,0:T(8,128)(2,1)} %get-tuple-element.75) | copy-start | bytes 5898244
  123.5 2.3 %copy-start.19 = (bf16[640,1536]{1,0:T(8,128)(2,1)S(1)}, bf16[640,1536]{1,0:T(8,128)(2,1)}, u32[]{:S(2)}) copy-start(bf16[640,1536]{1,0:T(8,128)(2,1)} %get-tuple-element.76) | copy-start | bytes 5898244
  123.6 2.8 %copy-start.16 = (bf16[640,1536]{1,0:T(8,128)(2,1)S(1)}, bf16[640,1536]{1,0:T(8,128)(2,1)}, u32[]{:S(2)}) copy-start(bf16[640,1536]{1,0:T(8,128)(2,1)} %get-tuple-element.77) | copy-start | bytes 5898244
  123.7 4.7 %copy-start.23 = (bf16[640,1536]{1,0:T(8,128)(2,1)}, bf16[640,1536]{1,0:T(8,128)(2,1)S(1)}, u32[]{:S(2)}) copy-start(bf16[640,1536]{1,0:T(8,128)(2,1)S(1)} %constant_dynamic-update-slice_fusion) | copy-start | bytes 5898244
  125.8 2.4 %copy-start.13 = (bf16[640,1536]{1,0:T(8,128)(2,1)S(1)}, bf16[640,1536]{1,0:T(8,128)(2,1)}, u32[]{:S(2)}) copy-start(bf16[640,1536]{1,0:T(8,128)(2,1)} %get-tuple-element.78) | copy-start | bytes 5898244
  125.9 6.0 %copy-start.20 = (bf16[640,1536]{1,0:T(8,128)(2,1)}, bf16[640,1536]{1,0:T(8,128)(2,1)S(1)}, u32[]{:S(2)}) copy-start(bf16[640,1536]{1,0:T(8,128)(2,1)S(1)} %constant_dynamic-update-slice_fusion.3) | copy-start | bytes 5898244
  128.3 3.6 %copy-start.17 = (bf16[640,1536]{1,0:T(8,128)(2,1)}, bf16[640,1536]{1,0:T(8,128)(2,1)S(1)}, u32[]{:S(2)}) copy-start(bf16[640,1536]{1,0:T(8,128)(2,1)S(1)} %constant_dynamic-update-slice_fusion.6) | copy-start | bytes 5898244
  128.3 3.5 %copy-start.14 = (bf16[640,1536]{1,0:T(8,128)(2,1)}, bf16[640,1536]{1,0:T(8,128)(2,1)S(1)}, u32[]{:S(2)}) copy-start(bf16[640,1536]{1,0:T(8,128)(2,1)S(1)} %constant_dynamic-update-slice_fusion.9) | copy-start | bytes 5898244
  131.8 15.1 %copy-start.7 = (bf16[192,1536]{1,0:T(8,128)(2,1)S(1)}, bf16[192,1536]{1,0:T(8,128)(2,1)}, u32[]{:S(2)}) copy-start(bf16[192,1536]{1,0:T(8,128)(2,1)} %copy-done.6) | copy-start | bytes 1769476
  131.8 29.7 %collective-permute-start.5 = (bf16[768,1536]{1,0:T(8,128)(2,1)}, bf16[768,1536]{1,0:T(8,128)(2,1)}, u32[]{:S(2)}, u32[]{:S(2)}) collective-permute-start(bf16[768,1536]{1,0:T(8,128)(2,1)} %convolution_convert_fusion.1), channel_id=1, source_target_pairs={{0,128},{128,0},{1,129},{129,1},{2,130},{130,2},{3,131},{131,3},{4... | collective-permute-start | bytes 7077896 | tf_op jit(solution)/shard_map/ppermute | solution.py:296
  135.4 31.8 %collective-permute-start.6 = (bf16[1536,768]{1,0:T(8,128)(2,1)}, bf16[1536,768]{1,0:T(8,128)(2,1)}, u32[]{:S(2)}, u32[]{:S(2)}) collective-permute-start(bf16[1536,768]{1,0:T(8,128)(2,1)} %convolution_convert_fusion), channel_id=1, source_target_pairs={{0,128},{128,0},{1,129},{129,1},{2,130},{130,2},{3,131},{131,3},{4... | collective-permute-start | bytes 7077896 | tf_op jit(solution)/shard_map/ppermute | solution.py:296
  135.8 11.1 %collective-permute-start.4 = (bf16[128,1536]{1,0:T(8,128)(2,1)S(1)}, bf16[128,1536]{1,0:T(8,128)(2,1)S(1)}, u32[]{:S(2)}, u32[]{:S(2)}) collective-permute-start(bf16[128,1536]{1,0:T(8,128)(2,1)S(1)} %get-tuple-element.47), channel_id=1, source_target_pairs={{0,1},{1,0},{2,3},{3,2},{4,5},{5,4},{6,7},{7,6},{8,9},{9,8},{10,11... | collective-permute-start | bytes 1179656 | tf_op jit(solution)/shard_map/ppermute | solution.py:281
  146.9 14.7 %copy-start.15 = (bf16[640,1536]{1,0:T(8,128)(2,1)S(1)}, bf16[640,1536]{1,0:T(8,128)(2,1)}, u32[]{:S(2)}) copy-start(bf16[640,1536]{1,0:T(8,128)(2,1)} %copy-done.14) | copy-start | bytes 5898244
  149.7 40.2 %all-to-all-start.2 = ((bf16[64,8,1024]{2,1,0:T(8,128)(2,1)}), bf16[64,8,1024]{2,1,0:T(8,128)(2,1)S(1)}, u32[]{:S(2)}, u32[]{:S(2)}) async-start(bf16[64,8,1024]{2,1,0:T(8,128)(2,1)} %bitcast.7), calls=%async_computation.2 | async-start | bytes 2097152 | tf_op jit(solution)/shard_map/all_to_all | solution.py:257
  161.6 5.6 %copy-start.18 = (bf16[640,1536]{1,0:T(8,128)(2,1)S(1)}, bf16[640,1536]{1,0:T(8,128)(2,1)}, u32[]{:S(2)}) copy-start(bf16[640,1536]{1,0:T(8,128)(2,1)} %copy-done.17) | copy-start | bytes 5898244
  161.6 5.6 %copy-start.21 = (bf16[640,1536]{1,0:T(8,128)(2,1)S(1)}, bf16[640,1536]{1,0:T(8,128)(2,1)}, u32[]{:S(2)}) copy-start(bf16[640,1536]{1,0:T(8,128)(2,1)} %copy-done.20) | copy-start | bytes 5898244
  167.2 22.8 %copy-start.12 = (s32[128,2]{0,1:T(2,128)S(1)}, s32[128,2]{0,1:T(2,128)}, u32[]{:S(2)}) copy-start(s32[128,2]{0,1:T(2,128)} %param.8) | copy-start | bytes 3076

commit v2 on v1

--- a/solution.py
+++ b/solution.py
@@ -14,7 +14,8 @@
 D = 1536
 TOK = 128
 EXPERTS = 64
-BLOCK = 768
+HALF = 768
+SMALL = pl.CostEstimate(flops=1, bytes_accessed=1, transcendentals=0)
 
 
 def iota(shape, dim):
@@ -43,6 +44,31 @@
 
 def params(mib=40):
     return pltpu.CompilerParams(vmem_limit_bytes=mib * 2**20)
+
+
+def in_hbm(x):
+    return pltpu.with_memory_space_constraint(x, pltpu.HBM)
+
+
+def hbm_shape(shape):
+    return pltpu.HBM(shape, BF)
+
+
+def after_kernel(x_ref, earlier_ref, out_ref):
+    pass
+
+
+def after(x, earlier):
+    anywhere = pl.BlockSpec(memory_space=pl.ANY)
+    return pl.pallas_call(
+        after_kernel,
+        in_specs=[anywhere, anywhere],
+        out_specs=anywhere,
+        out_shape=jax.ShapeDtypeStruct(x.shape, x.dtype),
+        input_output_aliases={0: 0},
+        cost_estimate=SMALL,
+        name="after",
+    )(in_hbm(x), in_hbm(earlier))
 
 
 def slot_matches(routes_t):
@@ -92,11 +118,11 @@
     return pl.pallas_call(
         pack_kernel,
         out_shape=(
-            jax.ShapeDtypeStruct((512, 1152), BF),
-            jax.ShapeDtypeStruct((1024, 768), BF),
+            hbm_shape((512, 1152)),
+            hbm_shape((1024, 768)),
         ),
         compiler_params=params(),
-        cost_estimate=pl.CostEstimate(flops=10**9, bytes_accessed=5 * 10**6, transcendentals=0),
+        cost_estimate=SMALL,
         name="pack",
     )(routes_t, gates_t, tokens, out_grad)
 
@@ -120,75 +146,128 @@
                 grad_ref[target, 1152:] = rows[224:256, j * 384:(j + 1) * 384]
 
 
-def expert_kernel(last, group_ref, got_ref, w1_ref, w2_ref, token_ref, grad_ref, hidden_ref, dpre_ref, *rest):
-    *part_refs, total = rest
+def expert_kernel(last, flags_ref, earlier_ref, got_ref, w1_mine, w1_other, w2_mine, w2_other, mine_ref, send_ref, *rest):
+    *part_refs, token, grad, total_mine, total_other = rest
     step = pl.program_id(0)
+    low, high = slice(0, HALF), slice(HALF, D)
+    first = flags_ref[0] == 0
+
+    def both_orders(run):
+        pl.when(first)(lambda: run(low, high))
+        pl.when(jnp.logical_not(first))(lambda: run(high, low))
 
     @pl.when(step == 0)
     def _():
-        unpack(last, got_ref, token_ref, grad_ref)
-
-    pre = dot(token_ref[...], w1_ref[...])
-    back = dot_nt(grad_ref[...], w2_ref[...])
+        unpack(last, got_ref, token, grad)
+
+        def split(own, other):
+            mine_ref[:, low] = token[:, own]
+            mine_ref[:, high] = grad[:, own]
+            send_ref[:, low] = token[:, other]
+            send_ref[:, high] = grad[:, other]
+
+        both_orders(split)
+
+    pre = dot(mine_ref[:, low], w1_mine[...]) + dot(send_ref[:, low], w1_other[...])
+    back = dot_nt(mine_ref[:, high], w2_mine[...]) + dot_nt(send_ref[:, high], w2_other[...])
     square = pre * pre
     th = jnp.tanh(ROOT_TWO_PI * (pre + CUBIC * square * pre))
     half = 0.5 * (1.0 + th)
-    hidden_ref[...] = (pre * half).astype(BF)
+    hidden = (pre * half).astype(BF)
     slope = half + 0.5 * pre * (1.0 - th * th) * ROOT_TWO_PI * (1.0 + 3.0 * CUBIC * square)
     d_pre = (back * slope).astype(BF)
-    dpre_ref[...] = d_pre
-    term = dot_nt(d_pre, w1_ref[...])
+    for k in range(2):
+        @pl.when(step == k)
+        def _(k=k):
+            send_ref[:, (2 + k) * HALF:(3 + k) * HALF] = hidden
+            send_ref[:, (4 + k) * HALF:(5 + k) * HALF] = d_pre
+    term_mine, term_other = dot_nt(d_pre, w1_mine[...]), dot_nt(d_pre, w1_other[...])
 
     @pl.when(step == 0)
     def _():
-        total[...] = term
-
-    @pl.when(step > 0)
+        total_mine[...] = term_mine
+        total_other[...] = term_other
+
+    @pl.when(step == 1)
     def _():
-        total[...] += term
-
-    @pl.when(step == pl.num_programs(0) - 1)
-    def _():
-        if last:
-            for k, part_ref in enumerate(part_refs):
-                group = group_ref[0] if k == 0 else 1 - group_ref[0]
-                part_ref[...] = total[pl.ds(pl.multiple_of(group * 128, 128), 128), :].astype(BF)
-        else:
-            part_refs[0][...] = total[...].astype(BF)
-
-
-def expert_rows(last, group, got, w1, w2):
+        total_mine[...] += term_mine
+        total_other[...] += term_other
+
+        def finish(own, other):
+            for columns, total in ((own, total_mine), (other, total_other)):
+                if last:
+                    for k, part_ref in enumerate(part_refs):
+                        group = flags_ref[1] if k == 0 else 1 - flags_ref[1]
+                        rows = pl.ds(pl.multiple_of(group * 128, 128), 128)
+                        part_ref[:, columns] = total[rows, :].astype(BF)
+                else:
+                    part_refs[0][:, columns] = total[...].astype(BF)
+
+        both_orders(finish)
+
+
+def expert_rows(last, flags, earlier, got, weights):
     rows = 256 if last else 192
     parts = [(128, D)] * 2 if last else [(192, D)]
-    hidden_units = w1.shape[1]
-    row_shape = jax.ShapeDtypeStruct((rows, D), BF)
-    hid_shape = jax.ShapeDtypeStruct((rows, hidden_units), BF)
+    first = pl.BlockSpec((HALF, HALF), lambda h: (0, h))
+    second = pl.BlockSpec((HALF, HALF), lambda h: (h, 0))
+    outs = [(rows, D), (rows, 3 * D), *parts]
     return pl.pallas_call(
         functools.partial(expert_kernel, last),
-        grid=(hidden_units // BLOCK,),
+        grid=(2,),
         in_specs=[
             pl.BlockSpec(memory_space=pltpu.SMEM),
+            pl.BlockSpec(memory_space=pl.ANY),
             whole(got.shape),
-            pl.BlockSpec((D, BLOCK), lambda h: (0, h)),
-            pl.BlockSpec((BLOCK, D), lambda h: (h, 0)),
+            first, first, second, second,
         ],
+        out_specs=tuple(whole(shape) for shape in outs),
+        out_shape=tuple(hbm_shape(shape) for shape in outs),
+        scratch_shapes=[pltpu.VMEM((rows, D), BF)] * 2 + [pltpu.VMEM((rows, HALF), F32)] * 2,
+        compiler_params=params(32),
+        cost_estimate=SMALL,
+        name="expert_last" if last else "expert_main",
+    )(flags, in_hbm(earlier), got, *weights)
+
+
+def weight_grads_kernel(*refs):
+    in_ref, out_ref = refs[-2:]
+    first = second = None
+    for i in range(0, 24, 4):
+        token_ref, grad_ref, hidden_ref, dpre_ref = refs[i:i + 4]
+        a, b = dot_tn(token_ref[...], dpre_ref[...]), dot_tn(hidden_ref[...], grad_ref[...])
+        first, second = (a, b) if first is None else (first + a, second + b)
+    in_ref[...] = first.astype(BF)
+    out_ref[...] = second.astype(BF)
+
+
+def weight_grads(sets):
+    specs, operands = [], []
+
+    def take(x, block, moves):
+        operands.append(in_hbm(x))
+        index = (lambda h: (0, block + h)) if moves else (lambda h: (0, block))
+        specs.append(pl.BlockSpec((x.shape[0], HALF), index))
+
+    for mine, send, received in sets:
+        for near, far in ((mine, send), (received, received)):
+            take(near, 0, False)
+            take(near, 1, False)
+            take(far, 2, True)
+            take(far, 4, True)
+    return pl.pallas_call(
+        weight_grads_kernel,
+        grid=(2,),
+        in_specs=specs,
         out_specs=(
-            whole((rows, D)),
-            whole((rows, D)),
-            pl.BlockSpec((rows, BLOCK), lambda h: (0, h)),
-            pl.BlockSpec((rows, BLOCK), lambda h: (0, h)),
-            *(whole(part) for part in parts),
+            pl.BlockSpec((HALF, HALF), lambda h: (0, h)),
+            pl.BlockSpec((HALF, HALF), lambda h: (h, 0)),
         ),
-        out_shape=(
-            row_shape, row_shape, hid_shape, hid_shape, *(jax.ShapeDtypeStruct(part, BF) for part in parts)
-        ),
-        scratch_shapes=[pltpu.VMEM((rows, D), F32)],
-        compiler_params=params(32),
-        cost_estimate=pl.CostEstimate(
-            flops=6 * rows * D * hidden_units, bytes_accessed=14 * 10**6, transcendentals=rows * hidden_units
-        ),
-        name="expert_last" if last else "expert_main",
-    )(group, got, w1, w2)
+        out_shape=(hbm_shape((HALF, D)), hbm_shape((D, HALF))),
+        compiler_params=params(48),
+        cost_estimate=SMALL,
+        name="weight_grads",
+    )(*operands)
 
 
 def merge_kernel(main_a, main_b, last_a, last_b, out_ref):
@@ -210,14 +289,14 @@
 def merge(*parts):
     return pl.pallas_call(
         merge_kernel,
-        out_shape=jax.ShapeDtypeStruct((512, 1024), BF),
+        out_shape=hbm_shape((512, 1024)),
         compiler_params=params(),
-        cost_estimate=pl.CostEstimate(flops=3 * 10**8, bytes_accessed=3 * 10**6, transcendentals=0),
+        cost_estimate=SMALL,
         name="merge",
-    )(*parts)
-
-
-def combine_kernel(routes_ref, got_ref, out_ref):
+    )(in_hbm(parts[0]), parts[1], in_hbm(parts[2]), parts[3])
+
+
+def combine_kernel(routes_ref, got_ref, earlier_ref, out_ref):
     _, match, rank = slot_matches(routes_ref[...])
     inner = iota((EXPERTS * 8, TOK), 0) & 7
     chosen = match & (rank == (inner & 3).astype(F32))
@@ -230,14 +309,16 @@
         out_ref[:, j * 256:(j + 1) * 256] = total.astype(BF)
 
 
-def combine(routes_t, got):
+def combine(routes_t, got, earlier):
     return pl.pallas_call(
         combine_kernel,
+        in_specs=[whole(routes_t.shape), whole(got.shape), pl.BlockSpec(memory_space=pl.ANY)],
+        out_specs=whole((TOK, D)),
         out_shape=jax.ShapeDtypeStruct((TOK, D), BF),
         compiler_params=params(),
-        cost_estimate=pl.CostEstimate(flops=4 * 10**8, bytes_accessed=2 * 10**6, transcendentals=0),
+        cost_estimate=SMALL,
         name="combine",
-    )(routes_t, got)
+    )(routes_t, got, in_hbm(earlier))
 
 
 def per_device(tokens, out_grad, routes, gate_probs, weight_in, weight_out):
@@ -247,9 +328,8 @@
     inner = [4 * i + x for i in range(32) for x in (1, 2)]
     halves, everyone = [outer, inner], [outer + inner]
     place = lax.axis_index("expert") & 3
-    group = jnp.where((place == 1) | (place == 2), 1, 0).astype(jnp.int32).reshape(1)
-    core = lax.axis_index("dp")
-    fence = lax.optimization_barrier
+    group = jnp.where((place == 1) | (place == 2), 1, 0)
+    flags = jnp.stack([lax.axis_index("dp"), group]).astype(jnp.int32)
 
     def exchange(rows, groups):
         count = len(groups[0])
@@ -259,46 +339,28 @@
         )
         return got.reshape(rows.shape)
 
-    def gather(weight, axis):
-        other = lax.ppermute(weight, "dp", cores)
-        first, second = jnp.where(core == 0, weight, other), jnp.where(core == 0, other, weight)
-        return jnp.concatenate([first, second], axis=axis)
-
+    def to_other_core(x):
+        return lax.ppermute(x, "dp", cores)
+
+    weights = (weight_in, to_other_core(weight_in), weight_out, to_other_core(weight_out))
     routes_t, gates_t = routes.T, gate_probs.T
     send_main, send_last = pack(routes_t, gates_t, tokens, out_grad)
-    weight_in, weight_out, send_main = fence((weight_in, weight_out, send_main))
-    w1, w2 = gather(weight_in, 0), gather(weight_out, 1)
     own_got = exchange(send_main, halves)
     pair_got = lax.ppermute(own_got, "expert", chips)
-    send_last, _ = fence((send_last, own_got[:8, :128] + 1))
+    own_mine, own_send, own_part = expert_rows(False, flags, send_main, own_got, weights)
     last_got = exchange(send_last, everyone)
-    own = expert_rows(False, group, own_got, w1, w2)
-    pair_got, _ = fence((pair_got, own[4]))
-    pair = expert_rows(False, group, pair_got, w1, w2)
-    other_main = lax.ppermute(pair[4], "expert", chips)
-    last_got, pair_part = fence((last_got, pair[4]))
-    last = expert_rows(True, group, last_got, w1, w2)
-    other_last = lax.ppermute(last[5], "expert", chips)
-    merged = merge(own[4], other_main, last[4], other_last)
+    pair_mine, pair_send, pair_part = expert_rows(False, flags, own_part, pair_got, weights)
+    other_main = lax.ppermute(pair_part, "expert", chips)
+    last_mine, last_send, last_part, last_away = expert_rows(True, flags, pair_part, last_got, weights)
+    other_last = lax.ppermute(last_away, "expert", chips)
+    merged = merge(own_part, other_main, last_part, other_last)
     got = exchange(merged, halves)
-
-    token_all, grad_all, hidden_all, dpre_all = (
-        jnp.concatenate([own[i], pair[i], last[i]], axis=0) for i in range(4)
-    )
-
-    def half(rows, index):
-        return lax.dynamic_slice_in_dim(rows, index * (D // 2), D // 2, axis=1)
-
-    def gradients(index, after):
-        tokens, grads, hidden, d_pre, _ = fence((token_all, grad_all, hidden_all, dpre_all, after))
-        return dot_tn(half(tokens, index), d_pre), dot_tn(hidden, half(grads, index))
-
-    sent_in, sent_out = (lax.ppermute(v.astype(BF), "dp", cores) for v in gradients(1 - core, other_main))
-    kept_in, kept_out = gradients(core, merged)
-    grad_in = (kept_in + sent_in.astype(F32)).astype(BF)
-    grad_out = (kept_out + sent_out.astype(F32)).astype(BF)
-    got, grad_in, grad_out = fence((got, grad_in, grad_out))
-    return combine(routes_t, got), grad_in, grad_out
+    grad_in, grad_out = weight_grads([
+        (own_mine, own_send, to_other_core(own_send)),
+        (pair_mine, pair_send, to_other_core(pair_send)),
+        (after(last_mine, merged), last_send, to_other_core(last_send)),
+    ])
+    return combine(routes_t, got, grad_in), grad_in, grad_out
 
 
 def solution(mesh):

time: 192 us -> 183 us (0.953)
  blocking collectives: 0 us -> 46.3 us
  waiting for transfers between devices: 85.6 us -> 55.6 us
  Pallas kernels: 25.5 us -> 48.6 us
  matrix products: 17.7 us -> 0 us
  starting transfers between devices: 38.3 us -> 24.4 us
  local copies, waits for them, and re-layouts: 15.9 us -> 6.76 us
  other arithmetic: 7.74 us -> 0.07 us
    all_to_all x0 -> x1, blocking collectives: none -> 46.3 us  [exchange(): lax.all_to_all(chunked, 'expert', split_axis=0, concat_axis=0, tiled=True...]
    all_to_all x3 -> x2, waiting for transfers between devices: 50.4 us -> 8.89 us  [exchange(): lax.all_to_all(chunked, 'expert', split_axis=0, concat_axis=0, tiled=True...]
    pallas_call x6 -> x8, Pallas kernels: 25.5 us -> 48.6 us  [the longest x3 27.8 us: expert_rows(): pl.pallas_call(functools.partial(expert_kernel, last), grid=(2,), in_spec...]
    dot_general x4 -> x0, matrix products: 17.7 us -> none  [dot_tn(): lax.dot_general(a, b, (((0,), (0,)), ((), ())), preferred_element_type=F32)]
    all_to_all x3 -> x2, starting transfers between devices: 33.5 us -> 19.1 us  [exchange(): lax.all_to_all(chunked, 'expert', split_axis=0, concat_axis=0, tiled=True...]
    ppermute x6 -> x7, waiting for transfers between devices: 9.73 us -> 22.1 us  [the longest x5 11.8 us: to_other_core(): return lax.ppermute(x, 'dp', cores)]
    unnamed x54 -> x18, local copies, waits for them, and re-layouts: 15.6 us -> 6.76 us
    select_n x2 -> x0, other arithmetic: 7.07 us -> none  [gather(): jnp.where(core == 0, weight, other)]
  transfers between devices with their start and end apart: 10 -> 10, of which waited for: 4 -> 7; matrix products, arithmetic and copies ran while one was open for 13% -> 0% of each run, Pallas kernels for 10% -> 24%
where the time goes in v2:
time: 183 us; the launch traced here: 182 us
  waiting for transfers between devices  55.6 us (30%)
  Pallas kernels  48.6 us (27%)
  blocking collectives  46.3 us (25%)
  starting transfers between devices  24.4 us (13%)
  local copies, waits for them, and re-layouts  6.76 us (4%)
    all_to_all x1, blocking collectives, exchange(): lax.all_to_all(chunked, 'expert', split_axis=0, concat_axis=0, tiled=True...  46.3 us
    pallas_call x3, Pallas kernels, expert_rows(): pl.pallas_call(functools.partial(expert_kernel, last), grid=(2,), in_spec...  27.8 us
    ppermute x1, waiting for transfers between devices, per_device(): pair_got = lax.ppermute(own_got, 'expert', chips)  24.6 us
    all_to_all x2, starting transfers between devices, exchange(): lax.all_to_all(chunked, 'expert', split_axis=0, concat_axis=0, tiled=True...  19.1 us
    pallas_call x1, Pallas kernels, weight_grads(): pl.pallas_call(weight_grads_kernel, grid=(2,), in_specs=specs, out_specs=...  12.4 us
    ppermute x5, waiting for transfers between devices, to_other_core(): return lax.ppermute(x, 'dp', cores)  11.8 us
    ppermute x1, waiting for transfers between devices, per_device(): other_last = lax.ppermute(last_away, 'expert', chips)  10.3 us
    all_to_all x2, waiting for transfers between devices, exchange(): lax.all_to_all(chunked, 'expert', split_axis=0, concat_axis=0, tiled=True...  8.89 us
  transfers between devices with their start and end apart: 10, of which 7 were waited for; matrix products, arithmetic and copies ran while one was open for 0% of the time, Pallas kernels for 24%

profile of v2, /device:TPU:8, one launch (start us, length us, event | category | flops | bytes accessed | tf_op | source)
XLA Modules:
  0.0 182.4 jit_solution(2635251726633585529)
XLA Ops:
  0.6 0.0 copy-start.3
  0.6 1.0 copy-done.3
  1.6 0.0 copy-start.4
  1.6 1.0 copy-done.4
  2.6 0.0 copy-start.5
  2.6 0.7 copy-done.5
  3.3 0.0 copy-start.7
  3.3 0.7 copy-done.7
  4.0 3.8 %pack.1 = (bf16[512,1152]{1,0:T(8,128)(2,1)}, bf16[1024,768]{1,0:T(8,128)(2,1)}) custom-call(s32[2,128]{1,0:T(2,128)S(1)} %bitcast.13, f32[2,128]{1,0:T(2,128)S(1)} %bitcast.15, bf16[128,1536]{1,0:T(8,128)(2,1)S(1)} %copy-done.3, bf16[128,1536]{1,0:T(8,128)(2,1)S(1)} %copy-done.4), custom_call_target="tpu_custom_call" | custom-call | flops 1 | bytes 1 | tf_op jit(solution)/shard_map/pack/pallas_call | solution.py:118
  7.7 46.3 %all_to_all.15 = bf16[64,8,1152]{2,1,0:T(8,128)(2,1)S(1)} all-to-all(bf16[64,8,1152]{2,1,0:T(8,128)(2,1)} %bitcast.17), channel_id=1, replica_groups={{0,3,4,7,8,11,12,15,16,19,20,23,24,27,28,31,32,35,36,39,40,43,44,47,48,..., dimensions={0} | all-to-all | bytes 2359296 | tf_op jit(solution)/shard_map/all_to_all | solution.py:337
  54.1 0.0 copy-start
  54.1 8.2 %all-to-all-start.1 = ((bf16[128,8,768]{2,1,0:T(8,128)(2,1)}), bf16[128,8,768]{2,1,0:T(8,128)(2,1)}, u32[]{:S(2)}, u32[]{:S(2)}) async-start(bf16[128,8,768]{2,1,0:T(8,128)(2,1)} %bitcast.18), calls=%async_computation.1 | async-start | bytes 3145728 | tf_op jit(solution)/shard_map/all_to_all | solution.py:337
  62.3 0.0 copy-done
  62.3 0.1 collective-permute-start
  62.4 0.5 collective-permute-start.1
  62.9 1.9 %collective-permute-start.2 = (bf16[512,1152]{1,0:T(8,128)(2,1)S(1)}, bf16[512,1152]{1,0:T(8,128)(2,1)}, u32[]{:S(2)}, u32[]{:S(2)}) collective-permute-start(bf16[512,1152]{1,0:T(8,128)(2,1)S(1)} %bitcast.10), channel_id=1, source_target_pairs={{0,1},{1,0},{2,3},{3,2},{4,5},{5,4},{6,7},{7,6},{8,9},{9,8},{10,11... | collective-permute-start | bytes 3538952 | tf_op jit(solution)/shard_map/ppermute | solution.py:349
  64.8 0.1 pad_add_fusion.flags_ref
  64.9 4.6 %collective-permute-done.w1_other = bf16[768,1536]{1,0:T(8,128)(2,1)} collective-permute-done((bf16[768,1536]{1,0:T(8,128)(2,1)S(1)}, bf16[768,1536]{1,0:T(8,128)(2,1)}, u32[]{:S(2)}, u32[]{:S(2)}) %collective-permute-start) | collective-permute-done | bytes 2359328 | tf_op jit(solution)/shard_map/ppermute | solution.py:343
  69.4 1.2 collective-permute-done.1.w2_other
  70.6 0.0 copy-start.1
  70.6 1.7 copy-done.1
  72.3 8.9 %expert_main.2 = (bf16[192,1536]{1,0:T(8,128)(2,1)}, bf16[192,4608]{1,0:T(8,128)(2,1)}, bf16[192,1536]{1,0:T(8,128)(2,1)}) custom-call(s32[2]{0:T(128)S(1)} %pad_add_fusion.flags_ref, bf16[512,1152]{1,0:T(8,128)(2,1)} %get-tuple-element.17.earlier_ref, bf16[512,1152]{1,0:T(8,128)(2,1)S(1)} %bitcast.11, bf16[768,1536]{1,0:T(8,128)(2,1)S(1)} %copy-done, ...), custom_call_target="tpu_custom_call" | custom-call | flops 1 | bytes 1 | tf_op jit(solution)/shard_map/expert_main/pallas_call | solution.py:215
  81.2 24.6 %collective-permute-done.2.got_ref = bf16[512,1152]{1,0:T(8,128)(2,1)} collective-permute-done((bf16[512,1152]{1,0:T(8,128)(2,1)S(1)}, bf16[512,1152]{1,0:T(8,128)(2,1)}, u32[]{:S(2)}, u32[]{:S(2)}) %collective-permute-start.2) | collective-permute-done | bytes 1179680 | tf_op jit(solution)/shard_map/ppermute | solution.py:349
  105.8 9.2 %expert_main.3 = (bf16[192,1536]{1,0:T(8,128)(2,1)}, bf16[192,4608]{1,0:T(8,128)(2,1)}, bf16[192,1536]{1,0:T(8,128)(2,1)}) custom-call(s32[2]{0:T(128)S(1)} %pad_add_fusion.flags_ref, bf16[192,1536]{1,0:T(8,128)(2,1)} %get-tuple-element.18.earlier_ref.main_a, bf16[512,1152]{1,0:T(8,128)(2,1)} %collective-permute-done.2.got_ref, ...), custom_call_target="tpu_custom_call" | custom-call | flops 1 | bytes 1 | tf_op jit(solution)/shard_map/expert_main/pallas_call | solution.py:215
  115.0 0.5 collective-permute-start.3
  115.5 0.0 all-to-all-done.1
  115.5 0.0 copy-start.2
  115.5 1.7 copy-done.2
  117.2 9.8 %expert_last.1 = (bf16[256,1536]{1,0:T(8,128)(2,1)}, bf16[256,4608]{1,0:T(8,128)(2,1)}, bf16[128,1536]{1,0:T(8,128)(2,1)}, bf16[128,1536]{1,0:T(8,128)(2,1)}) custom-call(s32[2]{0:T(128)S(1)} %pad_add_fusion.flags_ref, bf16[192,1536]{1,0:T(8,128)(2,1)} %get-tuple-element.19.earlier_ref, bf16[1024,768]{1,0:T(8,128)(2,1)} %bitcast.7.got_ref, ...), custom_call_target="tpu_custom_call" | custom-call | flops 1 | bytes 1 | tf_op jit(solution)/shard_map/expert_last/pallas_call | solution.py:215
  126.9 1.5 collective-permute-start.4
  128.4 0.0 collective-permute-start.7
  128.4 10.3 %collective-permute-done.4.last_b = bf16[128,1536]{1,0:T(8,128)(2,1)S(1)} collective-permute-done((bf16[128,1536]{1,0:T(8,128)(2,1)}, bf16[128,1536]{1,0:T(8,128)(2,1)S(1)}, u32[]{:S(2)}, u32[]{:S(2)}) %collective-permute-start.4) | collective-permute-done | bytes 393248 | tf_op jit(solution)/shard_map/ppermute | solution.py:355
  138.7 0.0 collective-permute-done.3.main_b
  138.7 2.9 %merge.1.earlier_ref = bf16[512,1024]{1,0:T(8,128)(2,1)} custom-call(bf16[192,1536]{1,0:T(8,128)(2,1)} %get-tuple-element.18.earlier_ref.main_a, bf16[192,1536]{1,0:T(8,128)(2,1)S(1)} %collective-permute-done.3.main_b, bf16[128,1536]{1,0:T(8,128)(2,1)} %get-tuple-element.21.last_a, bf16[128,1536]{1,0:T(8,128)(2,1)S(1)} %collective-permute-done.4.last_b), custom_call_target="tpu_custom_call" | custom-call | flops 1 | bytes 1 | tf_op jit(solution)/shard_map/merge/pallas_call | solution.py:290
  141.6 10.9 %all-to-all-start.2 = ((bf16[64,8,1024]{2,1,0:T(8,128)(2,1)}), bf16[64,8,1024]{2,1,0:T(8,128)(2,1)S(1)}, u32[]{:S(2)}, u32[]{:S(2)}) async-start(bf16[64,8,1024]{2,1,0:T(8,128)(2,1)} %bitcast.16), calls=%async_computation.2 | async-start | bytes 2097152 | tf_op jit(solution)/shard_map/all_to_all | solution.py:337
  152.5 0.3 collective-permute-start.5
  152.8 0.5 collective-permute-start.6
  153.3 4.9 %collective-permute-done.5.refs_4_.refs_5_.refs_6_.refs_7_ = bf16[192,4608]{1,0:T(8,128)(2,1)S(1)} collective-permute-done((bf16[192,4608]{1,0:T(8,128)(2,1)}, bf16[192,4608]{1,0:T(8,128)(2,1)S(1)}, u32[]{:S(2)}, u32[]{:S(2)}) %collective-permute-start.5) | collective-permute-done | bytes 1769504 | tf_op jit(solution)/shard_map/ppermute | solution.py:343
  158.3 0.0 copy-start.8
  158.3 1.1 collective-permute-done.6.refs_12_.refs_13_.refs_14_.refs_15_
  159.4 0.0 collective-permute-done.7.refs_20_.refs_21_.refs_22_.refs_23_
  159.4 0.1 copy-done.8
  159.5 0.0 copy-start.6
  159.5 12.4 %weight_grads.1 = (bf16[768,1536]{1,0:T(8,128)(2,1)}, bf16[1536,768]{1,0:T(8,128)(2,1)}) custom-call(bf16[192,1536]{1,0:T(8,128)(2,1)} %get-tuple-element.23.refs_0_.refs_1_, bf16[192,1536]{1,0:T(8,128)(2,1)} %get-tuple-element.23.refs_0_.refs_1_, bf16[192,4608]{1,0:T(8,128)(2,1)} %get-tuple-element.24.refs_2_.refs_3_, ...), custom_call_target="tpu_custom_call" | custom-call | flops 1 | bytes 1 | tf_op jit(solution)/shard_map/weight_grads/pallas_call | solution.py:258
  171.9 8.9 %all-to-all-done.2 = bf16[64,8,1024]{2,1,0:T(8,128)(2,1)S(1)} async-done(((bf16[64,8,1024]{2,1,0:T(8,128)(2,1)}), bf16[64,8,1024]{2,1,0:T(8,128)(2,1)S(1)}, u32[]{:S(2)}, u32[]{:S(2)}) %all-to-all-start.2) | async-done | bytes 1048608 | tf_op jit(solution)/shard_map/all_to_all | solution.py:337
  180.8 0.0 copy-done.6
  180.8 1.7 combine.1
  (1 shorter events, 0.0 us)
Async XLA Ops:
  0.6 1.0 copy-start.3
  1.6 1.0 copy-start.4
  2.6 0.7 copy-start.5
  3.3 0.7 copy-start.7
  54.1 8.2 %copy-start = (bf16[768,1536]{1,0:T(8,128)(2,1)S(1)}, bf16[768,1536]{1,0:T(8,128)(2,1)}, u32[]{:S(2)}) copy-start(bf16[768,1536]{1,0:T(8,128)(2,1)} %w1_mine.5) | copy-start | bytes 7077892
  54.1 61.4 %all-to-all-start.1 = ((bf16[128,8,768]{2,1,0:T(8,128)(2,1)}), bf16[128,8,768]{2,1,0:T(8,128)(2,1)}, u32[]{:S(2)}, u32[]{:S(2)}) async-start(bf16[128,8,768]{2,1,0:T(8,128)(2,1)} %bitcast.18), calls=%async_computation.1 | async-start | bytes 3145728 | tf_op jit(solution)/shard_map/all_to_all | solution.py:337
  62.3 7.1 %collective-permute-start = (bf16[768,1536]{1,0:T(8,128)(2,1)S(1)}, bf16[768,1536]{1,0:T(8,128)(2,1)}, u32[]{:S(2)}, u32[]{:S(2)}) collective-permute-start(bf16[768,1536]{1,0:T(8,128)(2,1)S(1)} %copy-done), channel_id=1, source_target_pairs={{0,128},{128,0},{1,129},{129,1},{2,130},{130,2},{3,131},{131,3},{4... | collective-permute-start | bytes 7077896 | tf_op jit(solution)/shard_map/ppermute | solution.py:343
  62.4 8.2 %collective-permute-start.1 = (bf16[1536,768]{1,0:T(8,128)(2,1)}, bf16[1536,768]{1,0:T(8,128)(2,1)}, u32[]{:S(2)}, u32[]{:S(2)}) collective-permute-start(bf16[1536,768]{1,0:T(8,128)(2,1)} %w2_mine.5), channel_id=1, source_target_pairs={{0,128},{128,0},{1,129},{129,1},{2,130},{130,2},{3,131},{131,3},{4... | collective-permute-start | bytes 7077896 | tf_op jit(solution)/shard_map/ppermute | solution.py:343
  62.9 42.9 %collective-permute-start.2 = (bf16[512,1152]{1,0:T(8,128)(2,1)S(1)}, bf16[512,1152]{1,0:T(8,128)(2,1)}, u32[]{:S(2)}, u32[]{:S(2)}) collective-permute-start(bf16[512,1152]{1,0:T(8,128)(2,1)S(1)} %bitcast.10), channel_id=1, source_target_pairs={{0,1},{1,0},{2,3},{3,2},{4,5},{5,4},{6,7},{7,6},{8,9},{9,8},{10,11... | collective-permute-start | bytes 3538952 | tf_op jit(solution)/shard_map/ppermute | solution.py:349
  70.6 1.7 copy-start.1
  115.0 23.7 %collective-permute-start.3 = (bf16[192,1536]{1,0:T(8,128)(2,1)}, bf16[192,1536]{1,0:T(8,128)(2,1)S(1)}, u32[]{:S(2)}, u32[]{:S(2)}) collective-permute-start(bf16[192,1536]{1,0:T(8,128)(2,1)} %get-tuple-element.19.earlier_ref), channel_id=1, source_target_pairs={{0,1},{1,0},{2,3},{3,2},{4,5},{5,4},{6,7},{7,6},{8,9},{9,8},{10,11... | collective-permute-start | bytes 1769480 | tf_op jit(solution)/shard_map/ppermute | solution.py:353
  115.5 1.7 copy-start.2
  126.9 11.8 %collective-permute-start.4 = (bf16[128,1536]{1,0:T(8,128)(2,1)}, bf16[128,1536]{1,0:T(8,128)(2,1)S(1)}, u32[]{:S(2)}, u32[]{:S(2)}) collective-permute-start(bf16[128,1536]{1,0:T(8,128)(2,1)} %get-tuple-element.22), channel_id=1, source_target_pairs={{0,1},{1,0},{2,3},{3,2},{4,5},{5,4},{6,7},{7,6},{8,9},{9,8},{10,11... | collective-permute-start | bytes 1179656 | tf_op jit(solution)/shard_map/ppermute | solution.py:355
  128.4 31.0 %collective-permute-start.7 = (bf16[256,4608]{1,0:T(8,128)(2,1)}, bf16[256,4608]{1,0:T(8,128)(2,1)}, u32[]{:S(2)}, u32[]{:S(2)}) collective-permute-start(bf16[256,4608]{1,0:T(8,128)(2,1)} %get-tuple-element.28.refs_18_.refs_19_), channel_id=1, source_target_pairs={{0,128},{128,0},{1,129},{129,1},{2,130},{130,2},{3,131},{131,3},{4... | collective-permute-start | bytes 7077896 | tf_op jit(solution)/shard_map/ppermute | solution.py:343
  141.6 39.2 %all-to-all-start.2 = ((bf16[64,8,1024]{2,1,0:T(8,128)(2,1)}), bf16[64,8,1024]{2,1,0:T(8,128)(2,1)S(1)}, u32[]{:S(2)}, u32[]{:S(2)}) async-start(bf16[64,8,1024]{2,1,0:T(8,128)(2,1)} %bitcast.16), calls=%async_computation.2 | async-start | bytes 2097152 | tf_op jit(solution)/shard_map/all_to_all | solution.py:337
  152.5 5.7 %collective-permute-start.5 = (bf16[192,4608]{1,0:T(8,128)(2,1)}, bf16[192,4608]{1,0:T(8,128)(2,1)S(1)}, u32[]{:S(2)}, u32[]{:S(2)}) collective-permute-start(bf16[192,4608]{1,0:T(8,128)(2,1)} %get-tuple-element.24.refs_2_.refs_3_), channel_id=1, source_target_pairs={{0,128},{128,0},{1,129},{129,1},{2,130},{130,2},{3,131},{131,3},{4... | collective-permute-start | bytes 5308424 | tf_op jit(solution)/shard_map/ppermute | solution.py:343
  152.8 6.6 %collective-permute-start.6 = (bf16[192,4608]{1,0:T(8,128)(2,1)}, bf16[192,4608]{1,0:T(8,128)(2,1)}, u32[]{:S(2)}, u32[]{:S(2)}) collective-permute-start(bf16[192,4608]{1,0:T(8,128)(2,1)} %get-tuple-element.26.refs_10_.refs_11_), channel_id=1, source_target_pairs={{0,128},{128,0},{1,129},{129,1},{2,130},{130,2},{3,131},{131,3},{4... | collective-permute-start | bytes 5308424 | tf_op jit(solution)/shard_map/ppermute | solution.py:343
  158.3 1.2 copy-start.8
  159.5 21.3 %copy-start.6 = (s32[128,2]{0,1:T(2,128)S(1)}, s32[128,2]{0,1:T(2,128)}, u32[]{:S(2)}) copy-start(s32[128,2]{0,1:T(2,128)} %param.8) | copy-start | bytes 3076

commit v3 on v2

--- a/solution.py
+++ b/solution.py
@@ -15,6 +15,7 @@
 TOK = 128
 EXPERTS = 64
 HALF = 768
+LARGE = pl.CostEstimate(flops=10**11, bytes_accessed=10**8, transcendentals=0)
 SMALL = pl.CostEstimate(flops=1, bytes_accessed=1, transcendentals=0)
 
 
@@ -124,7 +125,7 @@
         compiler_params=params(),
         cost_estimate=SMALL,
         name="pack",
-    )(routes_t, gates_t, tokens, out_grad)
+    )(*map(in_hbm, (routes_t, gates_t, tokens, out_grad)))
 
 
 def unpack(last, got_ref, token_ref, grad_ref):
@@ -146,88 +147,109 @@
                 grad_ref[target, 1152:] = rows[224:256, j * 384:(j + 1) * 384]
 
 
-def expert_kernel(last, flags_ref, earlier_ref, got_ref, w1_mine, w1_other, w2_mine, w2_other, mine_ref, send_ref, *rest):
-    *part_refs, token, grad, total_mine, total_other = rest
-    step = pl.program_id(0)
-    low, high = slice(0, HALF), slice(HALF, D)
+def expert_kernel(last, flags_ref, earlier_ref, got_ref, in_mine, in_other, out_mine, out_other, *rest):
+    count = 4 if last else 3
+    mine_out, send_out, *part_outs = rest[:count]
+    w1_mine, w1_other, w2_mine, w2_other, token, grad, mine, send, units_out, *parts, loads, stores = rest[count:]
+    low, high = pl.ds(0, HALF), pl.ds(HALF, HALF)
     first = flags_ref[0] == 0
+    weights = ((in_mine, w1_mine), (in_other, w1_other), (out_mine, w2_mine), (out_other, w2_other))
+    arrivals = []
+    for source, target in weights:
+        half = source.shape[0] // 2
+        for k in range(2):
+            rows = pl.ds(k * half, half)
+            arrivals.append(pltpu.make_async_copy(source.at[rows, :], target.at[rows, :], loads.at[len(arrivals)]))
+    for k in (0, 1, 2, 3, 4, 6, 5, 7):
+        arrivals[k].start()
+
+    unpack(last, got_ref, token, grad)
 
     def both_orders(run):
         pl.when(first)(lambda: run(low, high))
         pl.when(jnp.logical_not(first))(lambda: run(high, low))
 
-    @pl.when(step == 0)
-    def _():
-        unpack(last, got_ref, token, grad)
-
-        def split(own, other):
-            mine_ref[:, low] = token[:, own]
-            mine_ref[:, high] = grad[:, own]
-            send_ref[:, low] = token[:, other]
-            send_ref[:, high] = grad[:, other]
-
-        both_orders(split)
-
-    pre = dot(mine_ref[:, low], w1_mine[...]) + dot(send_ref[:, low], w1_other[...])
-    back = dot_nt(mine_ref[:, high], w2_mine[...]) + dot_nt(send_ref[:, high], w2_other[...])
-    square = pre * pre
-    th = jnp.tanh(ROOT_TWO_PI * (pre + CUBIC * square * pre))
-    half = 0.5 * (1.0 + th)
-    hidden = (pre * half).astype(BF)
-    slope = half + 0.5 * pre * (1.0 - th * th) * ROOT_TWO_PI * (1.0 + 3.0 * CUBIC * square)
-    d_pre = (back * slope).astype(BF)
+    def split(own, other):
+        mine[:, low] = token[:, own]
+        mine[:, high] = grad[:, own]
+        send[:, low] = token[:, other]
+        send[:, high] = grad[:, other]
+
+    both_orders(split)
+    departures = []
+
+    def depart(source, target):
+        departures.append(pltpu.make_async_copy(source, target, stores.at[len(departures)]))
+        departures[-1].start()
+
+    depart(mine, mine_out)
+    depart(send, send_out.at[:, pl.ds(0, D)])
+    pre = None
+    for k, (rows, w1) in enumerate(((mine, w1_mine), (mine, w1_mine), (send, w1_other), (send, w1_other))):
+        arrivals[k].wait()
+        part = pl.ds((k % 2) * (HALF // 2), HALF // 2)
+        term = dot(rows[:, part], w1[part, :])
+        pre = term if pre is None else pre + term
     for k in range(2):
-        @pl.when(step == k)
-        def _(k=k):
-            send_ref[:, (2 + k) * HALF:(3 + k) * HALF] = hidden
-            send_ref[:, (4 + k) * HALF:(5 + k) * HALF] = d_pre
-    term_mine, term_other = dot_nt(d_pre, w1_mine[...]), dot_nt(d_pre, w1_other[...])
-
-    @pl.when(step == 0)
-    def _():
-        total_mine[...] = term_mine
-        total_other[...] = term_other
-
-    @pl.when(step == 1)
-    def _():
-        total_mine[...] += term_mine
-        total_other[...] += term_other
-
-        def finish(own, other):
-            for columns, total in ((own, total_mine), (other, total_other)):
-                if last:
-                    for k, part_ref in enumerate(part_refs):
-                        group = flags_ref[1] if k == 0 else 1 - flags_ref[1]
-                        rows = pl.ds(pl.multiple_of(group * 128, 128), 128)
-                        part_ref[:, columns] = total[rows, :].astype(BF)
-                else:
-                    part_refs[0][:, columns] = total[...].astype(BF)
-
-        both_orders(finish)
-
-
-def expert_rows(last, flags, earlier, got, weights):
+        units = slice(k * HALF, (k + 1) * HALF)
+        arrivals[4 + k].wait()
+        arrivals[6 + k].wait()
+        back = dot_nt(mine[:, high], w2_mine[units, :]) + dot_nt(send[:, high], w2_other[units, :])
+        value = pre[:, units]
+        square = value * value
+        th = jnp.tanh(ROOT_TWO_PI * (value + CUBIC * square * value))
+        half = 0.5 * (1.0 + th)
+        slope = half + 0.5 * value * (1.0 - th * th) * ROOT_TWO_PI * (1.0 + 3.0 * CUBIC * square)
+        units_out[:, k * HALF:(k + 1) * HALF] = (value * half).astype(BF)
+        units_out[:, (2 + k) * HALF:(3 + k) * HALF] = (back * slope).astype(BF)
+    depart(units_out, send_out.at[:, pl.ds(D, 2 * D)])
+    d_pre = units_out[:, D:]
+    part_mine, part_other = dot_nt(d_pre, w1_mine[...]).astype(BF), dot_nt(d_pre, w1_other[...]).astype(BF)
+
+    def finish(own, other):
+        for columns, part in ((own, part_mine), (other, part_other)):
+            if last:
+                kept, away = parts
+
+                @pl.when(flags_ref[1] == 0)
+                def _():
+                    kept[:, columns], away[:, columns] = part[:128], part[128:]
+
+                @pl.when(flags_ref[1] != 0)
+                def _():
+                    kept[:, columns], away[:, columns] = part[128:], part[:128]
+            else:
+                parts[0][:, columns] = part
+
+    both_orders(finish)
+    for part, out in zip(parts, part_outs):
+        depart(part, out)
+    for copy in departures:
+        copy.wait()
+
+
+def expert_rows(last, flags, earlier, got, weights, cost=SMALL):
     rows = 256 if last else 192
     parts = [(128, D)] * 2 if last else [(192, D)]
-    first = pl.BlockSpec((HALF, HALF), lambda h: (0, h))
-    second = pl.BlockSpec((HALF, HALF), lambda h: (h, 0))
     outs = [(rows, D), (rows, 3 * D), *parts]
+    anywhere = pl.BlockSpec(memory_space=pl.ANY)
+    buffers = [(HALF, D)] * 2 + [(D, HALF)] * 2 + [(rows, D)] * 4 + [(rows, 2 * D)] + parts
     return pl.pallas_call(
         functools.partial(expert_kernel, last),
-        grid=(2,),
         in_specs=[
-            pl.BlockSpec(memory_space=pltpu.SMEM),
-            pl.BlockSpec(memory_space=pl.ANY),
-            whole(got.shape),
-            first, first, second, second,
+            pl.BlockSpec(memory_space=pltpu.SMEM), anywhere, whole(got.shape), *[anywhere] * 4
         ],
-        out_specs=tuple(whole(shape) for shape in outs),
+        out_specs=(anywhere,) * len(outs),
         out_shape=tuple(hbm_shape(shape) for shape in outs),
-        scratch_shapes=[pltpu.VMEM((rows, D), BF)] * 2 + [pltpu.VMEM((rows, HALF), F32)] * 2,
-        compiler_params=params(32),
-        cost_estimate=SMALL,
+        scratch_shapes=[
+            *(pltpu.VMEM(shape, BF) for shape in buffers),
+            pltpu.SemaphoreType.DMA((8,)),
+            pltpu.SemaphoreType.DMA((5,)),
+        ],
+        compiler_params=params(40),
+        cost_estimate=cost,
         name="expert_last" if last else "expert_main",
-    )(flags, in_hbm(earlier), got, *weights)
+    )(flags, in_hbm(earlier), got, *(in_hbm(weight) for weight in weights))
 
 
 def weight_grads_kernel(*refs):
@@ -349,7 +371,7 @@
     pair_got = lax.ppermute(own_got, "expert", chips)
     own_mine, own_send, own_part = expert_rows(False, flags, send_main, own_got, weights)
     last_got = exchange(send_last, everyone)
-    pair_mine, pair_send, pair_part = expert_rows(False, flags, own_part, pair_got, weights)
+    pair_mine, pair_send, pair_part = expert_rows(False, flags, own_part, pair_got, weights, LARGE)
     other_main = lax.ppermute(pair_part, "expert", chips)
     last_mine, last_send, last_part, last_away = expert_rows(True, flags, pair_part, last_got, weights)
     other_last = lax.ppermute(last_away, "expert", chips)

time: 183 us -> 160 us (0.87)
  blocking collectives: 46.3 us -> 0 us
  waiting for transfers between devices: 55.6 us -> 73.5 us
  starting transfers between devices: 24.4 us -> 35.9 us
  local copies, waits for them, and re-layouts: 6.76 us -> 0.01 us
    all_to_all x1 -> x0, blocking collectives: 46.3 us -> none  [exchange(): lax.all_to_all(chunked, 'expert', split_axis=0, concat_axis=0, tiled=True...]
    all_to_all x2 -> x3, waiting for transfers between devices: 8.89 us -> 39.7 us  [exchange(): lax.all_to_all(chunked, 'expert', split_axis=0, concat_axis=0, tiled=True...]
    all_to_all x2 -> x3, starting transfers between devices: 19.1 us -> 32.5 us  [exchange(): lax.all_to_all(chunked, 'expert', split_axis=0, concat_axis=0, tiled=True...]
    unnamed x18 -> x4, local copies, waits for them, and re-layouts: 6.76 us -> 0.01 us
    ppermute x5, waiting for transfers between devices: 11.8 us -> 6.06 us  [to_other_core(): return lax.ppermute(x, 'dp', cores)]
    ppermute x1, waiting for transfers between devices: 24.6 us -> 20.7 us  [per_device(): pair_got = lax.ppermute(own_got, 'expert', chips)]
    ppermute x1, waiting for transfers between devices: 10.3 us -> 7.04 us  [per_device(): other_last = lax.ppermute(last_away, 'expert', chips)]
    ppermute x1, starting transfers between devices: 1.88 us -> 0.01 us  [per_device(): pair_got = lax.ppermute(own_got, 'expert', chips)]
  transfers between devices with their start and end apart: 10 -> 11, of which waited for: 7 -> 6; matrix products, arithmetic and copies ran while one was open for 0% -> 0% of each run, Pallas kernels for 24% -> 27%
where the time goes in v3:
time: 160 us; the launch traced here: 159 us
  waiting for transfers between devices  73.5 us (46%)
  Pallas kernels  49.2 us (31%)
  starting transfers between devices  35.9 us (22%)
    all_to_all x3, waiting for transfers between devices, exchange(): lax.all_to_all(chunked, 'expert', split_axis=0, concat_axis=0, tiled=True...  39.7 us
    all_to_all x3, starting transfers between devices, exchange(): lax.all_to_all(chunked, 'expert', split_axis=0, concat_axis=0, tiled=True...  32.5 us
    pallas_call x3, Pallas kernels, expert_rows(): pl.pallas_call(functools.partial(expert_kernel, last), in_specs=[pl.Block...  27.4 us
    ppermute x1, waiting for transfers between devices, per_device(): pair_got = lax.ppermute(own_got, 'expert', chips)  20.7 us
    pallas_call x1, Pallas kernels, weight_grads(): pl.pallas_call(weight_grads_kernel, grid=(2,), in_specs=specs, out_specs=...  12.4 us
    ppermute x1, waiting for transfers between devices, per_device(): other_last = lax.ppermute(last_away, 'expert', chips)  7.04 us
    ppermute x5, waiting for transfers between devices, to_other_core(): return lax.ppermute(x, 'dp', cores)  6.06 us
    pallas_call x1, Pallas kernels, pack(): pl.pallas_call(pack_kernel, out_shape=(hbm_shape((512, 1152)), hbm_shape(...  4.85 us
  transfers between devices with their start and end apart: 11, of which 6 were waited for; matrix products, arithmetic and copies ran while one was open for 0% of the time, Pallas kernels for 27%

profile of v3, /device:TPU:8, one launch (start us, length us, event | category | flops | bytes accessed | tf_op | source)
XLA Modules:
  0.0 159.4 jit_solution(12386629173919275224)
XLA Ops:
  0.6 4.8 %pack.1 = (bf16[512,1152]{1,0:T(8,128)(2,1)}, bf16[1024,768]{1,0:T(8,128)(2,1)}) custom-call(s32[2,128]{1,0:T(2,128)} %bitcast.14, f32[2,128]{1,0:T(2,128)} %bitcast.19, bf16[128,1536]{1,0:T(8,128)(2,1)} %tokens_ref.1, bf16[128,1536]{1,0:T(8,128)(2,1)} %grads_ref.1), custom_call_target="tpu_custom_call" | custom-call | flops 1 | bytes 1 | tf_op jit(solution)/shard_map/pack/pallas_call | solution.py:119
  5.5 14.3 %all-to-all-start = ((bf16[64,8,1152]{2,1,0:T(8,128)(2,1)}), bf16[64,8,1152]{2,1,0:T(8,128)(2,1)S(1)}, u32[]{:S(2)}, u32[]{:S(2)}) async-start(bf16[64,8,1152]{2,1,0:T(8,128)(2,1)} %bitcast.17), calls=%async_computation | async-start | bytes 2359296 | tf_op jit(solution)/shard_map/all_to_all | solution.py:359
  19.8 0.1 collective-permute-start
  19.9 0.5 collective-permute-start.1
  20.4 31.4 %all-to-all-done = bf16[64,8,1152]{2,1,0:T(8,128)(2,1)S(1)} async-done(((bf16[64,8,1152]{2,1,0:T(8,128)(2,1)}), bf16[64,8,1152]{2,1,0:T(8,128)(2,1)S(1)}, u32[]{:S(2)}, u32[]{:S(2)}) %all-to-all-start) | async-done | bytes 1179680 | tf_op jit(solution)/shard_map/all_to_all | solution.py:359
  51.8 0.0 collective-permute-start.2
  51.8 9.1 %all-to-all-start.1 = ((bf16[128,8,768]{2,1,0:T(8,128)(2,1)}), bf16[128,8,768]{2,1,0:T(8,128)(2,1)S(1)}, u32[]{:S(2)}, u32[]{:S(2)}) async-start(bf16[128,8,768]{2,1,0:T(8,128)(2,1)} %bitcast.18), calls=%async_computation.1 | async-start | bytes 3145728 | tf_op jit(solution)/shard_map/all_to_all | solution.py:359
  61.0 0.1 pad_add_fusion.flags_ref
  61.0 0.0 collective-permute-done.in_other
  61.0 0.0 collective-permute-done.1.out_other
  61.1 8.8 %expert_main.2 = (bf16[192,1536]{1,0:T(8,128)(2,1)}, bf16[192,4608]{1,0:T(8,128)(2,1)}, bf16[192,1536]{1,0:T(8,128)(2,1)}) custom-call(s32[2]{0:T(128)S(1)} %pad_add_fusion.flags_ref, bf16[512,1152]{1,0:T(8,128)(2,1)} %get-tuple-element.17.earlier_ref, bf16[512,1152]{1,0:T(8,128)(2,1)S(1)} %bitcast.12, bf16[768,1536]{1,0:T(8,128)(2,1)} %in_mine.5, ...), custom_call_target="tpu_custom_call" | custom-call | flops 1 | bytes 1 | tf_op jit(solution)/shard_map/expert_main/pallas_call | solution.py:237
  69.9 20.7 %collective-permute-done.2.got_ref = bf16[512,1152]{1,0:T(8,128)(2,1)} collective-permute-done((bf16[512,1152]{1,0:T(8,128)(2,1)S(1)}, bf16[512,1152]{1,0:T(8,128)(2,1)}, u32[]{:S(2)}, u32[]{:S(2)}) %collective-permute-start.2) | collective-permute-done | bytes 1179680 | tf_op jit(solution)/shard_map/ppermute | solution.py:371
  90.6 9.2 %expert_main.3 = (bf16[192,1536]{1,0:T(8,128)(2,1)}, bf16[192,4608]{1,0:T(8,128)(2,1)}, bf16[192,1536]{1,0:T(8,128)(2,1)}) custom-call(s32[2]{0:T(128)S(1)} %pad_add_fusion.flags_ref, bf16[192,1536]{1,0:T(8,128)(2,1)} %get-tuple-element.18.earlier_ref.main_a, bf16[512,1152]{1,0:T(8,128)(2,1)} %collective-permute-done.2.got_ref, bf16[768,1536]{1,0:T(8,128)(2,1)} %in_mine.5, ...), custom_call_target="tpu_custom_call" | custom-call | flops 99999997952 | bytes 100000000 | tf_op jit(solution)/shard_map/expert_main/pallas_call | solution.py:237
  99.8 0.5 collective-permute-start.3
  100.3 0.0 all-to-all-done.1
  100.3 9.4 %expert_last.1 = (bf16[256,1536]{1,0:T(8,128)(2,1)}, bf16[256,4608]{1,0:T(8,128)(2,1)}, bf16[128,1536]{1,0:T(8,128)(2,1)}, bf16[128,1536]{1,0:T(8,128)(2,1)}) custom-call(s32[2]{0:T(128)S(1)} %pad_add_fusion.flags_ref, bf16[192,1536]{1,0:T(8,128)(2,1)} %get-tuple-element.19.earlier_ref, bf16[1024,768]{1,0:T(8,128)(2,1)S(1)} %bitcast.10, ...), custom_call_target="tpu_custom_call" | custom-call | flops 1 | bytes 1 | tf_op jit(solution)/shard_map/expert_last/pallas_call | solution.py:237
  109.7 1.7 %collective-permute-start.4 = (bf16[128,1536]{1,0:T(8,128)(2,1)}, bf16[128,1536]{1,0:T(8,128)(2,1)S(1)}, u32[]{:S(2)}, u32[]{:S(2)}) collective-permute-start(bf16[128,1536]{1,0:T(8,128)(2,1)} %get-tuple-element.22), channel_id=1, source_target_pairs={{0,1},{1,0},{2,3},{3,2},{4,5},{5,4},{6,7},{7,6},{8,9},{9,8},{10,11... | collective-permute-start | bytes 1179656 | tf_op jit(solution)/shard_map/ppermute | solution.py:377
  111.4 0.0 collective-permute-start.7
  111.4 7.0 %collective-permute-done.4.last_b = bf16[128,1536]{1,0:T(8,128)(2,1)S(1)} collective-permute-done((bf16[128,1536]{1,0:T(8,128)(2,1)}, bf16[128,1536]{1,0:T(8,128)(2,1)S(1)}, u32[]{:S(2)}, u32[]{:S(2)}) %collective-permute-start.4) | collective-permute-done | bytes 393248 | tf_op jit(solution)/shard_map/ppermute | solution.py:377
  118.4 0.0 collective-permute-done.3.main_b
  118.4 2.8 %merge.1.earlier_ref = bf16[512,1024]{1,0:T(8,128)(2,1)} custom-call(bf16[192,1536]{1,0:T(8,128)(2,1)} %get-tuple-element.18.earlier_ref.main_a, bf16[192,1536]{1,0:T(8,128)(2,1)S(1)} %collective-permute-done.3.main_b, bf16[128,1536]{1,0:T(8,128)(2,1)} %get-tuple-element.21.last_a, bf16[128,1536]{1,0:T(8,128)(2,1)S(1)} %collective-permute-done.4.last_b), custom_call_target="tpu_custom_call" | custom-call | flops 1 | bytes 1 | tf_op jit(solution)/shard_map/merge/pallas_call | solution.py:312
  121.3 9.1 %all-to-all-start.2 = ((bf16[64,8,1024]{2,1,0:T(8,128)(2,1)}), bf16[64,8,1024]{2,1,0:T(8,128)(2,1)S(1)}, u32[]{:S(2)}, u32[]{:S(2)}) async-start(bf16[64,8,1024]{2,1,0:T(8,128)(2,1)} %bitcast.16), calls=%async_computation.2 | async-start | bytes 2097152 | tf_op jit(solution)/shard_map/all_to_all | solution.py:359
  130.4 0.1 collective-permute-start.5
  130.5 0.5 collective-permute-start.6
  131.0 3.4 %collective-permute-done.5.refs_4_.refs_5_.refs_6_.refs_7_ = bf16[192,4608]{1,0:T(8,128)(2,1)S(1)} collective-permute-done((bf16[192,4608]{1,0:T(8,128)(2,1)}, bf16[192,4608]{1,0:T(8,128)(2,1)S(1)}, u32[]{:S(2)}, u32[]{:S(2)}) %collective-permute-start.5) | collective-permute-done | bytes 1769504 | tf_op jit(solution)/shard_map/ppermute | solution.py:365
  134.4 0.0 copy-start.1
  134.4 2.7 %collective-permute-done.6.refs_12_.refs_13_.refs_14_.refs_15_ = bf16[192,4608]{1,0:T(8,128)(2,1)} collective-permute-done((bf16[192,4608]{1,0:T(8,128)(2,1)}, bf16[192,4608]{1,0:T(8,128)(2,1)}, u32[]{:S(2)}, u32[]{:S(2)}) %collective-permute-start.6) | collective-permute-done | bytes 1769504 | tf_op jit(solution)/shard_map/ppermute | solution.py:365
  137.0 0.0 collective-permute-done.7.refs_20_.refs_21_.refs_22_.refs_23_
  137.0 0.0 copy-done.1
  137.0 0.0 copy-start
  137.0 12.4 %weight_grads.1 = (bf16[768,1536]{1,0:T(8,128)(2,1)}, bf16[1536,768]{1,0:T(8,128)(2,1)}) custom-call(bf16[192,1536]{1,0:T(8,128)(2,1)} %get-tuple-element.23.refs_0_.refs_1_, bf16[192,1536]{1,0:T(8,128)(2,1)} %get-tuple-element.23.refs_0_.refs_1_, bf16[192,4608]{1,0:T(8,128)(2,1)} %get-tuple-element.24.refs_2_.refs_3_, ...), custom_call_target="tpu_custom_call" | custom-call | flops 1 | bytes 1 | tf_op jit(solution)/shard_map/weight_grads/pallas_call | solution.py:280
  149.5 8.3 %all-to-all-done.2 = bf16[64,8,1024]{2,1,0:T(8,128)(2,1)S(1)} async-done(((bf16[64,8,1024]{2,1,0:T(8,128)(2,1)}), bf16[64,8,1024]{2,1,0:T(8,128)(2,1)S(1)}, u32[]{:S(2)}, u32[]{:S(2)}) %all-to-all-start.2) | async-done | bytes 1048608 | tf_op jit(solution)/shard_map/all_to_all | solution.py:359
  157.8 0.0 copy-done
  157.8 1.7 %combine.1 = bf16[128,1536]{1,0:T(8,128)(2,1)} custom-call(s32[2,128]{1,0:T(2,128)S(1)} %bitcast.15, bf16[512,1024]{1,0:T(8,128)(2,1)S(1)} %bitcast.13, bf16[768,1536]{1,0:T(8,128)(2,1)} %get-tuple-element.15.earlier_ref), custom_call_target="tpu_custom_call" | custom-call | flops 1 | bytes 1 | tf_op jit(solution)/shard_map/combine/pallas_call | solution.py:335
  (1 shorter events, 0.0 us)
Async XLA Ops:
  5.5 46.3 %all-to-all-start = ((bf16[64,8,1152]{2,1,0:T(8,128)(2,1)}), bf16[64,8,1152]{2,1,0:T(8,128)(2,1)S(1)}, u32[]{:S(2)}, u32[]{:S(2)}) async-start(bf16[64,8,1152]{2,1,0:T(8,128)(2,1)} %bitcast.17), calls=%async_computation | async-start | bytes 2359296 | tf_op jit(solution)/shard_map/all_to_all | solution.py:359
  19.8 41.3 %collective-permute-start = (bf16[768,1536]{1,0:T(8,128)(2,1)}, bf16[768,1536]{1,0:T(8,128)(2,1)}, u32[]{:S(2)}, u32[]{:S(2)}) collective-permute-start(bf16[768,1536]{1,0:T(8,128)(2,1)} %in_mine.5), channel_id=1, source_target_pairs={{0,128},{128,0},{1,129},{129,1},{2,130},{130,2},{3,131},{131,3},{4... | collective-permute-start | bytes 7077896 | tf_op jit(solution)/shard_map/ppermute | solution.py:365
  19.9 41.2 %collective-permute-start.1 = (bf16[1536,768]{1,0:T(8,128)(2,1)}, bf16[1536,768]{1,0:T(8,128)(2,1)}, u32[]{:S(2)}, u32[]{:S(2)}) collective-permute-start(bf16[1536,768]{1,0:T(8,128)(2,1)} %out_mine.5), channel_id=1, source_target_pairs={{0,128},{128,0},{1,129},{129,1},{2,130},{130,2},{3,131},{131,3},{4... | collective-permute-start | bytes 7077896 | tf_op jit(solution)/shard_map/ppermute | solution.py:365
  51.8 38.8 %collective-permute-start.2 = (bf16[512,1152]{1,0:T(8,128)(2,1)S(1)}, bf16[512,1152]{1,0:T(8,128)(2,1)}, u32[]{:S(2)}, u32[]{:S(2)}) collective-permute-start(bf16[512,1152]{1,0:T(8,128)(2,1)S(1)} %bitcast.11), channel_id=1, source_target_pairs={{0,1},{1,0},{2,3},{3,2},{4,5},{5,4},{6,7},{7,6},{8,9},{9,8},{10,11... | collective-permute-start | bytes 3538952 | tf_op jit(solution)/shard_map/ppermute | solution.py:371
  51.8 48.5 %all-to-all-start.1 = ((bf16[128,8,768]{2,1,0:T(8,128)(2,1)}), bf16[128,8,768]{2,1,0:T(8,128)(2,1)S(1)}, u32[]{:S(2)}, u32[]{:S(2)}) async-start(bf16[128,8,768]{2,1,0:T(8,128)(2,1)} %bitcast.18), calls=%async_computation.1 | async-start | bytes 3145728 | tf_op jit(solution)/shard_map/all_to_all | solution.py:359
  99.8 18.6 %collective-permute-start.3 = (bf16[192,1536]{1,0:T(8,128)(2,1)}, bf16[192,1536]{1,0:T(8,128)(2,1)S(1)}, u32[]{:S(2)}, u32[]{:S(2)}) collective-permute-start(bf16[192,1536]{1,0:T(8,128)(2,1)} %get-tuple-element.19.earlier_ref), channel_id=1, source_target_pairs={{0,1},{1,0},{2,3},{3,2},{4,5},{5,4},{6,7},{7,6},{8,9},{9,8},{10,11... | collective-permute-start | bytes 1769480 | tf_op jit(solution)/shard_map/ppermute | solution.py:375
  109.7 8.8 %collective-permute-start.4 = (bf16[128,1536]{1,0:T(8,128)(2,1)}, bf16[128,1536]{1,0:T(8,128)(2,1)S(1)}, u32[]{:S(2)}, u32[]{:S(2)}) collective-permute-start(bf16[128,1536]{1,0:T(8,128)(2,1)} %get-tuple-element.22), channel_id=1, source_target_pairs={{0,1},{1,0},{2,3},{3,2},{4,5},{5,4},{6,7},{7,6},{8,9},{9,8},{10,11... | collective-permute-start | bytes 1179656 | tf_op jit(solution)/shard_map/ppermute | solution.py:377
  111.4 25.6 %collective-permute-start.7 = (bf16[256,4608]{1,0:T(8,128)(2,1)}, bf16[256,4608]{1,0:T(8,128)(2,1)}, u32[]{:S(2)}, u32[]{:S(2)}) collective-permute-start(bf16[256,4608]{1,0:T(8,128)(2,1)} %get-tuple-element.28.refs_18_.refs_19_), channel_id=1, source_target_pairs={{0,128},{128,0},{1,129},{129,1},{2,130},{130,2},{3,131},{131,3},{4... | collective-permute-start | bytes 7077896 | tf_op jit(solution)/shard_map/ppermute | solution.py:365
  121.3 36.5 %all-to-all-start.2 = ((bf16[64,8,1024]{2,1,0:T(8,128)(2,1)}), bf16[64,8,1024]{2,1,0:T(8,128)(2,1)S(1)}, u32[]{:S(2)}, u32[]{:S(2)}) async-start(bf16[64,8,1024]{2,1,0:T(8,128)(2,1)} %bitcast.16), calls=%async_computation.2 | async-start | bytes 2097152 | tf_op jit(solution)/shard_map/all_to_all | solution.py:359
  130.4 4.0 %collective-permute-start.5 = (bf16[192,4608]{1,0:T(8,128)(2,1)}, bf16[192,4608]{1,0:T(8,128)(2,1)S(1)}, u32[]{:S(2)}, u32[]{:S(2)}) collective-permute-start(bf16[192,4608]{1,0:T(8,128)(2,1)} %get-tuple-element.24.refs_2_.refs_3_), channel_id=1, source_target_pairs={{0,128},{128,0},{1,129},{129,1},{2,130},{130,2},{3,131},{131,3},{4... | collective-permute-start | bytes 5308424 | tf_op jit(solution)/shard_map/ppermute | solution.py:365
  130.5 6.6 %collective-permute-start.6 = (bf16[192,4608]{1,0:T(8,128)(2,1)}, bf16[192,4608]{1,0:T(8,128)(2,1)}, u32[]{:S(2)}, u32[]{:S(2)}) collective-permute-start(bf16[192,4608]{1,0:T(8,128)(2,1)} %get-tuple-element.26.refs_10_.refs_11_), channel_id=1, source_target_pairs={{0,128},{128,0},{1,129},{129,1},{2,130},{130,2},{3,131},{131,3},{4... | collective-permute-start | bytes 5308424 | tf_op jit(solution)/shard_map/ppermute | solution.py:365
  134.4 2.7 %copy-start.1 = (bf16[192,4608]{1,0:T(8,128)(2,1)}, bf16[192,4608]{1,0:T(8,128)(2,1)S(1)}, u32[]{:S(2)}) copy-start(bf16[192,4608]{1,0:T(8,128)(2,1)S(1)} %collective-permute-done.5.refs_4_.refs_5_.refs_6_.refs_7_) | copy-start | bytes 5308420
  137.0 20.7 %copy-start = (s32[128,2]{0,1:T(2,128)S(1)}, s32[128,2]{0,1:T(2,128)}, u32[]{:S(2)}) copy-start(s32[128,2]{0,1:T(2,128)} %param.8) | copy-start | bytes 3076

commit v4 on v3

--- a/solution.py
+++ b/solution.py
@@ -81,29 +81,36 @@
     return first, match, rank
 
 
-def pack_kernel(routes_ref, gates_ref, tokens_ref, grads_ref, main_ref, last_ref):
+def pack_main_kernel(routes_ref, gates_ref, tokens_ref, grads_ref, main_ref):
     first, match, rank = slot_matches(routes_ref[...])
     gate = jnp.where(first, gates_ref[0:1, :], gates_ref[1:2, :])
     inner = iota((EXPERTS * 8, TOK), 0) & 7
-
-    def scale_of(chosen):
-        return jnp.sum(jnp.where(chosen, gate, 0.0), axis=1, keepdims=True)
-
     place = jnp.where(inner < 3, inner, inner - 3)
     chosen = match & (rank == place.astype(F32)) & (inner < 6)
-    from_tokens, from_grads, scale = mask(chosen & (inner < 3)), mask(chosen & (inner >= 3)), scale_of(chosen)
+    from_tokens, from_grads = mask(chosen & (inner < 3)), mask(chosen & (inner >= 3))
+    token_tail, grad_tail = tokens_ref[:, 1152:], grads_ref[:, 1152:]
     for j in range(3):
         columns = slice(j * 384, (j + 1) * 384)
-        rows = dot(from_tokens, tokens_ref[:, columns])
-        rows += dot(from_grads, grads_ref[:, columns]) * scale
-        chosen = match & (rank == float(j))
-        rows += dot(mask(chosen & (inner == 6)), tokens_ref[:, 1152:])
-        rows += dot(mask(chosen & (inner == 7)), grads_ref[:, 1152:]) * scale_of(chosen)
+        tail = match & (rank == float(j)) & (inner >= 6)
+        scale = jnp.sum(jnp.where(chosen | tail, gate, 0.0), axis=1, keepdims=True)
+        rows = dot(
+            jnp.concatenate([from_tokens, mask(tail & (inner == 6))], axis=1),
+            jnp.concatenate([tokens_ref[:, columns], token_tail], axis=0),
+        )
+        rows += scale * dot(
+            jnp.concatenate([from_grads, mask(tail & (inner == 7))], axis=1),
+            jnp.concatenate([grads_ref[:, columns], grad_tail], axis=0),
+        )
         main_ref[:, columns] = rows.astype(BF)
 
+
+def pack_last_kernel(routes_ref, gates_ref, tokens_ref, grads_ref, last_ref):
+    first, match, rank = slot_matches(routes_ref[...])
+    gate = jnp.where(first, gates_ref[0:1, :], gates_ref[1:2, :])
+    inner = iota((EXPERTS * 8, TOK), 0) & 7
     quarter = inner & 3
     chosen = match & (rank == (3 + (quarter & 1)).astype(F32))
-    scale = scale_of(chosen)
+    scale = jnp.sum(jnp.where(chosen, gate, 0.0), axis=1, keepdims=True)
     rows = jnp.zeros((EXPERTS * 8, 768), F32)
     for j in range(2):
         side = chosen & ((inner >> 2) == j)
@@ -115,17 +122,14 @@
     last_ref[512:1024, :] = last
 
 
-def pack(routes_t, gates_t, tokens, out_grad):
-    return pl.pallas_call(
-        pack_kernel,
-        out_shape=(
-            hbm_shape((512, 1152)),
-            hbm_shape((1024, 768)),
-        ),
+def pack(last, *operands):
+    return pl.pallas_call(
+        pack_last_kernel if last else pack_main_kernel,
+        out_shape=hbm_shape((1024, 768) if last else (512, 1152)),
         compiler_params=params(),
         cost_estimate=SMALL,
-        name="pack",
-    )(*map(in_hbm, (routes_t, gates_t, tokens, out_grad)))
+        name="pack_last" if last else "pack_main",
+    )(*map(in_hbm, operands))
 
 
 def unpack(last, got_ref, token_ref, grad_ref):
@@ -150,7 +154,7 @@
 def expert_kernel(last, flags_ref, earlier_ref, got_ref, in_mine, in_other, out_mine, out_other, *rest):
     count = 4 if last else 3
     mine_out, send_out, *part_outs = rest[:count]
-    w1_mine, w1_other, w2_mine, w2_other, token, grad, mine, send, units_out, *parts, loads, stores = rest[count:]
+    w1_mine, w1_other, w2_mine, w2_other, got, token, grad, mine, send, units_out, *parts, loads, stores = rest[count:]
     low, high = pl.ds(0, HALF), pl.ds(HALF, HALF)
     first = flags_ref[0] == 0
     weights = ((in_mine, w1_mine), (in_other, w1_other), (out_mine, w2_mine), (out_other, w2_other))
@@ -160,10 +164,12 @@
         for k in range(2):
             rows = pl.ds(k * half, half)
             arrivals.append(pltpu.make_async_copy(source.at[rows, :], target.at[rows, :], loads.at[len(arrivals)]))
+    got_here = pltpu.make_async_copy(got_ref, got, loads.at[8])
+    got_here.start()
     for k in (0, 1, 2, 3, 4, 6, 5, 7):
         arrivals[k].start()
-
-    unpack(last, got_ref, token, grad)
+    got_here.wait()
+    unpack(last, got, token, grad)
 
     def both_orders(run):
         pl.when(first)(lambda: run(low, high))
@@ -182,9 +188,7 @@
         departures.append(pltpu.make_async_copy(source, target, stores.at[len(departures)]))
         departures[-1].start()
 
-    depart(mine, mine_out)
-    depart(send, send_out.at[:, pl.ds(0, D)])
-    pre = None
+    pre = part_mine = part_other = None
     for k, (rows, w1) in enumerate(((mine, w1_mine), (mine, w1_mine), (send, w1_other), (send, w1_other))):
         arrivals[k].wait()
         part = pl.ds((k % 2) * (HALF // 2), HALF // 2)
@@ -200,11 +204,16 @@
         th = jnp.tanh(ROOT_TWO_PI * (value + CUBIC * square * value))
         half = 0.5 * (1.0 + th)
         slope = half + 0.5 * value * (1.0 - th * th) * ROOT_TWO_PI * (1.0 + 3.0 * CUBIC * square)
+        d_pre = (back * slope).astype(BF)
         units_out[:, k * HALF:(k + 1) * HALF] = (value * half).astype(BF)
-        units_out[:, (2 + k) * HALF:(3 + k) * HALF] = (back * slope).astype(BF)
-    depart(units_out, send_out.at[:, pl.ds(D, 2 * D)])
-    d_pre = units_out[:, D:]
-    part_mine, part_other = dot_nt(d_pre, w1_mine[...]).astype(BF), dot_nt(d_pre, w1_other[...]).astype(BF)
+        units_out[:, (2 + k) * HALF:(3 + k) * HALF] = d_pre
+        if k == 1:
+            depart(mine, mine_out)
+            depart(send, send_out.at[:, pl.ds(0, D)])
+            depart(units_out, send_out.at[:, pl.ds(D, 2 * D)])
+        terms = dot_nt(d_pre, w1_mine[:, units]), dot_nt(d_pre, w1_other[:, units])
+        part_mine, part_other = terms if k == 0 else (part_mine + terms[0], part_other + terms[1])
+    part_mine, part_other = part_mine.astype(BF), part_other.astype(BF)
 
     def finish(own, other):
         for columns, part in ((own, part_mine), (other, part_other)):
@@ -233,17 +242,17 @@
     parts = [(128, D)] * 2 if last else [(192, D)]
     outs = [(rows, D), (rows, 3 * D), *parts]
     anywhere = pl.BlockSpec(memory_space=pl.ANY)
-    buffers = [(HALF, D)] * 2 + [(D, HALF)] * 2 + [(rows, D)] * 4 + [(rows, 2 * D)] + parts
+    buffers = [(HALF, D)] * 2 + [(D, HALF)] * 2 + [got.shape] + [(rows, D)] * 4 + [(rows, 2 * D)] + parts
     return pl.pallas_call(
         functools.partial(expert_kernel, last),
         in_specs=[
-            pl.BlockSpec(memory_space=pltpu.SMEM), anywhere, whole(got.shape), *[anywhere] * 4
+            pl.BlockSpec(memory_space=pltpu.SMEM), *[anywhere] * 6
         ],
         out_specs=(anywhere,) * len(outs),
         out_shape=tuple(hbm_shape(shape) for shape in outs),
         scratch_shapes=[
             *(pltpu.VMEM(shape, BF) for shape in buffers),
-            pltpu.SemaphoreType.DMA((8,)),
+            pltpu.SemaphoreType.DMA((9,)),
             pltpu.SemaphoreType.DMA((5,)),
         ],
         compiler_params=params(40),
@@ -297,20 +306,21 @@
     target = ((column & 31) << 3) + (column >> 5)
     row6, column6 = iota((256, 192), 0), iota((256, 192), 1)
     spread = mask(row6 == ((column6 & 31) << 3) + (column6 >> 5))
-    for g in range(2):
-        a, b = slice(g * 96, (g + 1) * 96), slice(g * 64, (g + 1) * 64)
-        three = (main_a[a, :].astype(F32) + main_b[a, :].astype(F32)).astype(BF)
-        two = (last_a[b, :].astype(F32) + last_b[b, :].astype(F32)).astype(BF)
-        four = jnp.concatenate([three, two[:32]], axis=0)
-        folded = dot(mask(row == target), four[:, :768]) + dot(mask(row == target + 4), four[:, 768:])
-        out_ref[g * 256:(g + 1) * 256, :768] = folded.astype(BF)
-        fifth = jnp.concatenate([two[32:, j * 256:(j + 1) * 256] for j in range(6)], axis=0)
-        out_ref[g * 256:(g + 1) * 256, 768:] = dot(spread, fifth).astype(BF)
+    three = (main_a[...].astype(F32) + main_b[...].astype(F32)).astype(BF)
+    two = (last_a[...].astype(F32) + last_b[...].astype(F32)).astype(BF)
+    four = jnp.concatenate([three, two[:32]], axis=0)
+    folded = dot(mask(row == target), four[:, :768]) + dot(mask(row == target + 4), four[:, 768:])
+    out_ref[:, :768] = folded.astype(BF)
+    fifth = jnp.concatenate([two[32:, j * 256:(j + 1) * 256] for j in range(6)], axis=0)
+    out_ref[:, 768:] = dot(spread, fifth).astype(BF)
 
 
 def merge(*parts):
     return pl.pallas_call(
         merge_kernel,
+        grid=(2,),
+        in_specs=[pl.BlockSpec((rows, D), lambda g: (g, 0)) for rows in (96, 96, 64, 64)],
+        out_specs=pl.BlockSpec((256, 1024), lambda g: (g, 0)),
         out_shape=hbm_shape((512, 1024)),
         compiler_params=params(),
         cost_estimate=SMALL,
@@ -364,9 +374,11 @@
     def to_other_core(x):
         return lax.ppermute(x, "dp", cores)
 
-    weights = (weight_in, to_other_core(weight_in), weight_out, to_other_core(weight_out))
     routes_t, gates_t = routes.T, gate_probs.T
-    send_main, send_last = pack(routes_t, gates_t, tokens, out_grad)
+    send_main = pack(False, routes_t, gates_t, tokens, out_grad)
+    send_last = pack(True, routes_t, gates_t, tokens, out_grad)
+    weight_sent = after(weight_out, send_last)
+    weights = (weight_in, to_other_core(weight_in), weight_out, to_other_core(weight_sent))
     own_got = exchange(send_main, halves)
     pair_got = lax.ppermute(own_got, "expert", chips)
     own_mine, own_send, own_part = expert_rows(False, flags, send_main, own_got, weights)

time: 160 us -> 158 us (0.988)
  waiting for transfers between devices: 73.5 us -> 69.5 us
    all_to_all x3, waiting for transfers between devices: 39.7 us -> 34.7 us  [exchange(): lax.all_to_all(chunked, 'expert', split_axis=0, concat_axis=0, tiled=True...]
    pallas_call x2 -> x3, Pallas kernels: 7.67 us -> 9.86 us  [the longest x2 7.2 us: pack(): pl.pallas_call(pack_last_kernel if last else pack_main_kernel, out_shape=...]
  transfers between devices with their start and end apart: 11 -> 11, of which waited for: 6 -> 6; matrix products, arithmetic and copies ran while one was open for 0% -> 1% of each run, Pallas kernels for 27% -> 28%
where the time goes in v4:
time: 158 us
  waiting for transfers between devices  69.5 us (44%)
  Pallas kernels  49.9 us (32%)
  starting transfers between devices  36 us (23%)
    all_to_all x3, waiting for transfers between devices, exchange(): lax.all_to_all(chunked, 'expert', split_axis=0, concat_axis=0, tiled=True...  34.7 us
    all_to_all x3, starting transfers between devices, exchange(): lax.all_to_all(chunked, 'expert', split_axis=0, concat_axis=0, tiled=True...  32.5 us
    pallas_call x3, Pallas kernels, expert_rows(): pl.pallas_call(functools.partial(expert_kernel, last), in_specs=[pl.Block...  26 us
    ppermute x1, waiting for transfers between devices, per_device(): pair_got = lax.ppermute(own_got, 'expert', chips)  21.1 us
    pallas_call x1, Pallas kernels, weight_grads(): pl.pallas_call(weight_grads_kernel, grid=(2,), in_specs=specs, out_specs=...  12.4 us
    ppermute x1, waiting for transfers between devices, per_device(): other_last = lax.ppermute(last_away, 'expert', chips)  7.65 us
    pallas_call x2, Pallas kernels, pack(): pl.pallas_call(pack_last_kernel if last else pack_main_kernel, out_shape=...  7.2 us
    ppermute x5, waiting for transfers between devices, to_other_core(): return lax.ppermute(x, 'dp', cores)  6.06 us
  transfers between devices with their start and end apart: 11, of which 6 were waited for; matrix products, arithmetic and copies ran while one was open for 1% of the time, Pallas kernels for 28%

profile of v4, /device:TPU:8, one launch (start us, length us, event | category | flops | bytes accessed | tf_op | source)
XLA Modules:
  0.0 157.7 jit_solution(1501171907285573557)
XLA Ops:
  0.6 3.5 %pack_main.1.earlier_ref = bf16[512,1152]{1,0:T(8,128)(2,1)} custom-call(s32[2,128]{1,0:T(2,128)} %bitcast.14, f32[2,128]{1,0:T(2,128)} %bitcast.20, bf16[128,1536]{1,0:T(8,128)(2,1)} %tokens_ref.3, bf16[128,1536]{1,0:T(8,128)(2,1)} %grads_ref.3), custom_call_target="tpu_custom_call" | custom-call | flops 1 | bytes 1 | tf_op jit(solution)/shard_map/pack_main/pallas_call | solution.py:126
  4.2 14.3 %all-to-all-start = ((bf16[64,8,1152]{2,1,0:T(8,128)(2,1)}), bf16[64,8,1152]{2,1,0:T(8,128)(2,1)S(1)}, u32[]{:S(2)}, u32[]{:S(2)}) async-start(bf16[64,8,1152]{2,1,0:T(8,128)(2,1)} %bitcast.18), calls=%async_computation | async-start | bytes 2359296 | tf_op jit(solution)/shard_map/all_to_all | solution.py:369
  18.5 0.0 copy-start.2
  18.5 3.7 %pack_last.1.earlier_ref = bf16[1024,768]{1,0:T(8,128)(2,1)} custom-call(s32[2,128]{1,0:T(2,128)} %bitcast.15, f32[2,128]{1,0:T(2,128)} %bitcast.21, bf16[128,1536]{1,0:T(8,128)(2,1)} %tokens_ref.3, bf16[128,1536]{1,0:T(8,128)(2,1)} %grads_ref.3), custom_call_target="tpu_custom_call" | custom-call | flops 1 | bytes 1 | tf_op jit(solution)/shard_map/pack_last/pallas_call | solution.py:126
  22.2 0.0 copy-done.2
  22.2 1.4 copy.11.x_ref
  23.6 0.0 collective-permute-start.1
  23.6 0.5 collective-permute-start
  24.1 26.4 %all-to-all-done = bf16[64,8,1152]{2,1,0:T(8,128)(2,1)S(1)} async-done(((bf16[64,8,1152]{2,1,0:T(8,128)(2,1)}), bf16[64,8,1152]{2,1,0:T(8,128)(2,1)S(1)}, u32[]{:S(2)}, u32[]{:S(2)}) %all-to-all-start) | async-done | bytes 1179680 | tf_op jit(solution)/shard_map/all_to_all | solution.py:369
  50.5 0.0 collective-permute-start.2
  50.5 9.1 %all-to-all-start.1 = ((bf16[128,8,768]{2,1,0:T(8,128)(2,1)}), bf16[128,8,768]{2,1,0:T(8,128)(2,1)S(1)}, u32[]{:S(2)}, u32[]{:S(2)}) async-start(bf16[128,8,768]{2,1,0:T(8,128)(2,1)} %bitcast.17), calls=%async_computation.1 | async-start | bytes 3145728 | tf_op jit(solution)/shard_map/all_to_all | solution.py:369
  59.6 0.1 pad_add_fusion.flags_ref
  59.7 0.0 collective-permute-done.1.out_other
  59.7 0.0 collective-permute-done.in_other
  59.7 8.5 %expert_main.2 = (bf16[192,1536]{1,0:T(8,128)(2,1)}, bf16[192,4608]{1,0:T(8,128)(2,1)}, bf16[192,1536]{1,0:T(8,128)(2,1)}) custom-call(s32[2]{0:T(128)S(1)} %pad_add_fusion.flags_ref, bf16[512,1152]{1,0:T(8,128)(2,1)} %pack_main.1.earlier_ref, bf16[512,1152]{1,0:T(8,128)(2,1)S(1)} %bitcast.12, bf16[768,1536]{1,0:T(8,128)(2,1)} %in_mine.5, ...), custom_call_target="tpu_custom_call" | custom-call | flops 1 | bytes 1 | tf_op jit(solution)/shard_map/expert_main/pallas_call | solution.py:246
  68.2 21.1 %collective-permute-done.2.got_ref = bf16[512,1152]{1,0:T(8,128)(2,1)} collective-permute-done((bf16[512,1152]{1,0:T(8,128)(2,1)S(1)}, bf16[512,1152]{1,0:T(8,128)(2,1)}, u32[]{:S(2)}, u32[]{:S(2)}) %collective-permute-start.2) | collective-permute-done | bytes 1179680 | tf_op jit(solution)/shard_map/ppermute | solution.py:383
  89.3 8.7 %expert_main.3 = (bf16[192,1536]{1,0:T(8,128)(2,1)}, bf16[192,4608]{1,0:T(8,128)(2,1)}, bf16[192,1536]{1,0:T(8,128)(2,1)}) custom-call(s32[2]{0:T(128)S(1)} %pad_add_fusion.flags_ref, bf16[192,1536]{1,0:T(8,128)(2,1)} %get-tuple-element.15.earlier_ref.main_a, bf16[512,1152]{1,0:T(8,128)(2,1)} %collective-permute-done.2.got_ref, bf16[768,1536]{1,0:T(8,128)(2,1)} %in_mine.5, ...), custom_call_target="tpu_custom_call" | custom-call | flops 99999997952 | bytes 100000000 | tf_op jit(solution)/shard_map/expert_main/pallas_call | solution.py:246
  98.0 0.5 collective-permute-start.3
  98.5 0.0 all-to-all-done.1
  98.5 8.7 %expert_last.1 = (bf16[256,1536]{1,0:T(8,128)(2,1)}, bf16[256,4608]{1,0:T(8,128)(2,1)}, bf16[128,1536]{1,0:T(8,128)(2,1)}, bf16[128,1536]{1,0:T(8,128)(2,1)}) custom-call(s32[2]{0:T(128)S(1)} %pad_add_fusion.flags_ref, bf16[192,1536]{1,0:T(8,128)(2,1)} %get-tuple-element.16.earlier_ref, bf16[1024,768]{1,0:T(8,128)(2,1)S(1)} %bitcast.10, ...), custom_call_target="tpu_custom_call" | custom-call | flops 1 | bytes 1 | tf_op jit(solution)/shard_map/expert_last/pallas_call | solution.py:246
  107.3 1.7 %collective-permute-start.4 = (bf16[128,1536]{1,0:T(8,128)(2,1)}, bf16[128,1536]{1,0:T(8,128)(2,1)S(1)}, u32[]{:S(2)}, u32[]{:S(2)}) collective-permute-start(bf16[128,1536]{1,0:T(8,128)(2,1)} %get-tuple-element.18), channel_id=1, source_target_pairs={{0,1},{1,0},{2,3},{3,2},{4,5},{5,4},{6,7},{7,6},{8,9},{9,8},{10,11... | collective-permute-start | bytes 1179656 | tf_op jit(solution)/shard_map/ppermute | solution.py:389
  109.0 0.0 collective-permute-start.7
  109.0 7.6 %collective-permute-done.4.last_b = bf16[128,1536]{1,0:T(8,128)(2,1)S(1)} collective-permute-done((bf16[128,1536]{1,0:T(8,128)(2,1)}, bf16[128,1536]{1,0:T(8,128)(2,1)S(1)}, u32[]{:S(2)}, u32[]{:S(2)}) %collective-permute-start.4) | collective-permute-done | bytes 393248 | tf_op jit(solution)/shard_map/ppermute | solution.py:389
  116.6 0.0 collective-permute-done.3.main_b
  116.7 2.7 %merge.1.earlier_ref = bf16[512,1024]{1,0:T(8,128)(2,1)} custom-call(bf16[192,1536]{1,0:T(8,128)(2,1)} %get-tuple-element.15.earlier_ref.main_a, bf16[192,1536]{1,0:T(8,128)(2,1)S(1)} %collective-permute-done.3.main_b, bf16[128,1536]{1,0:T(8,128)(2,1)} %get-tuple-element.17.last_a, bf16[128,1536]{1,0:T(8,128)(2,1)S(1)} %collective-permute-done.4.last_b), custom_call_target="tpu_custom_call" | custom-call | flops 1 | bytes 1 | tf_op jit(solution)/shard_map/merge/pallas_call | solution.py:319
  119.3 9.1 %all-to-all-start.2 = ((bf16[64,8,1024]{2,1,0:T(8,128)(2,1)}), bf16[64,8,1024]{2,1,0:T(8,128)(2,1)S(1)}, u32[]{:S(2)}, u32[]{:S(2)}) async-start(bf16[64,8,1024]{2,1,0:T(8,128)(2,1)} %bitcast.19), calls=%async_computation.2 | async-start | bytes 2097152 | tf_op jit(solution)/shard_map/all_to_all | solution.py:369
  128.4 0.3 collective-permute-start.5
  128.7 0.5 collective-permute-start.6
  129.2 4.9 %collective-permute-done.5.refs_4_.refs_5_.refs_6_.refs_7_ = bf16[192,4608]{1,0:T(8,128)(2,1)S(1)} collective-permute-done((bf16[192,4608]{1,0:T(8,128)(2,1)}, bf16[192,4608]{1,0:T(8,128)(2,1)S(1)}, u32[]{:S(2)}, u32[]{:S(2)}) %collective-permute-start.5) | collective-permute-done | bytes 1769504 | tf_op jit(solution)/shard_map/ppermute | solution.py:375
  134.2 0.0 copy-start.1
  134.2 1.1 collective-permute-done.6.refs_12_.refs_13_.refs_14_.refs_15_
  135.3 0.0 collective-permute-done.7.refs_20_.refs_21_.refs_22_.refs_23_
  135.3 0.1 copy-done.1
  135.4 0.0 copy-start
  135.4 12.4 %weight_grads.1 = (bf16[768,1536]{1,0:T(8,128)(2,1)}, bf16[1536,768]{1,0:T(8,128)(2,1)}) custom-call(bf16[192,1536]{1,0:T(8,128)(2,1)} %get-tuple-element.19.refs_0_.refs_1_, bf16[192,1536]{1,0:T(8,128)(2,1)} %get-tuple-element.19.refs_0_.refs_1_, bf16[192,4608]{1,0:T(8,128)(2,1)} %get-tuple-element.20.refs_2_.refs_3_, ...), custom_call_target="tpu_custom_call" | custom-call | flops 1 | bytes 1 | tf_op jit(solution)/shard_map/weight_grads/pallas_call | solution.py:289
  147.8 8.3 %all-to-all-done.2 = bf16[64,8,1024]{2,1,0:T(8,128)(2,1)S(1)} async-done(((bf16[64,8,1024]{2,1,0:T(8,128)(2,1)}), bf16[64,8,1024]{2,1,0:T(8,128)(2,1)S(1)}, u32[]{:S(2)}, u32[]{:S(2)}) %all-to-all-start.2) | async-done | bytes 1048608 | tf_op jit(solution)/shard_map/all_to_all | solution.py:369
  156.1 0.0 copy-done
  156.1 1.7 %combine.1 = bf16[128,1536]{1,0:T(8,128)(2,1)} custom-call(s32[2,128]{1,0:T(2,128)S(1)} %bitcast.16, bf16[512,1024]{1,0:T(8,128)(2,1)S(1)} %bitcast.13, bf16[768,1536]{1,0:T(8,128)(2,1)} %get-tuple-element.13.earlier_ref), custom_call_target="tpu_custom_call" | custom-call | flops 1 | bytes 1 | tf_op jit(solution)/shard_map/combine/pallas_call | solution.py:345
  (2 shorter events, 0.0 us)
Async XLA Ops:
  4.2 46.3 %all-to-all-start = ((bf16[64,8,1152]{2,1,0:T(8,128)(2,1)}), bf16[64,8,1152]{2,1,0:T(8,128)(2,1)S(1)}, u32[]{:S(2)}, u32[]{:S(2)}) async-start(bf16[64,8,1152]{2,1,0:T(8,128)(2,1)} %bitcast.18), calls=%async_computation | async-start | bytes 2359296 | tf_op jit(solution)/shard_map/all_to_all | solution.py:369
  18.5 3.7 %copy-start.2 = (bf16[1536,768]{1,0:T(8,128)(2,1)S(1)}, bf16[1536,768]{1,0:T(8,128)(2,1)}, u32[]{:S(2)}) copy-start(bf16[1536,768]{1,0:T(8,128)(2,1)} %out_mine.5) | copy-start | bytes 7077892
  23.6 36.2 %collective-permute-start.1 = (bf16[1536,768]{1,0:T(8,128)(2,1)}, bf16[1536,768]{1,0:T(8,128)(2,1)}, u32[]{:S(2)}, u32[]{:S(2)}) collective-permute-start(bf16[1536,768]{1,0:T(8,128)(2,1)} %after.2), channel_id=1, source_target_pairs={{0,128},{128,0},{1,129},{129,1},{2,130},{130,2},{3,131},{131,3},{4... | collective-permute-start | bytes 7077896 | tf_op jit(solution)/shard_map/ppermute | solution.py:375
  23.6 36.2 %collective-permute-start = (bf16[768,1536]{1,0:T(8,128)(2,1)}, bf16[768,1536]{1,0:T(8,128)(2,1)}, u32[]{:S(2)}, u32[]{:S(2)}) collective-permute-start(bf16[768,1536]{1,0:T(8,128)(2,1)} %in_mine.5), channel_id=1, source_target_pairs={{0,128},{128,0},{1,129},{129,1},{2,130},{130,2},{3,131},{131,3},{4... | collective-permute-start | bytes 7077896 | tf_op jit(solution)/shard_map/ppermute | solution.py:375
  50.5 38.8 %collective-permute-start.2 = (bf16[512,1152]{1,0:T(8,128)(2,1)S(1)}, bf16[512,1152]{1,0:T(8,128)(2,1)}, u32[]{:S(2)}, u32[]{:S(2)}) collective-permute-start(bf16[512,1152]{1,0:T(8,128)(2,1)S(1)} %bitcast.11), channel_id=1, source_target_pairs={{0,1},{1,0},{2,3},{3,2},{4,5},{5,4},{6,7},{7,6},{8,9},{9,8},{10,11... | collective-permute-start | bytes 3538952 | tf_op jit(solution)/shard_map/ppermute | solution.py:383
  50.5 48.0 %all-to-all-start.1 = ((bf16[128,8,768]{2,1,0:T(8,128)(2,1)}), bf16[128,8,768]{2,1,0:T(8,128)(2,1)S(1)}, u32[]{:S(2)}, u32[]{:S(2)}) async-start(bf16[128,8,768]{2,1,0:T(8,128)(2,1)} %bitcast.17), calls=%async_computation.1 | async-start | bytes 3145728 | tf_op jit(solution)/shard_map/all_to_all | solution.py:369
  98.0 18.6 %collective-permute-start.3 = (bf16[192,1536]{1,0:T(8,128)(2,1)}, bf16[192,1536]{1,0:T(8,128)(2,1)S(1)}, u32[]{:S(2)}, u32[]{:S(2)}) collective-permute-start(bf16[192,1536]{1,0:T(8,128)(2,1)} %get-tuple-element.16.earlier_ref), channel_id=1, source_target_pairs={{0,1},{1,0},{2,3},{3,2},{4,5},{5,4},{6,7},{7,6},{8,9},{9,8},{10,11... | collective-permute-start | bytes 1769480 | tf_op jit(solution)/shard_map/ppermute | solution.py:387
  107.3 9.4 %collective-permute-start.4 = (bf16[128,1536]{1,0:T(8,128)(2,1)}, bf16[128,1536]{1,0:T(8,128)(2,1)S(1)}, u32[]{:S(2)}, u32[]{:S(2)}) collective-permute-start(bf16[128,1536]{1,0:T(8,128)(2,1)} %get-tuple-element.18), channel_id=1, source_target_pairs={{0,1},{1,0},{2,3},{3,2},{4,5},{5,4},{6,7},{7,6},{8,9},{9,8},{10,11... | collective-permute-start | bytes 1179656 | tf_op jit(solution)/shard_map/ppermute | solution.py:389
  109.0 26.3 %collective-permute-start.7 = (bf16[256,4608]{1,0:T(8,128)(2,1)}, bf16[256,4608]{1,0:T(8,128)(2,1)}, u32[]{:S(2)}, u32[]{:S(2)}) collective-permute-start(bf16[256,4608]{1,0:T(8,128)(2,1)} %get-tuple-element.24.refs_18_.refs_19_), channel_id=1, source_target_pairs={{0,128},{128,0},{1,129},{129,1},{2,130},{130,2},{3,131},{131,3},{4... | collective-permute-start | bytes 7077896 | tf_op jit(solution)/shard_map/ppermute | solution.py:375
  119.3 36.8 %all-to-all-start.2 = ((bf16[64,8,1024]{2,1,0:T(8,128)(2,1)}), bf16[64,8,1024]{2,1,0:T(8,128)(2,1)S(1)}, u32[]{:S(2)}, u32[]{:S(2)}) async-start(bf16[64,8,1024]{2,1,0:T(8,128)(2,1)} %bitcast.19), calls=%async_computation.2 | async-start | bytes 2097152 | tf_op jit(solution)/shard_map/all_to_all | solution.py:369
  128.4 5.7 %collective-permute-start.5 = (bf16[192,4608]{1,0:T(8,128)(2,1)}, bf16[192,4608]{1,0:T(8,128)(2,1)S(1)}, u32[]{:S(2)}, u32[]{:S(2)}) collective-permute-start(bf16[192,4608]{1,0:T(8,128)(2,1)} %get-tuple-element.20.refs_2_.refs_3_), channel_id=1, source_target_pairs={{0,128},{128,0},{1,129},{129,1},{2,130},{130,2},{3,131},{131,3},{4... | collective-permute-start | bytes 5308424 | tf_op jit(solution)/shard_map/ppermute | solution.py:375
  128.7 6.6 %collective-permute-start.6 = (bf16[192,4608]{1,0:T(8,128)(2,1)}, bf16[192,4608]{1,0:T(8,128)(2,1)}, u32[]{:S(2)}, u32[]{:S(2)}) collective-permute-start(bf16[192,4608]{1,0:T(8,128)(2,1)} %get-tuple-element.22.refs_10_.refs_11_), channel_id=1, source_target_pairs={{0,128},{128,0},{1,129},{129,1},{2,130},{130,2},{3,131},{131,3},{4... | collective-permute-start | bytes 5308424 | tf_op jit(solution)/shard_map/ppermute | solution.py:375
  134.2 1.2 copy-start.1
  135.4 20.7 %copy-start = (s32[128,2]{0,1:T(2,128)S(1)}, s32[128,2]{0,1:T(2,128)}, u32[]{:S(2)}) copy-start(s32[128,2]{0,1:T(2,128)} %param.8) | copy-start | bytes 3076

commit v5 on v4

--- a/solution.py
+++ b/solution.py
@@ -81,13 +81,14 @@
     return first, match, rank
 
 
-def pack_main_kernel(routes_ref, gates_ref, tokens_ref, grads_ref, main_ref):
+def pack_main_kernel(routes_ref, gates_ref, tokens_ref, grads_ref, main_ref, rows_ref, sems):
     first, match, rank = slot_matches(routes_ref[...])
     gate = jnp.where(first, gates_ref[0:1, :], gates_ref[1:2, :])
     inner = iota((EXPERTS * 8, TOK), 0) & 7
     place = jnp.where(inner < 3, inner, inner - 3)
     chosen = match & (rank == place.astype(F32)) & (inner < 6)
     from_tokens, from_grads = mask(chosen & (inner < 3)), mask(chosen & (inner >= 3))
+    copies = []
     token_tail, grad_tail = tokens_ref[:, 1152:], grads_ref[:, 1152:]
     for j in range(3):
         columns = slice(j * 384, (j + 1) * 384)
@@ -101,7 +102,11 @@
             jnp.concatenate([from_grads, mask(tail & (inner == 7))], axis=1),
             jnp.concatenate([grads_ref[:, columns], grad_tail], axis=0),
         )
-        main_ref[:, columns] = rows.astype(BF)
+        rows_ref[j] = rows.astype(BF)
+        copies.append(pltpu.make_async_copy(rows_ref.at[j], main_ref.at[:, pl.ds(j * 384, 384)], sems.at[j]))
+        copies[j].start()
+    for copy in copies:
+        copy.wait()
 
 
 def pack_last_kernel(routes_ref, gates_ref, tokens_ref, grads_ref, last_ref):
@@ -123,9 +128,13 @@
 
 
 def pack(last, *operands):
+    shape = (1024, 768) if last else (512, 1152)
+    scratch = [] if last else [pltpu.VMEM((3, 512, 384), BF), pltpu.SemaphoreType.DMA((3,))]
     return pl.pallas_call(
         pack_last_kernel if last else pack_main_kernel,
-        out_shape=hbm_shape((1024, 768) if last else (512, 1152)),
+        out_specs=whole(shape) if last else pl.BlockSpec(memory_space=pl.ANY),
+        out_shape=hbm_shape(shape),
+        scratch_shapes=scratch,
         compiler_params=params(),
         cost_estimate=SMALL,
         name="pack_last" if last else "pack_main",
@@ -151,10 +160,9 @@
                 grad_ref[target, 1152:] = rows[224:256, j * 384:(j + 1) * 384]
 
 
-def expert_kernel(last, flags_ref, earlier_ref, got_ref, in_mine, in_other, out_mine, out_other, *rest):
-    count = 4 if last else 3
-    mine_out, send_out, *part_outs = rest[:count]
-    w1_mine, w1_other, w2_mine, w2_other, got, token, grad, mine, send, units_out, *parts, loads, stores = rest[count:]
+def expert_kernel(last, away, flags_ref, earlier_ref, got_ref, in_mine, in_other, out_mine, out_other, *rest):
+    mine_out, send_out, part_out = rest[:3]
+    w1_mine, w1_other, w2_mine, w2_other, got, token, grad, mine, send, units_out, part, loads, stores = rest[3:]
     low, high = pl.ds(0, HALF), pl.ds(HALF, HALF)
     first = flags_ref[0] == 0
     weights = ((in_mine, w1_mine), (in_other, w1_other), (out_mine, w2_mine), (out_other, w2_other))
@@ -164,6 +172,9 @@
         for k in range(2):
             rows = pl.ds(k * half, half)
             arrivals.append(pltpu.make_async_copy(source.at[rows, :], target.at[rows, :], loads.at[len(arrivals)]))
+    if last:
+        group = 1 - flags_ref[1] if away else flags_ref[1]
+        got_ref = got_ref.at[pl.ds(pl.multiple_of(group * 512, 512), 512), :]
     got_here = pltpu.make_async_copy(got_ref, got, loads.at[8])
     got_here.start()
     for k in (0, 1, 2, 3, 4, 6, 5, 7):
@@ -191,8 +202,8 @@
     pre = part_mine = part_other = None
     for k, (rows, w1) in enumerate(((mine, w1_mine), (mine, w1_mine), (send, w1_other), (send, w1_other))):
         arrivals[k].wait()
-        part = pl.ds((k % 2) * (HALF // 2), HALF // 2)
-        term = dot(rows[:, part], w1[part, :])
+        chunk = pl.ds((k % 2) * (HALF // 2), HALF // 2)
+        term = dot(rows[:, chunk], w1[chunk, :])
         pre = term if pre is None else pre + term
     for k in range(2):
         units = slice(k * HALF, (k + 1) * HALF)
@@ -216,35 +227,22 @@
     part_mine, part_other = part_mine.astype(BF), part_other.astype(BF)
 
     def finish(own, other):
-        for columns, part in ((own, part_mine), (other, part_other)):
-            if last:
-                kept, away = parts
-
-                @pl.when(flags_ref[1] == 0)
-                def _():
-                    kept[:, columns], away[:, columns] = part[:128], part[128:]
-
-                @pl.when(flags_ref[1] != 0)
-                def _():
-                    kept[:, columns], away[:, columns] = part[128:], part[:128]
-            else:
-                parts[0][:, columns] = part
+        part[:, own] = part_mine
+        part[:, other] = part_other
 
     both_orders(finish)
-    for part, out in zip(parts, part_outs):
-        depart(part, out)
+    depart(part, part_out)
     for copy in departures:
         copy.wait()
 
 
-def expert_rows(last, flags, earlier, got, weights, cost=SMALL):
-    rows = 256 if last else 192
-    parts = [(128, D)] * 2 if last else [(192, D)]
-    outs = [(rows, D), (rows, 3 * D), *parts]
+def expert_rows(last, flags, earlier, got, weights, cost=SMALL, away=False):
+    rows = 128 if last else 192
+    outs = [(rows, D), (rows, 3 * D), (rows, D)]
     anywhere = pl.BlockSpec(memory_space=pl.ANY)
-    buffers = [(HALF, D)] * 2 + [(D, HALF)] * 2 + [got.shape] + [(rows, D)] * 4 + [(rows, 2 * D)] + parts
-    return pl.pallas_call(
-        functools.partial(expert_kernel, last),
+    buffers = [(HALF, D)] * 2 + [(D, HALF)] * 2 + [(512, got.shape[1])] + [(rows, D)] * 4 + [(rows, 2 * D), (rows, D)]
+    return pl.pallas_call(
+        functools.partial(expert_kernel, last, away),
         in_specs=[
             pl.BlockSpec(memory_space=pltpu.SMEM), *[anywhere] * 6
         ],
@@ -253,7 +251,7 @@
         scratch_shapes=[
             *(pltpu.VMEM(shape, BF) for shape in buffers),
             pltpu.SemaphoreType.DMA((9,)),
-            pltpu.SemaphoreType.DMA((5,)),
+            pltpu.SemaphoreType.DMA((4,)),
         ],
         compiler_params=params(40),
         cost_estimate=cost,
@@ -264,7 +262,7 @@
 def weight_grads_kernel(*refs):
     in_ref, out_ref = refs[-2:]
     first = second = None
-    for i in range(0, 24, 4):
+    for i in range(0, len(refs) - 2, 4):
         token_ref, grad_ref, hidden_ref, dpre_ref = refs[i:i + 4]
         a, b = dot_tn(token_ref[...], dpre_ref[...]), dot_tn(hidden_ref[...], grad_ref[...])
         first, second = (a, b) if first is None else (first + a, second + b)
@@ -385,13 +383,15 @@
     last_got = exchange(send_last, everyone)
     pair_mine, pair_send, pair_part = expert_rows(False, flags, own_part, pair_got, weights, LARGE)
     other_main = lax.ppermute(pair_part, "expert", chips)
-    last_mine, last_send, last_part, last_away = expert_rows(True, flags, pair_part, last_got, weights)
-    other_last = lax.ppermute(last_away, "expert", chips)
+    away_mine, away_send, away_part = expert_rows(True, flags, pair_part, last_got, weights, away=True)
+    other_last = lax.ppermute(away_part, "expert", chips)
+    last_mine, last_send, last_part = expert_rows(True, flags, away_part, last_got, weights)
     merged = merge(own_part, other_main, last_part, other_last)
     got = exchange(merged, halves)
     grad_in, grad_out = weight_grads([
         (own_mine, own_send, to_other_core(own_send)),
         (pair_mine, pair_send, to_other_core(pair_send)),
+        (away_mine, away_send, to_other_core(away_send)),
         (after(last_mine, merged), last_send, to_other_core(last_send)),
     ])
     return combine(routes_t, got, grad_in), grad_in, grad_out

time: 158 us -> 157 us (level)
  waiting for transfers between devices: 69.5 us -> 58.7 us
  Pallas kernels: 49.9 us -> 59.6 us
    ppermute x1, waiting for transfers between devices: 7.65 us -> 0.26 us  [per_device(): other_last = lax.ppermute(away_part, 'expert', chips)]
    pallas_call x5 -> x6, Pallas kernels: 33.2 us -> 40.3 us  [the longest x4 33.3 us: expert_rows(): pl.pallas_call(functools.partial(expert_kernel, last, away), in_specs=[pl...]
    all_to_all x3, waiting for transfers between devices: 34.7 us -> 28.5 us  [exchange(): lax.all_to_all(chunked, 'expert', split_axis=0, concat_axis=0, tiled=True...]
    ppermute x5 -> x6, waiting for transfers between devices: 6.06 us -> 8.92 us  [to_other_core(): return lax.ppermute(x, 'dp', cores)]
    pallas_call x1, Pallas kernels: 12.4 us -> 14.9 us  [weight_grads(): pl.pallas_call(weight_grads_kernel, grid=(2,), in_specs=specs, out_specs=...]
  transfers between devices with their start and end apart: 11 -> 12, of which waited for: 6 -> 7; matrix products, arithmetic and copies ran while one was open for 1% -> 1% of each run, Pallas kernels for 28% -> 33%
where the time goes in v5:
time: 157 us
  Pallas kernels  59.6 us (38%)
  waiting for transfers between devices  58.7 us (37%)
  starting transfers between devices  36.3 us (23%)
    pallas_call x4, Pallas kernels, expert_rows(): pl.pallas_call(functools.partial(expert_kernel, last, away), in_specs=[pl...  33.3 us
    all_to_all x3, starting transfers between devices, exchange(): lax.all_to_all(chunked, 'expert', split_axis=0, concat_axis=0, tiled=True...  32.5 us
    all_to_all x3, waiting for transfers between devices, exchange(): lax.all_to_all(chunked, 'expert', split_axis=0, concat_axis=0, tiled=True...  28.5 us
    ppermute x1, waiting for transfers between devices, per_device(): pair_got = lax.ppermute(own_got, 'expert', chips)  21.1 us
    pallas_call x1, Pallas kernels, weight_grads(): pl.pallas_call(weight_grads_kernel, grid=(2,), in_specs=specs, out_specs=...  14.9 us
    ppermute x6, waiting for transfers between devices, to_other_core(): return lax.ppermute(x, 'dp', cores)  8.92 us
    pallas_call x2, Pallas kernels, pack(): pl.pallas_call(pack_last_kernel if last else pack_main_kernel, out_specs=...  6.98 us
  transfers between devices with their start and end apart: 12, of which 7 were waited for; matrix products, arithmetic and copies ran while one was open for 1% of the time, Pallas kernels for 33%

profile of v5, /device:TPU:8, one launch (start us, length us, event | category | flops | bytes accessed | tf_op | source)
XLA Modules:
  0.0 156.9 jit_solution(14610108423389257017)
XLA Ops:
  0.6 3.3 %pack_main.1.earlier_ref = bf16[512,1152]{1,0:T(8,128)(2,1)} custom-call(s32[2,128]{1,0:T(2,128)} %bitcast.15, f32[2,128]{1,0:T(2,128)} %bitcast.21, bf16[128,1536]{1,0:T(8,128)(2,1)} %tokens_ref.3, bf16[128,1536]{1,0:T(8,128)(2,1)} %grads_ref.3), custom_call_target="tpu_custom_call" | custom-call | flops 1 | bytes 1 | tf_op jit(solution)/shard_map/pack_main/pallas_call | solution.py:133
  3.9 14.3 %all-to-all-start = ((bf16[64,8,1152]{2,1,0:T(8,128)(2,1)}), bf16[64,8,1152]{2,1,0:T(8,128)(2,1)S(1)}, u32[]{:S(2)}, u32[]{:S(2)}) async-start(bf16[64,8,1152]{2,1,0:T(8,128)(2,1)} %bitcast.19), calls=%async_computation | async-start | bytes 2359296 | tf_op jit(solution)/shard_map/all_to_all | solution.py:367
  18.3 0.0 copy-start.1
  18.3 3.7 %pack_last.1.earlier_ref = bf16[1024,768]{1,0:T(8,128)(2,1)} custom-call(s32[2,128]{1,0:T(2,128)} %bitcast.16, f32[2,128]{1,0:T(2,128)} %bitcast.22, bf16[128,1536]{1,0:T(8,128)(2,1)} %tokens_ref.3, bf16[128,1536]{1,0:T(8,128)(2,1)} %grads_ref.3), custom_call_target="tpu_custom_call" | custom-call | flops 1 | bytes 1 | tf_op jit(solution)/shard_map/pack_last/pallas_call | solution.py:133
  22.0 0.0 copy-done.1
  22.0 1.4 copy.11.x_ref
  23.4 0.0 collective-permute-start.1
  23.4 0.5 collective-permute-start
  23.9 26.4 %all-to-all-done = bf16[64,8,1152]{2,1,0:T(8,128)(2,1)S(1)} async-done(((bf16[64,8,1152]{2,1,0:T(8,128)(2,1)}), bf16[64,8,1152]{2,1,0:T(8,128)(2,1)S(1)}, u32[]{:S(2)}, u32[]{:S(2)}) %all-to-all-start) | async-done | bytes 1179680 | tf_op jit(solution)/shard_map/all_to_all | solution.py:367
  50.3 0.0 collective-permute-start.2
  50.3 9.1 %all-to-all-start.1 = ((bf16[128,8,768]{2,1,0:T(8,128)(2,1)}), bf16[128,8,768]{2,1,0:T(8,128)(2,1)S(1)}, u32[]{:S(2)}, u32[]{:S(2)}) async-start(bf16[128,8,768]{2,1,0:T(8,128)(2,1)} %bitcast.18), calls=%async_computation.1 | async-start | bytes 3145728 | tf_op jit(solution)/shard_map/all_to_all | solution.py:367
  59.5 0.1 pad_add_fusion.flags_ref
  59.5 0.0 collective-permute-done.1.out_other
  59.5 0.0 collective-permute-done.in_other
  59.5 8.5 %expert_main.2 = (bf16[192,1536]{1,0:T(8,128)(2,1)}, bf16[192,4608]{1,0:T(8,128)(2,1)}, bf16[192,1536]{1,0:T(8,128)(2,1)}) custom-call(s32[2]{0:T(128)S(1)} %pad_add_fusion.flags_ref, bf16[512,1152]{1,0:T(8,128)(2,1)} %pack_main.1.earlier_ref, bf16[512,1152]{1,0:T(8,128)(2,1)S(1)} %bitcast.13, bf16[768,1536]{1,0:T(8,128)(2,1)} %in_mine.7, ...), custom_call_target="tpu_custom_call" | custom-call | flops 1 | bytes 1 | tf_op jit(solution)/shard_map/expert_main/pallas_call | solution.py:244
  68.0 21.1 %collective-permute-done.2.got_ref = bf16[512,1152]{1,0:T(8,128)(2,1)} collective-permute-done((bf16[512,1152]{1,0:T(8,128)(2,1)S(1)}, bf16[512,1152]{1,0:T(8,128)(2,1)}, u32[]{:S(2)}, u32[]{:S(2)}) %collective-permute-start.2) | collective-permute-done | bytes 1179680 | tf_op jit(solution)/shard_map/ppermute | solution.py:381
  89.1 8.7 %expert_main.3 = (bf16[192,1536]{1,0:T(8,128)(2,1)}, bf16[192,4608]{1,0:T(8,128)(2,1)}, bf16[192,1536]{1,0:T(8,128)(2,1)}) custom-call(s32[2]{0:T(128)S(1)} %pad_add_fusion.flags_ref, bf16[192,1536]{1,0:T(8,128)(2,1)} %get-tuple-element.17.earlier_ref.main_a, bf16[512,1152]{1,0:T(8,128)(2,1)} %collective-permute-done.2.got_ref, bf16[768,1536]{1,0:T(8,128)(2,1)} %in_mine.7, ...), custom_call_target="tpu_custom_call" | custom-call | flops 99999997952 | bytes 100000000 | tf_op jit(solution)/shard_map/expert_main/pallas_call | solution.py:244
  97.8 0.5 collective-permute-start.3
  98.3 0.0 all-to-all-done.1
  98.3 8.1 %expert_last.2 = (bf16[128,1536]{1,0:T(8,128)(2,1)}, bf16[128,4608]{1,0:T(8,128)(2,1)}, bf16[128,1536]{1,0:T(8,128)(2,1)}) custom-call(s32[2]{0:T(128)S(1)} %pad_add_fusion.flags_ref, bf16[192,1536]{1,0:T(8,128)(2,1)} %get-tuple-element.18.earlier_ref, bf16[1024,768]{1,0:T(8,128)(2,1)S(1)} %bitcast.10, bf16[768,1536]{1,0:T(8,128)(2,1)} %in_mine.7, ...), custom_call_target="tpu_custom_call" | custom-call | flops 1 | bytes 1 | tf_op jit(solution)/shard_map/expert_last/pallas_call | solution.py:244
  106.4 1.7 %collective-permute-start.4 = (bf16[128,1536]{1,0:T(8,128)(2,1)}, bf16[128,1536]{1,0:T(8,128)(2,1)S(1)}, u32[]{:S(2)}, u32[]{:S(2)}) collective-permute-start(bf16[128,1536]{1,0:T(8,128)(2,1)} %get-tuple-element.19.earlier_ref), channel_id=1, source_target_pairs={{0,1},{1,0},{2,3},{3,2},{4,5},{5,4},{6,7},{7,6},{8,9},{9,8},{10,11... | collective-permute-start | bytes 1179656 | tf_op jit(solution)/shard_map/ppermute | solution.py:387
  108.1 8.1 %expert_last.3 = (bf16[128,1536]{1,0:T(8,128)(2,1)}, bf16[128,4608]{1,0:T(8,128)(2,1)}, bf16[128,1536]{1,0:T(8,128)(2,1)}) custom-call(s32[2]{0:T(128)S(1)} %pad_add_fusion.flags_ref, bf16[128,1536]{1,0:T(8,128)(2,1)} %get-tuple-element.19.earlier_ref, bf16[1024,768]{1,0:T(8,128)(2,1)S(1)} %bitcast.11, bf16[768,1536]{1,0:T(8,128)(2,1)} %in_mine.7, ...), custom_call_target="tpu_custom_call" | custom-call | flops 1 | bytes 1 | tf_op jit(solution)/shard_map/expert_last/pallas_call | solution.py:244
  116.2 0.3 collective-permute-done.4.last_b
  116.4 0.0 collective-permute-done.3.main_b
  116.4 2.7 %merge.1.earlier_ref = bf16[512,1024]{1,0:T(8,128)(2,1)} custom-call(bf16[192,1536]{1,0:T(8,128)(2,1)} %get-tuple-element.17.earlier_ref.main_a, bf16[192,1536]{1,0:T(8,128)(2,1)S(1)} %collective-permute-done.3.main_b, bf16[128,1536]{1,0:T(8,128)(2,1)} %get-tuple-element.20.last_a, bf16[128,1536]{1,0:T(8,128)(2,1)S(1)} %collective-permute-done.4.last_b), custom_call_target="tpu_custom_call" | custom-call | flops 1 | bytes 1 | tf_op jit(solution)/shard_map/merge/pallas_call | solution.py:317
  119.1 9.1 %all-to-all-start.2 = ((bf16[64,8,1024]{2,1,0:T(8,128)(2,1)}), bf16[64,8,1024]{2,1,0:T(8,128)(2,1)S(1)}, u32[]{:S(2)}, u32[]{:S(2)}) async-start(bf16[64,8,1024]{2,1,0:T(8,128)(2,1)} %bitcast.20), calls=%async_computation.2 | async-start | bytes 2097152 | tf_op jit(solution)/shard_map/all_to_all | solution.py:367
  128.2 0.1 collective-permute-start.5
  128.3 0.5 collective-permute-start.6
  128.8 0.1 collective-permute-start.8
  128.9 0.4 collective-permute-start.7
  129.3 4.4 %collective-permute-done.5.refs_4_.refs_5_.refs_6_.refs_7_ = bf16[192,4608]{1,0:T(8,128)(2,1)S(1)} collective-permute-done((bf16[192,4608]{1,0:T(8,128)(2,1)}, bf16[192,4608]{1,0:T(8,128)(2,1)S(1)}, u32[]{:S(2)}, u32[]{:S(2)}) %collective-permute-start.5) | collective-permute-done | bytes 1769504 | tf_op jit(solution)/shard_map/ppermute | solution.py:373
  133.7 0.0 copy-start.2
  133.7 2.8 %collective-permute-done.8.refs_28_.refs_29_.refs_30_.refs_31_ = bf16[128,4608]{1,0:T(8,128)(2,1)} collective-permute-done((bf16[128,4608]{1,0:T(8,128)(2,1)}, bf16[128,4608]{1,0:T(8,128)(2,1)}, u32[]{:S(2)}, u32[]{:S(2)}) %collective-permute-start.8) | collective-permute-done | bytes 1179680 | tf_op jit(solution)/shard_map/ppermute | solution.py:373
  136.5 1.7 %collective-permute-done.7.refs_20_.refs_21_.refs_22_.refs_23_ = bf16[128,4608]{1,0:T(8,128)(2,1)} collective-permute-done((bf16[128,4608]{1,0:T(8,128)(2,1)}, bf16[128,4608]{1,0:T(8,128)(2,1)}, u32[]{:S(2)}, u32[]{:S(2)}) %collective-permute-start.7) | collective-permute-done | bytes 1179680 | tf_op jit(solution)/shard_map/ppermute | solution.py:373
  138.2 0.0 collective-permute-done.6.refs_12_.refs_13_.refs_14_.refs_15_
  138.2 0.0 copy-done.2
  138.2 0.0 copy-start
  138.2 14.9 %weight_grads.1 = (bf16[768,1536]{1,0:T(8,128)(2,1)}, bf16[1536,768]{1,0:T(8,128)(2,1)}) custom-call(bf16[192,1536]{1,0:T(8,128)(2,1)} %get-tuple-element.21.refs_0_.refs_1_, bf16[192,1536]{1,0:T(8,128)(2,1)} %get-tuple-element.21.refs_0_.refs_1_, bf16[192,4608]{1,0:T(8,128)(2,1)} %get-tuple-element.22.refs_2_.refs_3_, ...), custom_call_target="tpu_custom_call" | custom-call | flops 1 | bytes 1 | tf_op jit(solution)/shard_map/weight_grads/pallas_call | solution.py:287
  153.2 2.0 %all-to-all-done.2 = bf16[64,8,1024]{2,1,0:T(8,128)(2,1)S(1)} async-done(((bf16[64,8,1024]{2,1,0:T(8,128)(2,1)}), bf16[64,8,1024]{2,1,0:T(8,128)(2,1)S(1)}, u32[]{:S(2)}, u32[]{:S(2)}) %all-to-all-start.2) | async-done | bytes 1048608 | tf_op jit(solution)/shard_map/all_to_all | solution.py:367
  155.2 0.0 copy-done
  155.2 1.7 %combine.1 = bf16[128,1536]{1,0:T(8,128)(2,1)} custom-call(s32[2,128]{1,0:T(2,128)S(1)} %bitcast.17, bf16[512,1024]{1,0:T(8,128)(2,1)S(1)} %bitcast.14, bf16[768,1536]{1,0:T(8,128)(2,1)} %get-tuple-element.15.earlier_ref), custom_call_target="tpu_custom_call" | custom-call | flops 1 | bytes 1 | tf_op jit(solution)/shard_map/combine/pallas_call | solution.py:343
  (2 shorter events, 0.0 us)
Async XLA Ops:
  3.9 46.4 %all-to-all-start = ((bf16[64,8,1152]{2,1,0:T(8,128)(2,1)}), bf16[64,8,1152]{2,1,0:T(8,128)(2,1)S(1)}, u32[]{:S(2)}, u32[]{:S(2)}) async-start(bf16[64,8,1152]{2,1,0:T(8,128)(2,1)} %bitcast.19), calls=%async_computation | async-start | bytes 2359296 | tf_op jit(solution)/shard_map/all_to_all | solution.py:367
  18.3 3.7 %copy-start.1 = (bf16[1536,768]{1,0:T(8,128)(2,1)S(1)}, bf16[1536,768]{1,0:T(8,128)(2,1)}, u32[]{:S(2)}) copy-start(bf16[1536,768]{1,0:T(8,128)(2,1)} %out_mine.7) | copy-start | bytes 7077892
  23.4 36.2 %collective-permute-start.1 = (bf16[1536,768]{1,0:T(8,128)(2,1)}, bf16[1536,768]{1,0:T(8,128)(2,1)}, u32[]{:S(2)}, u32[]{:S(2)}) collective-permute-start(bf16[1536,768]{1,0:T(8,128)(2,1)} %after.2), channel_id=1, source_target_pairs={{0,128},{128,0},{1,129},{129,1},{2,130},{130,2},{3,131},{131,3},{4... | collective-permute-start | bytes 7077896 | tf_op jit(solution)/shard_map/ppermute | solution.py:373
  23.4 36.2 %collective-permute-start = (bf16[768,1536]{1,0:T(8,128)(2,1)}, bf16[768,1536]{1,0:T(8,128)(2,1)}, u32[]{:S(2)}, u32[]{:S(2)}) collective-permute-start(bf16[768,1536]{1,0:T(8,128)(2,1)} %in_mine.7), channel_id=1, source_target_pairs={{0,128},{128,0},{1,129},{129,1},{2,130},{130,2},{3,131},{131,3},{4... | collective-permute-start | bytes 7077896 | tf_op jit(solution)/shard_map/ppermute | solution.py:373
  50.3 38.8 %collective-permute-start.2 = (bf16[512,1152]{1,0:T(8,128)(2,1)S(1)}, bf16[512,1152]{1,0:T(8,128)(2,1)}, u32[]{:S(2)}, u32[]{:S(2)}) collective-permute-start(bf16[512,1152]{1,0:T(8,128)(2,1)S(1)} %bitcast.12), channel_id=1, source_target_pairs={{0,1},{1,0},{2,3},{3,2},{4,5},{5,4},{6,7},{7,6},{8,9},{9,8},{10,11... | collective-permute-start | bytes 3538952 | tf_op jit(solution)/shard_map/ppermute | solution.py:381
  50.3 48.0 %all-to-all-start.1 = ((bf16[128,8,768]{2,1,0:T(8,128)(2,1)}), bf16[128,8,768]{2,1,0:T(8,128)(2,1)S(1)}, u32[]{:S(2)}, u32[]{:S(2)}) async-start(bf16[128,8,768]{2,1,0:T(8,128)(2,1)} %bitcast.18), calls=%async_computation.1 | async-start | bytes 3145728 | tf_op jit(solution)/shard_map/all_to_all | solution.py:367
  97.8 18.6 %collective-permute-start.3 = (bf16[192,1536]{1,0:T(8,128)(2,1)}, bf16[192,1536]{1,0:T(8,128)(2,1)S(1)}, u32[]{:S(2)}, u32[]{:S(2)}) collective-permute-start(bf16[192,1536]{1,0:T(8,128)(2,1)} %get-tuple-element.18.earlier_ref), channel_id=1, source_target_pairs={{0,1},{1,0},{2,3},{3,2},{4,5},{5,4},{6,7},{7,6},{8,9},{9,8},{10,11... | collective-permute-start | bytes 1769480 | tf_op jit(solution)/shard_map/ppermute | solution.py:385
  106.4 10.1 %collective-permute-start.4 = (bf16[128,1536]{1,0:T(8,128)(2,1)}, bf16[128,1536]{1,0:T(8,128)(2,1)S(1)}, u32[]{:S(2)}, u32[]{:S(2)}) collective-permute-start(bf16[128,1536]{1,0:T(8,128)(2,1)} %get-tuple-element.19.earlier_ref), channel_id=1, source_target_pairs={{0,1},{1,0},{2,3},{3,2},{4,5},{5,4},{6,7},{7,6},{8,9},{9,8},{10,11... | collective-permute-start | bytes 1179656 | tf_op jit(solution)/shard_map/ppermute | solution.py:387
  119.1 36.1 %all-to-all-start.2 = ((bf16[64,8,1024]{2,1,0:T(8,128)(2,1)}), bf16[64,8,1024]{2,1,0:T(8,128)(2,1)S(1)}, u32[]{:S(2)}, u32[]{:S(2)}) async-start(bf16[64,8,1024]{2,1,0:T(8,128)(2,1)} %bitcast.20), calls=%async_computation.2 | async-start | bytes 2097152 | tf_op jit(solution)/shard_map/all_to_all | solution.py:367
  128.2 5.5 %collective-permute-start.5 = (bf16[192,4608]{1,0:T(8,128)(2,1)}, bf16[192,4608]{1,0:T(8,128)(2,1)S(1)}, u32[]{:S(2)}, u32[]{:S(2)}) collective-permute-start(bf16[192,4608]{1,0:T(8,128)(2,1)} %get-tuple-element.22.refs_2_.refs_3_), channel_id=1, source_target_pairs={{0,128},{128,0},{1,129},{129,1},{2,130},{130,2},{3,131},{131,3},{4... | collective-permute-start | bytes 5308424 | tf_op jit(solution)/shard_map/ppermute | solution.py:373
  128.3 9.9 %collective-permute-start.6 = (bf16[192,4608]{1,0:T(8,128)(2,1)}, bf16[192,4608]{1,0:T(8,128)(2,1)}, u32[]{:S(2)}, u32[]{:S(2)}) collective-permute-start(bf16[192,4608]{1,0:T(8,128)(2,1)} %get-tuple-element.24.refs_10_.refs_11_), channel_id=1, source_target_pairs={{0,128},{128,0},{1,129},{129,1},{2,130},{130,2},{3,131},{131,3},{4... | collective-permute-start | bytes 5308424 | tf_op jit(solution)/shard_map/ppermute | solution.py:373
  128.8 7.7 %collective-permute-start.8 = (bf16[128,4608]{1,0:T(8,128)(2,1)}, bf16[128,4608]{1,0:T(8,128)(2,1)}, u32[]{:S(2)}, u32[]{:S(2)}) collective-permute-start(bf16[128,4608]{1,0:T(8,128)(2,1)} %get-tuple-element.28.refs_26_.refs_27_), channel_id=1, source_target_pairs={{0,128},{128,0},{1,129},{129,1},{2,130},{130,2},{3,131},{131,3},{4... | collective-permute-start | bytes 3538952 | tf_op jit(solution)/shard_map/ppermute | solution.py:373
  128.9 9.3 %collective-permute-start.7 = (bf16[128,4608]{1,0:T(8,128)(2,1)}, bf16[128,4608]{1,0:T(8,128)(2,1)}, u32[]{:S(2)}, u32[]{:S(2)}) collective-permute-start(bf16[128,4608]{1,0:T(8,128)(2,1)} %get-tuple-element.26.refs_18_.refs_19_), channel_id=1, source_target_pairs={{0,128},{128,0},{1,129},{129,1},{2,130},{130,2},{3,131},{131,3},{4... | collective-permute-start | bytes 3538952 | tf_op jit(solution)/shard_map/ppermute | solution.py:373
  133.7 4.5 %copy-start.2 = (bf16[192,4608]{1,0:T(8,128)(2,1)}, bf16[192,4608]{1,0:T(8,128)(2,1)S(1)}, u32[]{:S(2)}) copy-start(bf16[192,4608]{1,0:T(8,128)(2,1)S(1)} %collective-permute-done.5.refs_4_.refs_5_.refs_6_.refs_7_) | copy-start | bytes 5308420
  138.2 17.0 %copy-start = (s32[128,2]{0,1:T(2,128)S(1)}, s32[128,2]{0,1:T(2,128)}, u32[]{:S(2)}) copy-start(s32[128,2]{0,1:T(2,128)} %param.8) | copy-start | bytes 3076

commit v6 on v5

--- a/solution.py
+++ b/solution.py
@@ -260,14 +260,12 @@
 
 
 def weight_grads_kernel(*refs):
-    in_ref, out_ref = refs[-2:]
-    first = second = None
-    for i in range(0, len(refs) - 2, 4):
-        token_ref, grad_ref, hidden_ref, dpre_ref = refs[i:i + 4]
-        a, b = dot_tn(token_ref[...], dpre_ref[...]), dot_tn(hidden_ref[...], grad_ref[...])
-        first, second = (a, b) if first is None else (first + a, second + b)
-    in_ref[...] = first.astype(BF)
-    out_ref[...] = second.astype(BF)
+    *operands, in_ref, out_ref = refs
+    tokens, grads, hidden, d_pre = (
+        jnp.concatenate([ref[...] for ref in operands[i::4]], axis=0) for i in range(4)
+    )
+    in_ref[...] = dot_tn(tokens, d_pre).astype(BF)
+    out_ref[...] = dot_tn(hidden, grads).astype(BF)
 
 
 def weight_grads(sets):

time: 157 us -> 157 us (level)
  Pallas kernels: 59.6 us -> 55.6 us
  waiting for transfers between devices: 58.7 us -> 62.7 us
    all_to_all x3, waiting for transfers between devices: 28.5 us -> 32.4 us  [exchange(): lax.all_to_all(chunked, 'expert', split_axis=0, concat_axis=0, tiled=True...]
    pallas_call x1, Pallas kernels: 14.9 us -> 11 us  [weight_grads(): pl.pallas_call(weight_grads_kernel, grid=(2,), in_specs=specs, out_specs=...]
  transfers between devices with their start and end apart: 12 -> 12, of which waited for: 7 -> 7; matrix products, arithmetic and copies ran while one was open for 1% -> 1% of each run, Pallas kernels for 33% -> 31%
where the time goes in v6:
time: 157 us
  waiting for transfers between devices  62.7 us (40%)
  Pallas kernels  55.6 us (35%)
  starting transfers between devices  36.3 us (23%)
    pallas_call x4, Pallas kernels, expert_rows(): pl.pallas_call(functools.partial(expert_kernel, last, away), in_specs=[pl...  33.3 us
    all_to_all x3, starting transfers between devices, exchange(): lax.all_to_all(chunked, 'expert', split_axis=0, concat_axis=0, tiled=True...  32.5 us
    all_to_all x3, waiting for transfers between devices, exchange(): lax.all_to_all(chunked, 'expert', split_axis=0, concat_axis=0, tiled=True...  32.4 us
    ppermute x1, waiting for transfers between devices, per_device(): pair_got = lax.ppermute(own_got, 'expert', chips)  21.1 us
    pallas_call x1, Pallas kernels, weight_grads(): pl.pallas_call(weight_grads_kernel, grid=(2,), in_specs=specs, out_specs=...  11 us
    ppermute x6, waiting for transfers between devices, to_other_core(): return lax.ppermute(x, 'dp', cores)  8.92 us
    pallas_call x2, Pallas kernels, pack(): pl.pallas_call(pack_last_kernel if last else pack_main_kernel, out_specs=...  6.98 us
  transfers between devices with their start and end apart: 12, of which 7 were waited for; matrix products, arithmetic and copies ran while one was open for 1% of the time, Pallas kernels for 31%

profile of v6, /device:TPU:8, one launch (start us, length us, event | category | flops | bytes accessed | tf_op | source)
XLA Modules:
  0.0 156.9 jit_solution(18235973944945936739)
XLA Ops:
  0.6 3.3 %pack_main.1.earlier_ref = bf16[512,1152]{1,0:T(8,128)(2,1)} custom-call(s32[2,128]{1,0:T(2,128)} %bitcast.15, f32[2,128]{1,0:T(2,128)} %bitcast.21, bf16[128,1536]{1,0:T(8,128)(2,1)} %tokens_ref.3, bf16[128,1536]{1,0:T(8,128)(2,1)} %grads_ref.3), custom_call_target="tpu_custom_call" | custom-call | flops 1 | bytes 1 | tf_op jit(solution)/shard_map/pack_main/pallas_call | solution.py:133
  3.9 14.3 %all-to-all-start = ((bf16[64,8,1152]{2,1,0:T(8,128)(2,1)}), bf16[64,8,1152]{2,1,0:T(8,128)(2,1)S(1)}, u32[]{:S(2)}, u32[]{:S(2)}) async-start(bf16[64,8,1152]{2,1,0:T(8,128)(2,1)} %bitcast.19), calls=%async_computation | async-start | bytes 2359296 | tf_op jit(solution)/shard_map/all_to_all | solution.py:365
  18.3 0.0 copy-start.1
  18.3 3.7 %pack_last.1.earlier_ref = bf16[1024,768]{1,0:T(8,128)(2,1)} custom-call(s32[2,128]{1,0:T(2,128)} %bitcast.16, f32[2,128]{1,0:T(2,128)} %bitcast.22, bf16[128,1536]{1,0:T(8,128)(2,1)} %tokens_ref.3, bf16[128,1536]{1,0:T(8,128)(2,1)} %grads_ref.3), custom_call_target="tpu_custom_call" | custom-call | flops 1 | bytes 1 | tf_op jit(solution)/shard_map/pack_last/pallas_call | solution.py:133
  22.0 0.0 copy-done.1
  22.0 1.4 copy.11.x_ref
  23.4 0.0 collective-permute-start.1
  23.4 0.5 collective-permute-start
  23.9 26.4 %all-to-all-done = bf16[64,8,1152]{2,1,0:T(8,128)(2,1)S(1)} async-done(((bf16[64,8,1152]{2,1,0:T(8,128)(2,1)}), bf16[64,8,1152]{2,1,0:T(8,128)(2,1)S(1)}, u32[]{:S(2)}, u32[]{:S(2)}) %all-to-all-start) | async-done | bytes 1179680 | tf_op jit(solution)/shard_map/all_to_all | solution.py:365
  50.3 0.0 collective-permute-start.2
  50.3 9.1 %all-to-all-start.1 = ((bf16[128,8,768]{2,1,0:T(8,128)(2,1)}), bf16[128,8,768]{2,1,0:T(8,128)(2,1)S(1)}, u32[]{:S(2)}, u32[]{:S(2)}) async-start(bf16[128,8,768]{2,1,0:T(8,128)(2,1)} %bitcast.18), calls=%async_computation.1 | async-start | bytes 3145728 | tf_op jit(solution)/shard_map/all_to_all | solution.py:365
  59.5 0.1 pad_add_fusion.flags_ref
  59.5 0.0 collective-permute-done.1.out_other
  59.5 0.0 collective-permute-done.in_other
  59.5 8.5 %expert_main.2 = (bf16[192,1536]{1,0:T(8,128)(2,1)}, bf16[192,4608]{1,0:T(8,128)(2,1)}, bf16[192,1536]{1,0:T(8,128)(2,1)}) custom-call(s32[2]{0:T(128)S(1)} %pad_add_fusion.flags_ref, bf16[512,1152]{1,0:T(8,128)(2,1)} %pack_main.1.earlier_ref, bf16[512,1152]{1,0:T(8,128)(2,1)S(1)} %bitcast.13, bf16[768,1536]{1,0:T(8,128)(2,1)} %in_mine.7, ...), custom_call_target="tpu_custom_call" | custom-call | flops 1 | bytes 1 | tf_op jit(solution)/shard_map/expert_main/pallas_call | solution.py:244
  68.0 21.1 %collective-permute-done.2.got_ref = bf16[512,1152]{1,0:T(8,128)(2,1)} collective-permute-done((bf16[512,1152]{1,0:T(8,128)(2,1)S(1)}, bf16[512,1152]{1,0:T(8,128)(2,1)}, u32[]{:S(2)}, u32[]{:S(2)}) %collective-permute-start.2) | collective-permute-done | bytes 1179680 | tf_op jit(solution)/shard_map/ppermute | solution.py:379
  89.1 8.7 %expert_main.3 = (bf16[192,1536]{1,0:T(8,128)(2,1)}, bf16[192,4608]{1,0:T(8,128)(2,1)}, bf16[192,1536]{1,0:T(8,128)(2,1)}) custom-call(s32[2]{0:T(128)S(1)} %pad_add_fusion.flags_ref, bf16[192,1536]{1,0:T(8,128)(2,1)} %get-tuple-element.17.earlier_ref.main_a, bf16[512,1152]{1,0:T(8,128)(2,1)} %collective-permute-done.2.got_ref, bf16[768,1536]{1,0:T(8,128)(2,1)} %in_mine.7, ...), custom_call_target="tpu_custom_call" | custom-call | flops 99999997952 | bytes 100000000 | tf_op jit(solution)/shard_map/expert_main/pallas_call | solution.py:244
  97.8 0.5 collective-permute-start.3
  98.3 0.0 all-to-all-done.1
  98.3 8.1 %expert_last.2 = (bf16[128,1536]{1,0:T(8,128)(2,1)}, bf16[128,4608]{1,0:T(8,128)(2,1)}, bf16[128,1536]{1,0:T(8,128)(2,1)}) custom-call(s32[2]{0:T(128)S(1)} %pad_add_fusion.flags_ref, bf16[192,1536]{1,0:T(8,128)(2,1)} %get-tuple-element.18.earlier_ref, bf16[1024,768]{1,0:T(8,128)(2,1)S(1)} %bitcast.10, bf16[768,1536]{1,0:T(8,128)(2,1)} %in_mine.7, ...), custom_call_target="tpu_custom_call" | custom-call | flops 1 | bytes 1 | tf_op jit(solution)/shard_map/expert_last/pallas_call | solution.py:244
  106.4 1.7 %collective-permute-start.4 = (bf16[128,1536]{1,0:T(8,128)(2,1)}, bf16[128,1536]{1,0:T(8,128)(2,1)S(1)}, u32[]{:S(2)}, u32[]{:S(2)}) collective-permute-start(bf16[128,1536]{1,0:T(8,128)(2,1)} %get-tuple-element.19.earlier_ref), channel_id=1, source_target_pairs={{0,1},{1,0},{2,3},{3,2},{4,5},{5,4},{6,7},{7,6},{8,9},{9,8},{10,11... | collective-permute-start | bytes 1179656 | tf_op jit(solution)/shard_map/ppermute | solution.py:385
  108.1 8.1 %expert_last.3 = (bf16[128,1536]{1,0:T(8,128)(2,1)}, bf16[128,4608]{1,0:T(8,128)(2,1)}, bf16[128,1536]{1,0:T(8,128)(2,1)}) custom-call(s32[2]{0:T(128)S(1)} %pad_add_fusion.flags_ref, bf16[128,1536]{1,0:T(8,128)(2,1)} %get-tuple-element.19.earlier_ref, bf16[1024,768]{1,0:T(8,128)(2,1)S(1)} %bitcast.11, bf16[768,1536]{1,0:T(8,128)(2,1)} %in_mine.7, ...), custom_call_target="tpu_custom_call" | custom-call | flops 1 | bytes 1 | tf_op jit(solution)/shard_map/expert_last/pallas_call | solution.py:244
  116.2 0.3 collective-permute-done.4.last_b
  116.4 0.0 collective-permute-done.3.main_b
  116.4 2.7 %merge.1.earlier_ref = bf16[512,1024]{1,0:T(8,128)(2,1)} custom-call(bf16[192,1536]{1,0:T(8,128)(2,1)} %get-tuple-element.17.earlier_ref.main_a, bf16[192,1536]{1,0:T(8,128)(2,1)S(1)} %collective-permute-done.3.main_b, bf16[128,1536]{1,0:T(8,128)(2,1)} %get-tuple-element.20.last_a, bf16[128,1536]{1,0:T(8,128)(2,1)S(1)} %collective-permute-done.4.last_b), custom_call_target="tpu_custom_call" | custom-call | flops 1 | bytes 1 | tf_op jit(solution)/shard_map/merge/pallas_call | solution.py:315
  119.1 9.1 %all-to-all-start.2 = ((bf16[64,8,1024]{2,1,0:T(8,128)(2,1)}), bf16[64,8,1024]{2,1,0:T(8,128)(2,1)S(1)}, u32[]{:S(2)}, u32[]{:S(2)}) async-start(bf16[64,8,1024]{2,1,0:T(8,128)(2,1)} %bitcast.20), calls=%async_computation.2 | async-start | bytes 2097152 | tf_op jit(solution)/shard_map/all_to_all | solution.py:365
  128.2 0.1 collective-permute-start.5
  128.3 0.5 collective-permute-start.6
  128.8 0.1 collective-permute-start.8
  128.9 0.4 collective-permute-start.7
  129.3 4.4 %collective-permute-done.5.refs_4_.refs_5_.refs_6_.refs_7_ = bf16[192,4608]{1,0:T(8,128)(2,1)S(1)} collective-permute-done((bf16[192,4608]{1,0:T(8,128)(2,1)}, bf16[192,4608]{1,0:T(8,128)(2,1)S(1)}, u32[]{:S(2)}, u32[]{:S(2)}) %collective-permute-start.5) | collective-permute-done | bytes 1769504 | tf_op jit(solution)/shard_map/ppermute | solution.py:371
  133.7 0.0 copy-start.2
  133.7 2.8 %collective-permute-done.8.refs_28_.refs_29_.refs_30_.refs_31_ = bf16[128,4608]{1,0:T(8,128)(2,1)} collective-permute-done((bf16[128,4608]{1,0:T(8,128)(2,1)}, bf16[128,4608]{1,0:T(8,128)(2,1)}, u32[]{:S(2)}, u32[]{:S(2)}) %collective-permute-start.8) | collective-permute-done | bytes 1179680 | tf_op jit(solution)/shard_map/ppermute | solution.py:371
  136.5 1.7 %collective-permute-done.7.refs_20_.refs_21_.refs_22_.refs_23_ = bf16[128,4608]{1,0:T(8,128)(2,1)} collective-permute-done((bf16[128,4608]{1,0:T(8,128)(2,1)}, bf16[128,4608]{1,0:T(8,128)(2,1)}, u32[]{:S(2)}, u32[]{:S(2)}) %collective-permute-start.7) | collective-permute-done | bytes 1179680 | tf_op jit(solution)/shard_map/ppermute | solution.py:371
  138.2 0.0 collective-permute-done.6.refs_12_.refs_13_.refs_14_.refs_15_
  138.2 0.0 copy-done.2
  138.2 0.0 copy-start
  138.2 11.0 %weight_grads.1 = (bf16[768,1536]{1,0:T(8,128)(2,1)}, bf16[1536,768]{1,0:T(8,128)(2,1)}) custom-call(bf16[192,1536]{1,0:T(8,128)(2,1)} %get-tuple-element.21.refs_0_.refs_1_, bf16[192,1536]{1,0:T(8,128)(2,1)} %get-tuple-element.21.refs_0_.refs_1_, bf16[192,4608]{1,0:T(8,128)(2,1)} %get-tuple-element.22.refs_2_.refs_3_, ...), custom_call_target="tpu_custom_call" | custom-call | flops 1 | bytes 1 | tf_op jit(solution)/shard_map/weight_grads/pallas_call | solution.py:285
  149.2 6.0 %all-to-all-done.2 = bf16[64,8,1024]{2,1,0:T(8,128)(2,1)S(1)} async-done(((bf16[64,8,1024]{2,1,0:T(8,128)(2,1)}), bf16[64,8,1024]{2,1,0:T(8,128)(2,1)S(1)}, u32[]{:S(2)}, u32[]{:S(2)}) %all-to-all-start.2) | async-done | bytes 1048608 | tf_op jit(solution)/shard_map/all_to_all | solution.py:365
  155.2 0.0 copy-done
  155.2 1.7 %combine.1 = bf16[128,1536]{1,0:T(8,128)(2,1)} custom-call(s32[2,128]{1,0:T(2,128)S(1)} %bitcast.17, bf16[512,1024]{1,0:T(8,128)(2,1)S(1)} %bitcast.14, bf16[768,1536]{1,0:T(8,128)(2,1)} %get-tuple-element.15.earlier_ref), custom_call_target="tpu_custom_call" | custom-call | flops 1 | bytes 1 | tf_op jit(solution)/shard_map/combine/pallas_call | solution.py:341
  (2 shorter events, 0.0 us)
Async XLA Ops:
  3.9 46.4 %all-to-all-start = ((bf16[64,8,1152]{2,1,0:T(8,128)(2,1)}), bf16[64,8,1152]{2,1,0:T(8,128)(2,1)S(1)}, u32[]{:S(2)}, u32[]{:S(2)}) async-start(bf16[64,8,1152]{2,1,0:T(8,128)(2,1)} %bitcast.19), calls=%async_computation | async-start | bytes 2359296 | tf_op jit(solution)/shard_map/all_to_all | solution.py:365
  18.3 3.7 %copy-start.1 = (bf16[1536,768]{1,0:T(8,128)(2,1)S(1)}, bf16[1536,768]{1,0:T(8,128)(2,1)}, u32[]{:S(2)}) copy-start(bf16[1536,768]{1,0:T(8,128)(2,1)} %out_mine.7) | copy-start | bytes 7077892
  23.4 36.2 %collective-permute-start.1 = (bf16[1536,768]{1,0:T(8,128)(2,1)}, bf16[1536,768]{1,0:T(8,128)(2,1)}, u32[]{:S(2)}, u32[]{:S(2)}) collective-permute-start(bf16[1536,768]{1,0:T(8,128)(2,1)} %after.2), channel_id=1, source_target_pairs={{0,128},{128,0},{1,129},{129,1},{2,130},{130,2},{3,131},{131,3},{4... | collective-permute-start | bytes 7077896 | tf_op jit(solution)/shard_map/ppermute | solution.py:371
  23.4 36.2 %collective-permute-start = (bf16[768,1536]{1,0:T(8,128)(2,1)}, bf16[768,1536]{1,0:T(8,128)(2,1)}, u32[]{:S(2)}, u32[]{:S(2)}) collective-permute-start(bf16[768,1536]{1,0:T(8,128)(2,1)} %in_mine.7), channel_id=1, source_target_pairs={{0,128},{128,0},{1,129},{129,1},{2,130},{130,2},{3,131},{131,3},{4... | collective-permute-start | bytes 7077896 | tf_op jit(solution)/shard_map/ppermute | solution.py:371
  50.3 38.8 %collective-permute-start.2 = (bf16[512,1152]{1,0:T(8,128)(2,1)S(1)}, bf16[512,1152]{1,0:T(8,128)(2,1)}, u32[]{:S(2)}, u32[]{:S(2)}) collective-permute-start(bf16[512,1152]{1,0:T(8,128)(2,1)S(1)} %bitcast.12), channel_id=1, source_target_pairs={{0,1},{1,0},{2,3},{3,2},{4,5},{5,4},{6,7},{7,6},{8,9},{9,8},{10,11... | collective-permute-start | bytes 3538952 | tf_op jit(solution)/shard_map/ppermute | solution.py:379
  50.3 48.0 %all-to-all-start.1 = ((bf16[128,8,768]{2,1,0:T(8,128)(2,1)}), bf16[128,8,768]{2,1,0:T(8,128)(2,1)S(1)}, u32[]{:S(2)}, u32[]{:S(2)}) async-start(bf16[128,8,768]{2,1,0:T(8,128)(2,1)} %bitcast.18), calls=%async_computation.1 | async-start | bytes 3145728 | tf_op jit(solution)/shard_map/all_to_all | solution.py:365
  97.8 18.6 %collective-permute-start.3 = (bf16[192,1536]{1,0:T(8,128)(2,1)}, bf16[192,1536]{1,0:T(8,128)(2,1)S(1)}, u32[]{:S(2)}, u32[]{:S(2)}) collective-permute-start(bf16[192,1536]{1,0:T(8,128)(2,1)} %get-tuple-element.18.earlier_ref), channel_id=1, source_target_pairs={{0,1},{1,0},{2,3},{3,2},{4,5},{5,4},{6,7},{7,6},{8,9},{9,8},{10,11... | collective-permute-start | bytes 1769480 | tf_op jit(solution)/shard_map/ppermute | solution.py:383
  106.4 10.1 %collective-permute-start.4 = (bf16[128,1536]{1,0:T(8,128)(2,1)}, bf16[128,1536]{1,0:T(8,128)(2,1)S(1)}, u32[]{:S(2)}, u32[]{:S(2)}) collective-permute-start(bf16[128,1536]{1,0:T(8,128)(2,1)} %get-tuple-element.19.earlier_ref), channel_id=1, source_target_pairs={{0,1},{1,0},{2,3},{3,2},{4,5},{5,4},{6,7},{7,6},{8,9},{9,8},{10,11... | collective-permute-start | bytes 1179656 | tf_op jit(solution)/shard_map/ppermute | solution.py:385
  119.1 36.1 %all-to-all-start.2 = ((bf16[64,8,1024]{2,1,0:T(8,128)(2,1)}), bf16[64,8,1024]{2,1,0:T(8,128)(2,1)S(1)}, u32[]{:S(2)}, u32[]{:S(2)}) async-start(bf16[64,8,1024]{2,1,0:T(8,128)(2,1)} %bitcast.20), calls=%async_computation.2 | async-start | bytes 2097152 | tf_op jit(solution)/shard_map/all_to_all | solution.py:365
  128.2 5.5 %collective-permute-start.5 = (bf16[192,4608]{1,0:T(8,128)(2,1)}, bf16[192,4608]{1,0:T(8,128)(2,1)S(1)}, u32[]{:S(2)}, u32[]{:S(2)}) collective-permute-start(bf16[192,4608]{1,0:T(8,128)(2,1)} %get-tuple-element.22.refs_2_.refs_3_), channel_id=1, source_target_pairs={{0,128},{128,0},{1,129},{129,1},{2,130},{130,2},{3,131},{131,3},{4... | collective-permute-start | bytes 5308424 | tf_op jit(solution)/shard_map/ppermute | solution.py:371
  128.3 9.9 %collective-permute-start.6 = (bf16[192,4608]{1,0:T(8,128)(2,1)}, bf16[192,4608]{1,0:T(8,128)(2,1)}, u32[]{:S(2)}, u32[]{:S(2)}) collective-permute-start(bf16[192,4608]{1,0:T(8,128)(2,1)} %get-tuple-element.24.refs_10_.refs_11_), channel_id=1, source_target_pairs={{0,128},{128,0},{1,129},{129,1},{2,130},{130,2},{3,131},{131,3},{4... | collective-permute-start | bytes 5308424 | tf_op jit(solution)/shard_map/ppermute | solution.py:371
  128.8 7.7 %collective-permute-start.8 = (bf16[128,4608]{1,0:T(8,128)(2,1)}, bf16[128,4608]{1,0:T(8,128)(2,1)}, u32[]{:S(2)}, u32[]{:S(2)}) collective-permute-start(bf16[128,4608]{1,0:T(8,128)(2,1)} %get-tuple-element.28.refs_26_.refs_27_), channel_id=1, source_target_pairs={{0,128},{128,0},{1,129},{129,1},{2,130},{130,2},{3,131},{131,3},{4... | collective-permute-start | bytes 3538952 | tf_op jit(solution)/shard_map/ppermute | solution.py:371
  128.9 9.3 %collective-permute-start.7 = (bf16[128,4608]{1,0:T(8,128)(2,1)}, bf16[128,4608]{1,0:T(8,128)(2,1)}, u32[]{:S(2)}, u32[]{:S(2)}) collective-permute-start(bf16[128,4608]{1,0:T(8,128)(2,1)} %get-tuple-element.26.refs_18_.refs_19_), channel_id=1, source_target_pairs={{0,128},{128,0},{1,129},{129,1},{2,130},{130,2},{3,131},{131,3},{4... | collective-permute-start | bytes 3538952 | tf_op jit(solution)/shard_map/ppermute | solution.py:371
  133.7 4.5 %copy-start.2 = (bf16[192,4608]{1,0:T(8,128)(2,1)}, bf16[192,4608]{1,0:T(8,128)(2,1)S(1)}, u32[]{:S(2)}) copy-start(bf16[192,4608]{1,0:T(8,128)(2,1)S(1)} %collective-permute-done.5.refs_4_.refs_5_.refs_6_.refs_7_) | copy-start | bytes 5308420
  138.2 17.0 %copy-start = (s32[128,2]{0,1:T(2,128)S(1)}, s32[128,2]{0,1:T(2,128)}, u32[]{:S(2)}) copy-start(s32[128,2]{0,1:T(2,128)} %param.8) | copy-start | bytes 3076

commit v7 on v4

--- a/solution.py
+++ b/solution.py
@@ -81,13 +81,14 @@
     return first, match, rank
 
 
-def pack_main_kernel(routes_ref, gates_ref, tokens_ref, grads_ref, main_ref):
+def pack_main_kernel(routes_ref, gates_ref, tokens_ref, grads_ref, main_ref, rows_ref, sems):
     first, match, rank = slot_matches(routes_ref[...])
     gate = jnp.where(first, gates_ref[0:1, :], gates_ref[1:2, :])
     inner = iota((EXPERTS * 8, TOK), 0) & 7
     place = jnp.where(inner < 3, inner, inner - 3)
     chosen = match & (rank == place.astype(F32)) & (inner < 6)
     from_tokens, from_grads = mask(chosen & (inner < 3)), mask(chosen & (inner >= 3))
+    copies = []
     token_tail, grad_tail = tokens_ref[:, 1152:], grads_ref[:, 1152:]
     for j in range(3):
         columns = slice(j * 384, (j + 1) * 384)
@@ -101,7 +102,11 @@
             jnp.concatenate([from_grads, mask(tail & (inner == 7))], axis=1),
             jnp.concatenate([grads_ref[:, columns], grad_tail], axis=0),
         )
-        main_ref[:, columns] = rows.astype(BF)
+        rows_ref[j] = rows.astype(BF)
+        copies.append(pltpu.make_async_copy(rows_ref.at[j], main_ref.at[:, pl.ds(j * 384, 384)], sems.at[j]))
+        copies[j].start()
+    for copy in copies:
+        copy.wait()
 
 
 def pack_last_kernel(routes_ref, gates_ref, tokens_ref, grads_ref, last_ref):
@@ -123,9 +128,13 @@
 
 
 def pack(last, *operands):
+    shape = (1024, 768) if last else (512, 1152)
+    scratch = [] if last else [pltpu.VMEM((3, 512, 384), BF), pltpu.SemaphoreType.DMA((3,))]
     return pl.pallas_call(
         pack_last_kernel if last else pack_main_kernel,
-        out_shape=hbm_shape((1024, 768) if last else (512, 1152)),
+        out_specs=whole(shape) if last else pl.BlockSpec(memory_space=pl.ANY),
+        out_shape=hbm_shape(shape),
+        scratch_shapes=scratch,
         compiler_params=params(),
         cost_estimate=SMALL,
         name="pack_last" if last else "pack_main",
@@ -262,14 +271,12 @@
 
 
 def weight_grads_kernel(*refs):
-    in_ref, out_ref = refs[-2:]
-    first = second = None
-    for i in range(0, 24, 4):
-        token_ref, grad_ref, hidden_ref, dpre_ref = refs[i:i + 4]
-        a, b = dot_tn(token_ref[...], dpre_ref[...]), dot_tn(hidden_ref[...], grad_ref[...])
-        first, second = (a, b) if first is None else (first + a, second + b)
-    in_ref[...] = first.astype(BF)
-    out_ref[...] = second.astype(BF)
+    *operands, in_ref, out_ref = refs
+    tokens, grads, hidden, d_pre = (
+        jnp.concatenate([ref[...] for ref in operands[i::4]], axis=0) for i in range(4)
+    )
+    in_ref[...] = dot_tn(tokens, d_pre).astype(BF)
+    out_ref[...] = dot_tn(hidden, grads).astype(BF)
 
 
 def weight_grads(sets):

time: 158 us -> 158 us (level)
  Pallas kernels: 49.9 us -> 48.2 us
  transfers between devices with their start and end apart: 11 -> 11, of which waited for: 6 -> 6; matrix products, arithmetic and copies ran while one was open for 1% -> 1% of each run, Pallas kernels for 28% -> 27%
where the time goes in v7:
time: 158 us
  waiting for transfers between devices  71 us (45%)
  Pallas kernels  48.2 us (31%)
  starting transfers between devices  36.1 us (23%)
    all_to_all x3, waiting for transfers between devices, exchange(): lax.all_to_all(chunked, 'expert', split_axis=0, concat_axis=0, tiled=True...  36.2 us
    all_to_all x3, starting transfers between devices, exchange(): lax.all_to_all(chunked, 'expert', split_axis=0, concat_axis=0, tiled=True...  32.5 us
    pallas_call x3, Pallas kernels, expert_rows(): pl.pallas_call(functools.partial(expert_kernel, last), in_specs=[pl.Block...  26 us
    ppermute x1, waiting for transfers between devices, per_device(): pair_got = lax.ppermute(own_got, 'expert', chips)  21.1 us
    pallas_call x1, Pallas kernels, weight_grads(): pl.pallas_call(weight_grads_kernel, grid=(2,), in_specs=specs, out_specs=...  10.9 us
    ppermute x1, waiting for transfers between devices, per_device(): other_last = lax.ppermute(last_away, 'expert', chips)  7.65 us
    pallas_call x2, Pallas kernels, pack(): pl.pallas_call(pack_last_kernel if last else pack_main_kernel, out_specs=...  7 us
    ppermute x5, waiting for transfers between devices, to_other_core(): return lax.ppermute(x, 'dp', cores)  6.06 us
  transfers between devices with their start and end apart: 11, of which 6 were waited for; matrix products, arithmetic and copies ran while one was open for 1% of the time, Pallas kernels for 27%

profile of v7, /device:TPU:8, one launch (start us, length us, event | category | flops | bytes accessed | tf_op | source)
XLA Modules:
  0.0 157.6 jit_solution(7938797760550840570)
XLA Ops:
  0.6 3.3 %pack_main.1.earlier_ref = bf16[512,1152]{1,0:T(8,128)(2,1)} custom-call(s32[2,128]{1,0:T(2,128)} %bitcast.14, f32[2,128]{1,0:T(2,128)} %bitcast.20, bf16[128,1536]{1,0:T(8,128)(2,1)} %tokens_ref.3, bf16[128,1536]{1,0:T(8,128)(2,1)} %grads_ref.3), custom_call_target="tpu_custom_call" | custom-call | flops 1 | bytes 1 | tf_op jit(solution)/shard_map/pack_main/pallas_call | solution.py:133
  4.0 14.3 %all-to-all-start = ((bf16[64,8,1152]{2,1,0:T(8,128)(2,1)}), bf16[64,8,1152]{2,1,0:T(8,128)(2,1)S(1)}, u32[]{:S(2)}, u32[]{:S(2)}) async-start(bf16[64,8,1152]{2,1,0:T(8,128)(2,1)} %bitcast.18), calls=%async_computation | async-start | bytes 2359296 | tf_op jit(solution)/shard_map/all_to_all | solution.py:376
  18.3 0.0 copy-start.2
  18.3 3.7 %pack_last.1.earlier_ref = bf16[1024,768]{1,0:T(8,128)(2,1)} custom-call(s32[2,128]{1,0:T(2,128)} %bitcast.15, f32[2,128]{1,0:T(2,128)} %bitcast.21, bf16[128,1536]{1,0:T(8,128)(2,1)} %tokens_ref.3, bf16[128,1536]{1,0:T(8,128)(2,1)} %grads_ref.3), custom_call_target="tpu_custom_call" | custom-call | flops 1 | bytes 1 | tf_op jit(solution)/shard_map/pack_last/pallas_call | solution.py:133
  22.0 0.0 copy-done.2
  22.0 1.4 copy.11.x_ref
  23.4 0.0 collective-permute-start.1
  23.4 0.5 collective-permute-start
  23.9 26.4 %all-to-all-done = bf16[64,8,1152]{2,1,0:T(8,128)(2,1)S(1)} async-done(((bf16[64,8,1152]{2,1,0:T(8,128)(2,1)}), bf16[64,8,1152]{2,1,0:T(8,128)(2,1)S(1)}, u32[]{:S(2)}, u32[]{:S(2)}) %all-to-all-start) | async-done | bytes 1179680 | tf_op jit(solution)/shard_map/all_to_all | solution.py:376
  50.3 0.0 collective-permute-start.2
  50.3 9.1 %all-to-all-start.1 = ((bf16[128,8,768]{2,1,0:T(8,128)(2,1)}), bf16[128,8,768]{2,1,0:T(8,128)(2,1)S(1)}, u32[]{:S(2)}, u32[]{:S(2)}) async-start(bf16[128,8,768]{2,1,0:T(8,128)(2,1)} %bitcast.17), calls=%async_computation.1 | async-start | bytes 3145728 | tf_op jit(solution)/shard_map/all_to_all | solution.py:376
  59.5 0.1 pad_add_fusion.flags_ref
  59.5 0.0 collective-permute-done.1.out_other
  59.6 0.0 collective-permute-done.in_other
  59.6 8.5 %expert_main.2 = (bf16[192,1536]{1,0:T(8,128)(2,1)}, bf16[192,4608]{1,0:T(8,128)(2,1)}, bf16[192,1536]{1,0:T(8,128)(2,1)}) custom-call(s32[2]{0:T(128)S(1)} %pad_add_fusion.flags_ref, bf16[512,1152]{1,0:T(8,128)(2,1)} %pack_main.1.earlier_ref, bf16[512,1152]{1,0:T(8,128)(2,1)S(1)} %bitcast.12, bf16[768,1536]{1,0:T(8,128)(2,1)} %in_mine.5, ...), custom_call_target="tpu_custom_call" | custom-call | flops 1 | bytes 1 | tf_op jit(solution)/shard_map/expert_main/pallas_call | solution.py:255
  68.1 21.1 %collective-permute-done.2.got_ref = bf16[512,1152]{1,0:T(8,128)(2,1)} collective-permute-done((bf16[512,1152]{1,0:T(8,128)(2,1)S(1)}, bf16[512,1152]{1,0:T(8,128)(2,1)}, u32[]{:S(2)}, u32[]{:S(2)}) %collective-permute-start.2) | collective-permute-done | bytes 1179680 | tf_op jit(solution)/shard_map/ppermute | solution.py:390
  89.1 8.7 %expert_main.3 = (bf16[192,1536]{1,0:T(8,128)(2,1)}, bf16[192,4608]{1,0:T(8,128)(2,1)}, bf16[192,1536]{1,0:T(8,128)(2,1)}) custom-call(s32[2]{0:T(128)S(1)} %pad_add_fusion.flags_ref, bf16[192,1536]{1,0:T(8,128)(2,1)} %get-tuple-element.15.earlier_ref.main_a, bf16[512,1152]{1,0:T(8,128)(2,1)} %collective-permute-done.2.got_ref, bf16[768,1536]{1,0:T(8,128)(2,1)} %in_mine.5, ...), custom_call_target="tpu_custom_call" | custom-call | flops 99999997952 | bytes 100000000 | tf_op jit(solution)/shard_map/expert_main/pallas_call | solution.py:255
  97.9 0.5 collective-permute-start.3
  98.3 0.0 all-to-all-done.1
  98.3 8.7 %expert_last.1 = (bf16[256,1536]{1,0:T(8,128)(2,1)}, bf16[256,4608]{1,0:T(8,128)(2,1)}, bf16[128,1536]{1,0:T(8,128)(2,1)}, bf16[128,1536]{1,0:T(8,128)(2,1)}) custom-call(s32[2]{0:T(128)S(1)} %pad_add_fusion.flags_ref, bf16[192,1536]{1,0:T(8,128)(2,1)} %get-tuple-element.16.earlier_ref, bf16[1024,768]{1,0:T(8,128)(2,1)S(1)} %bitcast.10, ...), custom_call_target="tpu_custom_call" | custom-call | flops 1 | bytes 1 | tf_op jit(solution)/shard_map/expert_last/pallas_call | solution.py:255
  107.1 1.7 %collective-permute-start.4 = (bf16[128,1536]{1,0:T(8,128)(2,1)}, bf16[128,1536]{1,0:T(8,128)(2,1)S(1)}, u32[]{:S(2)}, u32[]{:S(2)}) collective-permute-start(bf16[128,1536]{1,0:T(8,128)(2,1)} %get-tuple-element.18), channel_id=1, source_target_pairs={{0,1},{1,0},{2,3},{3,2},{4,5},{5,4},{6,7},{7,6},{8,9},{9,8},{10,11... | collective-permute-start | bytes 1179656 | tf_op jit(solution)/shard_map/ppermute | solution.py:396
  108.8 0.0 collective-permute-start.7
  108.8 7.6 %collective-permute-done.4.last_b = bf16[128,1536]{1,0:T(8,128)(2,1)S(1)} collective-permute-done((bf16[128,1536]{1,0:T(8,128)(2,1)}, bf16[128,1536]{1,0:T(8,128)(2,1)S(1)}, u32[]{:S(2)}, u32[]{:S(2)}) %collective-permute-start.4) | collective-permute-done | bytes 393248 | tf_op jit(solution)/shard_map/ppermute | solution.py:396
  116.5 0.0 collective-permute-done.3.main_b
  116.5 2.7 %merge.1.earlier_ref = bf16[512,1024]{1,0:T(8,128)(2,1)} custom-call(bf16[192,1536]{1,0:T(8,128)(2,1)} %get-tuple-element.15.earlier_ref.main_a, bf16[192,1536]{1,0:T(8,128)(2,1)S(1)} %collective-permute-done.3.main_b, bf16[128,1536]{1,0:T(8,128)(2,1)} %get-tuple-element.17.last_a, bf16[128,1536]{1,0:T(8,128)(2,1)S(1)} %collective-permute-done.4.last_b), custom_call_target="tpu_custom_call" | custom-call | flops 1 | bytes 1 | tf_op jit(solution)/shard_map/merge/pallas_call | solution.py:326
  119.1 9.1 %all-to-all-start.2 = ((bf16[64,8,1024]{2,1,0:T(8,128)(2,1)}), bf16[64,8,1024]{2,1,0:T(8,128)(2,1)S(1)}, u32[]{:S(2)}, u32[]{:S(2)}) async-start(bf16[64,8,1024]{2,1,0:T(8,128)(2,1)} %bitcast.19), calls=%async_computation.2 | async-start | bytes 2097152 | tf_op jit(solution)/shard_map/all_to_all | solution.py:376
  128.2 0.3 collective-permute-start.5
  128.6 0.5 collective-permute-start.6
  129.1 4.9 %collective-permute-done.5.refs_4_.refs_5_.refs_6_.refs_7_ = bf16[192,4608]{1,0:T(8,128)(2,1)S(1)} collective-permute-done((bf16[192,4608]{1,0:T(8,128)(2,1)}, bf16[192,4608]{1,0:T(8,128)(2,1)S(1)}, u32[]{:S(2)}, u32[]{:S(2)}) %collective-permute-start.5) | collective-permute-done | bytes 1769504 | tf_op jit(solution)/shard_map/ppermute | solution.py:382
  134.0 0.0 copy-start.1
  134.0 1.1 collective-permute-done.6.refs_12_.refs_13_.refs_14_.refs_15_
  135.1 0.0 collective-permute-done.7.refs_20_.refs_21_.refs_22_.refs_23_
  135.1 0.1 copy-done.1
  135.2 0.0 copy-start
  135.2 10.9 %weight_grads.1 = (bf16[768,1536]{1,0:T(8,128)(2,1)}, bf16[1536,768]{1,0:T(8,128)(2,1)}) custom-call(bf16[192,1536]{1,0:T(8,128)(2,1)} %get-tuple-element.19.refs_0_.refs_1_, bf16[192,1536]{1,0:T(8,128)(2,1)} %get-tuple-element.19.refs_0_.refs_1_, bf16[192,4608]{1,0:T(8,128)(2,1)} %get-tuple-element.20.refs_2_.refs_3_, ...), custom_call_target="tpu_custom_call" | custom-call | flops 1 | bytes 1 | tf_op jit(solution)/shard_map/weight_grads/pallas_call | solution.py:296
  146.1 9.8 %all-to-all-done.2 = bf16[64,8,1024]{2,1,0:T(8,128)(2,1)S(1)} async-done(((bf16[64,8,1024]{2,1,0:T(8,128)(2,1)}), bf16[64,8,1024]{2,1,0:T(8,128)(2,1)S(1)}, u32[]{:S(2)}, u32[]{:S(2)}) %all-to-all-start.2) | async-done | bytes 1048608 | tf_op jit(solution)/shard_map/all_to_all | solution.py:376
  155.9 0.0 copy-done
  155.9 1.7 %combine.1 = bf16[128,1536]{1,0:T(8,128)(2,1)} custom-call(s32[2,128]{1,0:T(2,128)S(1)} %bitcast.16, bf16[512,1024]{1,0:T(8,128)(2,1)S(1)} %bitcast.13, bf16[768,1536]{1,0:T(8,128)(2,1)} %get-tuple-element.13.earlier_ref), custom_call_target="tpu_custom_call" | custom-call | flops 1 | bytes 1 | tf_op jit(solution)/shard_map/combine/pallas_call | solution.py:352
  (2 shorter events, 0.0 us)
Async XLA Ops:
  4.0 46.4 %all-to-all-start = ((bf16[64,8,1152]{2,1,0:T(8,128)(2,1)}), bf16[64,8,1152]{2,1,0:T(8,128)(2,1)S(1)}, u32[]{:S(2)}, u32[]{:S(2)}) async-start(bf16[64,8,1152]{2,1,0:T(8,128)(2,1)} %bitcast.18), calls=%async_computation | async-start | bytes 2359296 | tf_op jit(solution)/shard_map/all_to_all | solution.py:376
  18.3 3.7 %copy-start.2 = (bf16[1536,768]{1,0:T(8,128)(2,1)S(1)}, bf16[1536,768]{1,0:T(8,128)(2,1)}, u32[]{:S(2)}) copy-start(bf16[1536,768]{1,0:T(8,128)(2,1)} %out_mine.5) | copy-start | bytes 7077892
  23.4 36.2 %collective-permute-start.1 = (bf16[1536,768]{1,0:T(8,128)(2,1)}, bf16[1536,768]{1,0:T(8,128)(2,1)}, u32[]{:S(2)}, u32[]{:S(2)}) collective-permute-start(bf16[1536,768]{1,0:T(8,128)(2,1)} %after.2), channel_id=1, source_target_pairs={{0,128},{128,0},{1,129},{129,1},{2,130},{130,2},{3,131},{131,3},{4... | collective-permute-start | bytes 7077896 | tf_op jit(solution)/shard_map/ppermute | solution.py:382
  23.4 36.2 %collective-permute-start = (bf16[768,1536]{1,0:T(8,128)(2,1)}, bf16[768,1536]{1,0:T(8,128)(2,1)}, u32[]{:S(2)}, u32[]{:S(2)}) collective-permute-start(bf16[768,1536]{1,0:T(8,128)(2,1)} %in_mine.5), channel_id=1, source_target_pairs={{0,128},{128,0},{1,129},{129,1},{2,130},{130,2},{3,131},{131,3},{4... | collective-permute-start | bytes 7077896 | tf_op jit(solution)/shard_map/ppermute | solution.py:382
  50.3 38.8 %collective-permute-start.2 = (bf16[512,1152]{1,0:T(8,128)(2,1)S(1)}, bf16[512,1152]{1,0:T(8,128)(2,1)}, u32[]{:S(2)}, u32[]{:S(2)}) collective-permute-start(bf16[512,1152]{1,0:T(8,128)(2,1)S(1)} %bitcast.11), channel_id=1, source_target_pairs={{0,1},{1,0},{2,3},{3,2},{4,5},{5,4},{6,7},{7,6},{8,9},{9,8},{10,11... | collective-permute-start | bytes 3538952 | tf_op jit(solution)/shard_map/ppermute | solution.py:390
  50.3 48.0 %all-to-all-start.1 = ((bf16[128,8,768]{2,1,0:T(8,128)(2,1)}), bf16[128,8,768]{2,1,0:T(8,128)(2,1)S(1)}, u32[]{:S(2)}, u32[]{:S(2)}) async-start(bf16[128,8,768]{2,1,0:T(8,128)(2,1)} %bitcast.17), calls=%async_computation.1 | async-start | bytes 3145728 | tf_op jit(solution)/shard_map/all_to_all | solution.py:376
  97.9 18.6 %collective-permute-start.3 = (bf16[192,1536]{1,0:T(8,128)(2,1)}, bf16[192,1536]{1,0:T(8,128)(2,1)S(1)}, u32[]{:S(2)}, u32[]{:S(2)}) collective-permute-start(bf16[192,1536]{1,0:T(8,128)(2,1)} %get-tuple-element.16.earlier_ref), channel_id=1, source_target_pairs={{0,1},{1,0},{2,3},{3,2},{4,5},{5,4},{6,7},{7,6},{8,9},{9,8},{10,11... | collective-permute-start | bytes 1769480 | tf_op jit(solution)/shard_map/ppermute | solution.py:394
  107.1 9.4 %collective-permute-start.4 = (bf16[128,1536]{1,0:T(8,128)(2,1)}, bf16[128,1536]{1,0:T(8,128)(2,1)S(1)}, u32[]{:S(2)}, u32[]{:S(2)}) collective-permute-start(bf16[128,1536]{1,0:T(8,128)(2,1)} %get-tuple-element.18), channel_id=1, source_target_pairs={{0,1},{1,0},{2,3},{3,2},{4,5},{5,4},{6,7},{7,6},{8,9},{9,8},{10,11... | collective-permute-start | bytes 1179656 | tf_op jit(solution)/shard_map/ppermute | solution.py:396
  108.8 26.3 %collective-permute-start.7 = (bf16[256,4608]{1,0:T(8,128)(2,1)}, bf16[256,4608]{1,0:T(8,128)(2,1)}, u32[]{:S(2)}, u32[]{:S(2)}) collective-permute-start(bf16[256,4608]{1,0:T(8,128)(2,1)} %get-tuple-element.24.refs_18_.refs_19_), channel_id=1, source_target_pairs={{0,128},{128,0},{1,129},{129,1},{2,130},{130,2},{3,131},{131,3},{4... | collective-permute-start | bytes 7077896 | tf_op jit(solution)/shard_map/ppermute | solution.py:382
  119.1 36.8 %all-to-all-start.2 = ((bf16[64,8,1024]{2,1,0:T(8,128)(2,1)}), bf16[64,8,1024]{2,1,0:T(8,128)(2,1)S(1)}, u32[]{:S(2)}, u32[]{:S(2)}) async-start(bf16[64,8,1024]{2,1,0:T(8,128)(2,1)} %bitcast.19), calls=%async_computation.2 | async-start | bytes 2097152 | tf_op jit(solution)/shard_map/all_to_all | solution.py:376
  128.2 5.7 %collective-permute-start.5 = (bf16[192,4608]{1,0:T(8,128)(2,1)}, bf16[192,4608]{1,0:T(8,128)(2,1)S(1)}, u32[]{:S(2)}, u32[]{:S(2)}) collective-permute-start(bf16[192,4608]{1,0:T(8,128)(2,1)} %get-tuple-element.20.refs_2_.refs_3_), channel_id=1, source_target_pairs={{0,128},{128,0},{1,129},{129,1},{2,130},{130,2},{3,131},{131,3},{4... | collective-permute-start | bytes 5308424 | tf_op jit(solution)/shard_map/ppermute | solution.py:382
  128.6 6.6 %collective-permute-start.6 = (bf16[192,4608]{1,0:T(8,128)(2,1)}, bf16[192,4608]{1,0:T(8,128)(2,1)}, u32[]{:S(2)}, u32[]{:S(2)}) collective-permute-start(bf16[192,4608]{1,0:T(8,128)(2,1)} %get-tuple-element.22.refs_10_.refs_11_), channel_id=1, source_target_pairs={{0,128},{128,0},{1,129},{129,1},{2,130},{130,2},{3,131},{131,3},{4... | collective-permute-start | bytes 5308424 | tf_op jit(solution)/shard_map/ppermute | solution.py:382
  134.0 1.2 copy-start.1
  135.2 20.7 %copy-start = (s32[128,2]{0,1:T(2,128)S(1)}, s32[128,2]{0,1:T(2,128)}, u32[]{:S(2)}) copy-start(s32[128,2]{0,1:T(2,128)} %param.8) | copy-start | bytes 3076
